TPU v7x, 32 devices: a whole 2x2x4 slice. The times are simulated.
32 devices in a mesh: dp: 8 (over y, x, core), fsdp: 4 (over z).
Axes of the slice: x: 2, y: 2, z: 4, core: 2. Of those that a mesh axis runs over, the one named last changes fastest.
Arguments:
- tokens: bfloat16 [16384, 768], P(('dp', 'fsdp')), may hold values from -6 to 6
- coarse_view: bfloat16 [4096, 768], P(('dp', 'fsdp')), may hold values from -6 to 6
- segment_ids: int32 [32, 512], P(('dp', 'fsdp')), may hold values from 0 to 2, as said below
- partner_device: int32 [128, 1], P(('dp', 'fsdp')), may hold values from 0 to 7; in each aligned block of 4 rows (0 to 3, 4 to 7, ...) at most 2 rows name the same one
- partner_slot: int32 [128], P(('dp', 'fsdp')), may hold values from 0 to 3
- mix_weight: float32 [128], P(('dp', 'fsdp')), may hold values from 0.25 to 0.75
- ln1_gain: bfloat16 [768], P(('dp', 'fsdp')), may hold values from 0.5 to 1.5
- w_qkv: bfloat16 [768, 2304], P(None, ('dp', 'fsdp')), may hold values from -0.21875 to 0.21875
- w_out: bfloat16 [768, 768], P(('dp', 'fsdp')), may hold values from -3.5 to 3.5
- lnx_gain: bfloat16 [768], P(('dp', 'fsdp')), may hold values from 0.5 to 1.5
- w_cq: bfloat16 [768, 768], P(('dp', 'fsdp')), may hold values from -0.21875 to 0.21875
- w_ckv: bfloat16 [768, 1536], P(None, ('dp', 'fsdp')), may hold values from -0.21875 to 0.21875
- w_cout: bfloat16 [768, 768], P(('dp', 'fsdp')), may hold values from -3.5 to 3.5
- ln2_gain: bfloat16 [768], P(('dp', 'fsdp')), may hold values from 0.5 to 1.5
- w_up: bfloat16 [768, 3072], P(None, ('dp', 'fsdp')), may hold values from -0.21875 to 0.21875
- w_down: bfloat16 [3072, 768], P(('dp', 'fsdp')), may hold values from -0.109375 to 0.109375
- cotangent: bfloat16 [16384, 768], P(('dp', 'fsdp')), may hold values from -6 to 6
Outputs:
- output: bfloat16 [16384, 768], P(('dp', 'fsdp'))
- token_grad: float32 [16384, 768], P(('dp', 'fsdp'))
- coarse_grad: float32 [4096, 768], P(('dp', 'fsdp'))
- ln1_grad: float32 [768], P(('dp', 'fsdp'))
- qkv_grad: float32 [768, 2304], P(None, ('dp', 'fsdp'))
- out_grad: float32 [768, 768], P(('dp', 'fsdp'))
- lnx_grad: float32 [768], P(('dp', 'fsdp'))
- cq_grad: float32 [768, 768], P(('dp', 'fsdp'))
- ckv_grad: float32 [768, 1536], P(None, ('dp', 'fsdp'))
- cout_grad: float32 [768, 768], P(('dp', 'fsdp'))
- ln2_grad: float32 [768], P(('dp', 'fsdp'))
- up_grad: float32 [768, 3072], P(None, ('dp', 'fsdp'))
- down_grad: float32 [3072, 768], P(('dp', 'fsdp'))
Inputs may be any that keep to these rules, and one draw needn't show every extreme that they name: `partner_device`: among the 4 blocks of one device no value appears more than 2 times, and some device has a value exactly 2 times. `segment_ids`: ids never fall along a device's row; each device holds three videos, each a whole number of mixup blocks of 128 tokens, the longest exactly 256 tokens.
All inputs are finite; a program needn't handle non-finite values.
Results may differ from a plain program's by a relative error of at most 0.02.
Values may be sent and summed in bfloat16 or wider, within the bound.
No kernel may reach another device: no remote copies, remote signals or barrier semaphores. Data moves between devices by JAX's collectives and lax.ppermute only.
A program may use at most 256 MiB of HBM per device.

v0:
```python
import jax
import jax.numpy as jnp
from jax import lax
from jax.sharding import PartitionSpec as P

HEADS = 12
HEAD = 64
CAP = 2


highest = lax.Precision.HIGHEST


def norm_rows(values, gain):
    centre = jnp.mean(values, axis=-1, keepdims=True)
    shifted = values - centre
    spread = jnp.mean(shifted * shifted, axis=-1, keepdims=True)
    return shifted * lax.rsqrt(spread + 1e-06) * gain


def exact_gelu(values):
    return jax.nn.gelu(values, approximate=False)


def masked_scores(query_rows, keys_all, query_seg, key_seg):
    scores = jnp.einsum("qhd,khd->hqk", query_rows, keys_all, preferred_element_type=jnp.float32)
    same_video = query_seg[:, None] == key_seg[None, :]
    return jnp.where(same_video[None, :, :], scores, -1e30)


def attend_rows(queries, keys_all, values_all, query_seg, key_seg, block_rows):
    row_count = queries.shape[0]
    model_width = queries.shape[1] * queries.shape[2]
    starts = jnp.arange(row_count // block_rows, dtype=jnp.int32) * block_rows

    def forward_block(start):
        scores = masked_scores(queries, keys_all, query_seg, key_seg)
        largest = jnp.max(scores, axis=-1, keepdims=True)
        raised = jnp.exp(scores - largest)
        total_sum = jnp.sum(raised, axis=-1, keepdims=True)
        soft_low = (raised / total_sum).astype(jnp.bfloat16)
        attended_rows = jnp.einsum(
            "hqk,khd->qhd", soft_low, values_all, preferred_element_type=jnp.float32
        )
        return (
            attended_rows.reshape(block_rows, model_width),
            (largest + jnp.log(total_sum))[..., 0],
        )

    parts, log_sums = lax.map(forward_block, starts)
    return (parts.reshape(row_count, model_width).astype(jnp.bfloat16), log_sums)


def attend_grads(
    queries, keys_all, values_all, query_seg, key_seg, block_rows, log_sums, grad_attended
):
    row_count = queries.shape[0]
    key_count = keys_all.shape[0]
    model_width = queries.shape[1] * queries.shape[2]
    starts = jnp.arange(row_count // block_rows, dtype=jnp.int32) * block_rows
    grad_heads = grad_attended.reshape(queries.shape)

    def backward_block(carried, inputs_now):
        key_sum, value_sum = carried
        start, log_rows = inputs_now
        scores = masked_scores(queries, keys_all, query_seg, key_seg)
        soft_rows = jnp.exp(scores - log_rows[..., None])
        soft_low = soft_rows.astype(jnp.bfloat16)
        value_sum = value_sum + jnp.einsum(
            "hqk,qhd->khd", soft_low, grad_heads, preferred_element_type=jnp.float32
        )
        grad_soft = jnp.einsum(
            "qhd,khd->hqk", grad_heads, values_all, preferred_element_type=jnp.float32
        )
        inner_sum = jnp.sum(soft_rows * grad_soft, axis=-1, keepdims=True)
        grad_scores = (soft_rows * (grad_soft - inner_sum)).astype(jnp.bfloat16)
        query_part = jnp.einsum(
            "hqk,khd->qhd", grad_scores, keys_all, preferred_element_type=jnp.float32
        )
        key_sum = key_sum + jnp.einsum(
            "hqk,qhd->khd", grad_scores, queries, preferred_element_type=jnp.float32
        )
        return (
            (key_sum, value_sum),
            query_part.astype(jnp.bfloat16).reshape(block_rows, model_width),
        )

    zero_heads = jnp.zeros(keys_all.shape, jnp.float32)
    sums_out, query_parts = lax.scan(backward_block, (zero_heads, zero_heads), (starts, log_sums))
    key_total, value_total = sums_out
    return (
        query_parts.reshape(row_count, model_width),
        key_total.reshape(key_count, model_width).astype(jnp.bfloat16),
        value_total.reshape(key_count, model_width).astype(jnp.bfloat16),
    )


def shards(
    tokens,
    coarse_view,
    segment_ids,
    partner_device,
    partner_slot,
    mix_weight,
    ln1_gain,
    w_qkv,
    w_out,
    lnx_gain,
    w_cq,
    w_ckv,
    w_cout,
    ln2_gain,
    w_up,
    w_down,
    cotangent,
):
    row_count, model_width = tokens.shape
    coarse_rows = coarse_view.shape[0]
    block_count = mix_weight.shape[0]
    clip_rows = row_count // block_count
    peer_count = lax.axis_size("dp")
    slot_count = peer_count * CAP
    target = partner_device[:, 0]
    target_hot = (target[:, None] == jnp.arange(peer_count, dtype=jnp.int32)[None, :]).astype(
        jnp.int32
    )
    earlier = jnp.cumsum(target_hot, axis=0) - target_hot
    order_in = jnp.sum(earlier * target_hot, axis=1)
    position = target * CAP + order_in
    pick_int = (position[:, None] == jnp.arange(slot_count, dtype=jnp.int32)[None, :]).astype(
        jnp.int32
    )
    wanted = jnp.sum(pick_int * partner_slot[:, None], axis=0).reshape(peer_count, CAP)
    filled = jnp.sum(pick_int, axis=0).reshape(peer_count, CAP)
    asked, asked_filled = (
        lax.all_to_all(wanted, "dp", split_axis=0, concat_axis=0, tiled=True),
        lax.all_to_all(filled, "dp", split_axis=0, concat_axis=0, tiled=True),
    )
    owner_hot = (
        asked.reshape(slot_count)[:, None] == jnp.arange(block_count, dtype=jnp.int32)[None, :]
    ) & (asked_filled.reshape(slot_count)[:, None] > 0)
    own_blocks = tokens.reshape(block_count, clip_rows * model_width)
    reply = jnp.dot(
        owner_hot.astype(jnp.bfloat16), own_blocks, preferred_element_type=jnp.float32
    ).astype(jnp.bfloat16)
    answers = lax.all_to_all(
        reply.reshape(peer_count, CAP * clip_rows * model_width),
        "dp",
        split_axis=0,
        concat_axis=0,
        tiled=True,
    )
    partner_rows = jnp.dot(
        pick_int.astype(jnp.bfloat16),
        answers.reshape(slot_count, clip_rows * model_width),
        preferred_element_type=jnp.float32,
    )
    mixing = mix_weight[:, None]
    blended = (mixing * own_blocks.astype(jnp.float32) + (1.0 - mixing) * partner_rows).reshape(
        row_count, model_width
    )
    attn_full = (
        lax.all_gather(ln1_gain, ("dp", "fsdp"), axis=0, tiled=True),
        lax.all_gather(w_qkv, ("dp", "fsdp"), axis=1, tiled=True),
        lax.all_gather(w_out, ("dp", "fsdp"), axis=0, tiled=True),
        lax.all_gather(lnx_gain, ("dp", "fsdp"), axis=0, tiled=True),
        lax.all_gather(w_cq, ("dp", "fsdp"), axis=0, tiled=True),
        lax.all_gather(w_ckv, ("dp", "fsdp"), axis=1, tiled=True),
        lax.all_gather(w_cout, ("dp", "fsdp"), axis=0, tiled=True),
    )
    gain_one, qkv_full, out_full, gain_cross, cq_full, ckv_full, cout_full = attn_full
    segments = segment_ids[0]
    coarse_seg = segments.reshape(coarse_rows, row_count // coarse_rows)[:, 0]
    block_rows = min(512, row_count)
    normed = norm_rows(blended, gain_one.astype(jnp.float32)).astype(jnp.bfloat16)
    projected = jnp.dot(normed, qkv_full, preferred_element_type=jnp.float32)
    queries = (
        (projected[:, :model_width] * 0.125).astype(jnp.bfloat16).reshape(row_count, HEADS, HEAD)
    )
    keys_all = (
        projected[:, model_width : 2 * model_width]
        .astype(jnp.bfloat16)
        .reshape(row_count, HEADS, HEAD)
    )
    values_all = (
        projected[:, 2 * model_width :].astype(jnp.bfloat16).reshape(row_count, HEADS, HEAD)
    )
    attended, self_lse = attend_rows(queries, keys_all, values_all, segments, segments, block_rows)
    residual = blended + jnp.dot(attended, out_full, preferred_element_type=jnp.float32)
    crossed_in = norm_rows(residual, gain_cross.astype(jnp.float32)).astype(jnp.bfloat16)
    cross_q = (
        (jnp.dot(crossed_in, cq_full, preferred_element_type=jnp.float32) * 0.125)
        .astype(jnp.bfloat16)
        .reshape(row_count, HEADS, HEAD)
    )
    coarse_proj = jnp.dot(coarse_view, ckv_full, preferred_element_type=jnp.float32)
    cross_k = coarse_proj[:, :model_width].astype(jnp.bfloat16).reshape(coarse_rows, HEADS, HEAD)
    cross_v = coarse_proj[:, model_width:].astype(jnp.bfloat16).reshape(coarse_rows, HEADS, HEAD)
    crossed, cross_lse = attend_rows(cross_q, cross_k, cross_v, segments, coarse_seg, block_rows)
    joined = residual + jnp.dot(crossed, cout_full, preferred_element_type=jnp.float32)
    gain_two, up_full, down_full = (
        lax.all_gather(ln2_gain, ("dp", "fsdp"), axis=0, tiled=True),
        lax.all_gather(w_up, ("dp", "fsdp"), axis=1, tiled=True),
        lax.all_gather(w_down, ("dp", "fsdp"), axis=0, tiled=True),
    )
    second = norm_rows(joined, gain_two.astype(jnp.float32)).astype(jnp.bfloat16)
    pre_act = jnp.dot(second, up_full, preferred_element_type=jnp.float32)
    hidden = exact_gelu(pre_act).astype(jnp.bfloat16)
    output = (joined + jnp.dot(hidden, down_full, preferred_element_type=jnp.float32)).astype(
        jnp.bfloat16
    )
    back_mlp = (
        lax.all_gather(ln2_gain, ("dp", "fsdp"), axis=0, tiled=True),
        lax.all_gather(w_up, ("dp", "fsdp"), axis=1, tiled=True),
        lax.all_gather(w_down, ("dp", "fsdp"), axis=0, tiled=True),
    )
    gain_two_back, up_back, down_back = back_mlp
    down_grad = jnp.einsum("tf,td->fd", hidden, cotangent, preferred_element_type=jnp.float32)
    grad_hidden = jnp.einsum("td,fd->tf", cotangent, down_back, preferred_element_type=jnp.float32)
    gelu_value, gelu_pull = jax.vjp(exact_gelu, pre_act)
    grad_pre = gelu_pull(grad_hidden)[0].astype(jnp.bfloat16)
    up_grad = jnp.einsum("td,tf->df", second, grad_pre, preferred_element_type=jnp.float32)
    grad_second = jnp.einsum("tf,df->td", grad_pre, up_back, preferred_element_type=jnp.float32)
    norm_value, norm_pull = jax.vjp(norm_rows, joined, gain_two_back.astype(jnp.float32))
    grad_joined_norm, ln2_piece = norm_pull(grad_second)
    grad_joined = cotangent.astype(jnp.float32) + grad_joined_norm
    ln2_grad, up_shard, down_shard = (
        lax.psum_scatter(ln2_piece, ("dp", "fsdp"), scatter_dimension=0, tiled=True),
        lax.psum_scatter(up_grad, ("dp", "fsdp"), scatter_dimension=1, tiled=True),
        lax.psum_scatter(down_grad, ("dp", "fsdp"), scatter_dimension=0, tiled=True),
    )
    back_attn = (
        lax.all_gather(ln1_gain, ("dp", "fsdp"), axis=0, tiled=True),
        lax.all_gather(w_qkv, ("dp", "fsdp"), axis=1, tiled=True),
        lax.all_gather(w_out, ("dp", "fsdp"), axis=0, tiled=True),
        lax.all_gather(lnx_gain, ("dp", "fsdp"), axis=0, tiled=True),
        lax.all_gather(w_cq, ("dp", "fsdp"), axis=0, tiled=True),
        lax.all_gather(w_ckv, ("dp", "fsdp"), axis=1, tiled=True),
        lax.all_gather(w_cout, ("dp", "fsdp"), axis=0, tiled=True),
    )
    gain_one_back, qkv_back, out_back, cross_gain_back, cq_back, ckv_back, cout_back = back_attn
    grad_joined_low = grad_joined.astype(jnp.bfloat16)
    cout_grad = jnp.einsum(
        "td,te->de", crossed, grad_joined_low, preferred_element_type=jnp.float32
    )
    grad_crossed = jnp.einsum(
        "te,de->td", grad_joined_low, cout_back, preferred_element_type=jnp.float32
    ).astype(jnp.bfloat16)
    cq_part, ck_part, cv_part = attend_grads(
        cross_q, cross_k, cross_v, segments, coarse_seg, block_rows, cross_lse, grad_crossed
    )
    grad_cq = cq_part * 0.125
    cq_grad = jnp.einsum("td,te->de", crossed_in, grad_cq, preferred_element_type=jnp.float32)
    grad_crossed_in = jnp.einsum("te,de->td", grad_cq, cq_back, preferred_element_type=jnp.float32)
    grad_ckv = jnp.concatenate([ck_part, cv_part], axis=1)
    ckv_grad = jnp.einsum("td,te->de", coarse_view, grad_ckv, preferred_element_type=jnp.float32)
    coarse_grad = jnp.einsum("te,de->td", grad_ckv, ckv_back, preferred_element_type=jnp.float32)
    cross_value, cross_pull = jax.vjp(norm_rows, residual, cross_gain_back.astype(jnp.float32))
    grad_res_norm, lnx_piece = cross_pull(grad_crossed_in)
    grad_residual = grad_joined + grad_res_norm
    grad_res_low = grad_residual.astype(jnp.bfloat16)
    out_grad = jnp.einsum("td,te->de", attended, grad_res_low, preferred_element_type=jnp.float32)
    grad_attended = jnp.einsum(
        "te,de->td", grad_res_low, out_back, preferred_element_type=jnp.float32
    ).astype(jnp.bfloat16)
    query_part, key_part, value_part = attend_grads(
        queries, keys_all, values_all, segments, segments, block_rows, self_lse, grad_attended
    )
    grad_projected = jnp.concatenate([query_part * 0.125, key_part, value_part], axis=1)
    qkv_grad = jnp.einsum("td,te->de", normed, grad_projected, preferred_element_type=jnp.float32)
    grad_normed = jnp.einsum(
        "te,de->td", grad_projected, qkv_back, preferred_element_type=jnp.float32
    )
    first_value, first_pull = jax.vjp(norm_rows, blended, gain_one_back.astype(jnp.float32))
    grad_blend_norm, ln1_piece = first_pull(grad_normed)
    grad_blended = grad_residual + grad_blend_norm
    attn_shards = (
        lax.psum_scatter(ln1_piece, ("dp", "fsdp"), scatter_dimension=0, tiled=True),
        lax.psum_scatter(qkv_grad, ("dp", "fsdp"), scatter_dimension=1, tiled=True),
        lax.psum_scatter(out_grad, ("dp", "fsdp"), scatter_dimension=0, tiled=True),
        lax.psum_scatter(lnx_piece, ("dp", "fsdp"), scatter_dimension=0, tiled=True),
        lax.psum_scatter(cq_grad, ("dp", "fsdp"), scatter_dimension=0, tiled=True),
        lax.psum_scatter(ckv_grad, ("dp", "fsdp"), scatter_dimension=1, tiled=True),
        lax.psum_scatter(cout_grad, ("dp", "fsdp"), scatter_dimension=0, tiled=True),
    )
    ln1_grad, qkv_shard, out_shard, lnx_grad, cq_shard, ckv_shard, cout_shard = attn_shards
    grad_blocks = grad_blended.reshape(block_count, clip_rows * model_width)
    outgoing = jnp.dot(
        pick_int.T.astype(jnp.float32), (1.0 - mixing) * grad_blocks, precision=highest
    )
    returned = lax.all_to_all(
        outgoing.reshape(peer_count, CAP * clip_rows * model_width).astype(jnp.bfloat16),
        "dp",
        split_axis=0,
        concat_axis=0,
        tiled=True,
    ).astype(jnp.float32)
    incoming = jnp.dot(
        owner_hot.T.astype(jnp.float32),
        returned.reshape(slot_count, clip_rows * model_width),
        precision=highest,
    )
    token_grad = (mixing * grad_blocks + incoming).reshape(row_count, model_width)
    return (
        output,
        token_grad,
        coarse_grad,
        ln1_grad,
        qkv_shard,
        out_shard,
        lnx_grad,
        cq_shard,
        ckv_shard,
        cout_shard,
        ln2_grad,
        up_shard,
        down_shard,
    )


def solution(mesh):
    in_specs = (
        P(("dp", "fsdp"), None),
        P(("dp", "fsdp"), None),
        P(("dp", "fsdp"), None),
        P(("dp", "fsdp"), None),
        P(("dp", "fsdp")),
        P(("dp", "fsdp")),
        P(("dp", "fsdp")),
        P(None, ("dp", "fsdp")),
        P(("dp", "fsdp"), None),
        P(("dp", "fsdp")),
        P(("dp", "fsdp"), None),
        P(None, ("dp", "fsdp")),
        P(("dp", "fsdp"), None),
        P(("dp", "fsdp")),
        P(None, ("dp", "fsdp")),
        P(("dp", "fsdp"), None),
        P(("dp", "fsdp"), None),
    )
    out_specs = (
        P(("dp", "fsdp"), None),
        P(("dp", "fsdp"), None),
        P(("dp", "fsdp"), None),
        P(("dp", "fsdp")),
        P(None, ("dp", "fsdp")),
        P(("dp", "fsdp"), None),
        P(("dp", "fsdp")),
        P(("dp", "fsdp"), None),
        P(None, ("dp", "fsdp")),
        P(("dp", "fsdp"), None),
        P(("dp", "fsdp")),
        P(None, ("dp", "fsdp")),
        P(("dp", "fsdp"), None),
    )
    return jax.shard_map(shards, mesh=mesh, in_specs=in_specs, out_specs=out_specs, check_vma=False)
```

profile of v0, /device:TPU:0, one launch (start us, length us, event | category | flops | bytes accessed | tf_op | source)
XLA Modules:
  0.0 1318.4 jit_solution(204792632502469016)
XLA Ops:
  41.6 19.5 %reduce.14 = bf16[8,196608]{1,0:T(8,128)(2,1)S(1)} reduce(bf16[8,1,196608]{2,1,0:T(2,128)(2,1)} %all_to_all.29, bf16[]{:T(256)} %broadcast.444), dimensions={1}, to_apply=%all_to_all.29.reduce_sub_computation | reduce | bytes 6291458 | tf_op jit(solution)/shard_map/all_to_all | solution.py:146
  71.8 71.8 %all-reduce.7 = (bf16[768]{0:T(1024)(128)(2,1)S(1)}, bf16[768]{0:T(1024)(128)(2,1)S(1)}, bf16[768]{0:T(1024)(128)(2,1)S(1)}) all-reduce(bf16[768]{0:T(1024)(128)(2,1)S(1)} %dynamic-update-slice, bf16[768]{0:T(1024)(128)(2,1)S(1)} %dynamic-update-slice.1, ...), channel_id=1, replica_groups=mesh['dp'=8,'fsdp'=4] {'dp','fsdp'}, use_global_device_ids=true, to_apply=%add | all-reduce | flops 2304 | bytes 9216
  151.3 20.6 %reduce.2 = bf16[8,196608]{1,0:T(8,128)(2,1)} reduce(bf16[8,1,196608]{2,1,0:T(2,128)(2,1)} %reshape.365, bf16[]{:T(256)} %constant.186), dimensions={1}, to_apply=%all_to_all.27.reduce_sub_computation | reduce | bytes 6291458 | tf_op jit(solution)/shard_map/all_to_all | solution.py:146
  214.1 38.0 %all-gather.14.cloned.1.call-done = bf16[768,768]{1,0:T(8,128)(2,1)} async-done(((bf16[24,768]{1,0:T(8,128)(2,1)}), bf16[768,768]{1,0:T(8,128)(2,1)}) %all-gather.14.cloned.1.call-update) | async-done | bytes 1179664 | tf_op jit(solution)/shard_map/all_gather | solution.py:167
  260.4 47.5 %all-gather.16.cloned.1.call-done = bf16[768,768]{1,0:T(8,128)(2,1)} async-done(((bf16[24,768]{1,0:T(8,128)(2,1)}), bf16[768,768]{1,0:T(8,128)(2,1)}) %all-gather.16.cloned.1.call-update) | async-done | bytes 1179664 | tf_op jit(solution)/shard_map/all_gather | solution.py:169
  312.8 60.2 %all-gather.18.cloned.1.call-done = bf16[768,3072]{0,1:T(8,128)(2,1)} async-done(((bf16[768,96]{0,1:T(8,128)(2,1)}), bf16[768,3072]{0,1:T(8,128)(2,1)}) %all-gather.18.cloned.1.call-update) | async-done | bytes 4718608 | tf_op jit(solution)/shard_map/all_gather | solution.py:203
  373.0 8.2 fusion.70
  381.2 57.0 %all-gather.20.cloned.1.call-done = bf16[3072,768]{1,0:T(8,128)(2,1)} async-done(((bf16[96,768]{1,0:T(8,128)(2,1)}), bf16[3072,768]{1,0:T(8,128)(2,1)}) %all-gather.20.cloned.1.call-update) | async-done | bytes 4718608 | tf_op jit(solution)/shard_map/all_gather | solution.py:204
  438.2 20.1 %add_convert_fusion = (bf16[512,3072]{1,0:T(8,128)(2,1)S(1)}, f32[512,3072]{1,0:T(8,128)}) fusion(f32[512,3072]{1,0:T(8,128)} %fusion.70, bf16[512,768]{1,0:T(8,128)(2,1)} %param.33, bf16[3072,768]{1,0:T(8,128)(2,1)} %all-gather.20.cloned.1.call-done), kind=kOutput, calls=%fused_computation.17 | convolution fusion | flops 2529165312 | bytes 21233664 | tf_op jit(solution)/shard_map/td,fd->tf/dot_general | solution.py:219
  506.1 11.0 multiply_reduce_fusion
  519.0 7.1 multiply_convert_fusion
  540.0 8.3 fusion.69
  573.1 6.8 convolution_convert_fusion
  579.9 7.7 convert_element_type.231
  587.7 21.3 %reduce.15 = bf16[8,196608]{1,0:T(8,128)(2,1)} reduce(bf16[8,1,196608]{2,1,0:T(2,128)(2,1)} %convert_element_type.231, bf16[]{:T(256)} %broadcast.444), dimensions={1}, to_apply=%convert_element_type.231.reduce_sub_computation | reduce | bytes 6291458 | tf_op jit(solution)/shard_map/convert_element_type | solution.py:292
  609.0 6.4 reshape.366
  620.1 75.2 %all-reduce.6 = (f32[768]{0:T(1024)S(1)}, f32[768]{0:T(1024)S(1)}, f32[768]{0:T(1024)S(1)}) all-reduce(f32[768]{0:T(1024)S(1)} %copy-done.85, f32[768]{0:T(1024)S(1)} %copy-done.84, f32[768]{0:T(1024)S(1)} %copy-done.83), channel_id=2, replica_groups=mesh['dp'=8,'fsdp'=4] {'dp','fsdp'}, use_global_device_ids=true, to_apply=%region_23.24.clone | all-reduce | flops 2304 | bytes 18432
  705.9 7.8 reshape.367
  713.7 20.5 %reduce.5 = bf16[8,196608]{1,0:T(8,128)(2,1)} reduce(bf16[8,1,196608]{2,1,0:T(2,128)(2,1)} %reshape.367, bf16[]{:T(256)} %constant.186), dimensions={1}, to_apply=%all_to_all.28.reduce_sub_computation | reduce | bytes 6291458 | tf_op jit(solution)/shard_map/all_to_all | solution.py:291
  744.1 46.9 %reduce-scatter.10.cloned.1.call-done = f32[24,768]{1,0:T(8,128)} async-done(((f32[768,768]{1,0:T(8,128)}), f32[24,768]{1,0:T(8,128)}) %reduce-scatter.10.cloned.1.call-update) | async-done | bytes 73744 | tf_op jit(solution)/shard_map/reduce_scatter | solution.py:280
  791.0 113.0 %reduce-scatter.14.cloned.1.call-done = f32[768,48]{0,1:T(8,128)} async-done(((f32[768,1536]{0,1:T(8,128)}), f32[768,48]{0,1:T(8,128)}) %reduce-scatter.14.cloned.1.call-update) | async-done | bytes 147472 | tf_op jit(solution)/shard_map/reduce_scatter | solution.py:283
  904.0 124.3 %reduce-scatter.8.cloned.1.call-done = f32[768,72]{0,1:T(8,128)} async-done(((f32[768,2304]{0,1:T(8,128)}), f32[768,72]{0,1:T(8,128)}) %reduce-scatter.8.cloned.1.call-update) | async-done | bytes 221200 | tf_op jit(solution)/shard_map/reduce_scatter | solution.py:279
  1028.3 142.4 %reduce-scatter.18.cloned.1.call-done = f32[768,96]{0,1:T(8,128)} async-done(((f32[768,3072]{0,1:T(8,128)}), f32[768,96]{0,1:T(8,128)}) %reduce-scatter.18.cloned.1.call-update) | async-done | bytes 294928 | tf_op jit(solution)/shard_map/reduce_scatter | solution.py:229
  1170.7 141.0 %reduce-scatter.20.cloned.1.call-done = f32[96,768]{1,0:T(8,128)} async-done(((f32[3072,768]{1,0:T(8,128)}), f32[96,768]{1,0:T(8,128)}) %reduce-scatter.20.cloned.1.call-update) | async-done | bytes 294928 | tf_op jit(solution)/shard_map/reduce_scatter | solution.py:230
  (345 shorter events, 220.7 us)
Async XLA Ops:
  7.2 174.1 %copy-start = (bf16[128,768]{1,0:T(8,128)(2,1)S(1)}, bf16[128,768]{1,0:T(8,128)(2,1)}, u32[]{:S(2)}) copy-start(bf16[128,768]{1,0:T(8,128)(2,1)} %param.18) | copy-start | bytes 589828
  7.2 174.1 %all-gather.12.cloned.1.call-start = ((), (), s32[]{:S(2)}) async-start(), calls=%async_computation.13 | async-start | bytes 2433024 | tf_op jit(solution)/shard_map/all_gather | solution.py:168
  7.9 177.0 %all-gather.8.cloned.1.call-start = ((), (), s32[]{:S(2)}) async-start(), calls=%async_computation.11 | async-start | bytes 3649536 | tf_op jit(solution)/shard_map/all_gather | solution.py:164
  8.7 201.9 %all-gather.10.cloned.1.call-start = ((), (), s32[]{:S(2)}) async-start(), calls=%async_computation.12 | async-start | bytes 1216512 | tf_op jit(solution)/shard_map/all_gather | solution.py:165
  9.4 242.7 %all-gather.14.cloned.1.call-start = ((), (), s32[]{:S(2)}) async-start(), calls=%async_computation.14 | async-start | bytes 1216512 | tf_op jit(solution)/shard_map/all_gather | solution.py:167
  10.0 297.8 %all-gather.16.cloned.1.call-start = ((), (), s32[]{:S(2)}) async-start(), calls=%async_computation.15 | async-start | bytes 1216512 | tf_op jit(solution)/shard_map/all_gather | solution.py:169
  10.6 362.4 %all-gather.18.cloned.1.call-start = ((), (), s32[]{:S(2)}) async-start(), calls=%async_computation.16 | async-start | bytes 4866048 | tf_op jit(solution)/shard_map/all_gather | solution.py:203
  13.4 161.6 %copy-start.81 = (s32[4]{0:T(128)}, s32[4]{0:T(128)S(1)}, u32[]{:S(2)}) copy-start(s32[4]{0:T(128)S(1)} %fusion.58) | copy-start | bytes 52
  14.8 9.8 all-to-all-start
  24.6 7.8 all-to-all-start.1
  65.7 78.6 %copy-start.71 = (f32[4]{0:T(128)S(1)}, f32[4]{0:T(128)}, u32[]{:S(2)}) copy-start(f32[4]{0:T(128)} %param.22) | copy-start | bytes 52
  65.7 80.3 %all-to-all-start.2 = ((bf16[8,2,98304]{2,1,0:T(2,128)(2,1)}), bf16[8,2,98304]{2,1,0:T(2,128)(2,1)S(1)}, u32[]{:S(2)}, u32[]{:S(2)}) async-start(bf16[8,2,98304]{2,1,0:T(2,128)(2,1)} %reshape.364), calls=%async_computation.2 | async-start | bytes 6291456 | tf_op jit(solution)/shard_map/all_to_all | solution.py:146
  69.6 368.6 %all-gather.20.cloned.1.call-start = ((), (), s32[]{:S(2)}) async-start(), calls=%async_computation.17 | async-start | bytes 4866048 | tf_op jit(solution)/shard_map/all_gather | solution.py:204
  70.3 673.8 %reduce-scatter.16.cloned.1.call-start = ((), (), s32[]{:S(2)}) async-start(), calls=%async_computation.22 | async-start | bytes 2433024 | tf_op jit(solution)/shard_map/reduce_scatter | solution.py:284
  213.0 42.4 %copy-start.4 = (f32[512,768]{1,0:T(8,128)}, f32[512,768]{1,0:T(8,128)S(1)}, u32[]{:S(2)}) copy-start(f32[512,768]{1,0:T(8,128)S(1)} %get-tuple-element.152) | copy-start | bytes 4718596
  214.1 43.1 %copy-start.57 = (f32[512]{0:T(512)}, f32[512]{0:T(512)S(1)}, u32[]{:S(2)}) copy-start(f32[512]{0:T(512)S(1)} %fusion.55) | copy-start | bytes 6148
  466.9 277.2 %reduce-scatter.12.cloned.1.call-start = ((), (), s32[]{:S(2)}) async-start(), calls=%async_computation.20 | async-start | bytes 2433024 | tf_op jit(solution)/shard_map/reduce_scatter | solution.py:282
  482.5 308.5 %reduce-scatter.10.cloned.1.call-start = ((), (), s32[]{:S(2)}) async-start(), calls=%async_computation.19 | async-start | bytes 2433024 | tf_op jit(solution)/shard_map/reduce_scatter | solution.py:280
  492.1 411.8 %reduce-scatter.14.cloned.1.call-start = ((), (), s32[]{:S(2)}) async-start(), calls=%async_computation.21 | async-start | bytes 4866048 | tf_op jit(solution)/shard_map/reduce_scatter | solution.py:283
  500.2 528.0 %reduce-scatter.8.cloned.1.call-start = ((), (), s32[]{:S(2)}) async-start(), calls=%async_computation.18 | async-start | bytes 7299072 | tf_op jit(solution)/shard_map/reduce_scatter | solution.py:279
  538.6 632.0 %reduce-scatter.18.cloned.1.call-start = ((), (), s32[]{:S(2)}) async-start(), calls=%async_computation.23 | async-start | bytes 9732096 | tf_op jit(solution)/shard_map/reduce_scatter | solution.py:229
  548.4 763.3 %reduce-scatter.20.cloned.1.call-start = ((), (), s32[]{:S(2)}) async-start(), calls=%async_computation.24 | async-start | bytes 9732096 | tf_op jit(solution)/shard_map/reduce_scatter | solution.py:230
  615.4 81.6 %copy-start.41 = (bf16[12,64,128]{2,1,0:T(8,128)(2,1)S(1)}, bf16[12,64,128]{2,1,0:T(8,128)(2,1)}, u32[]{:S(2)}) copy-start(bf16[12,64,128]{2,1,0:T(8,128)(2,1)} %copy-done.40) | copy-start | bytes 589828
  615.5 90.4 %all-to-all-start.3 = ((bf16[8,2,98304]{2,1,0:T(2,128)(2,1)}), bf16[8,2,98304]{2,1,0:T(2,128)(2,1)}, u32[]{:S(2)}, u32[]{:S(2)}) async-start(bf16[8,2,98304]{2,1,0:T(2,128)(2,1)} %reshape.366), calls=%async_computation.3 | async-start | bytes 6291456 | tf_op jit(solution)/shard_map/all_to_all | solution.py:291
  (90 other events, 481.1 us)
Sparse Core Ops, SparseCore 0:
  10.8 60.3 all-gather.11
  74.0 66.5 all-gather.7
  143.3 53.0 all-gather.9
  199.1 53.0 all-gather.13
  254.8 53.0 all-gather.15
  310.5 62.4 all-gather.17
  375.8 62.3 all-gather.19
  467.0 97.8 reduce-scatter.15
  571.7 115.5 reduce-scatter.11
  692.9 97.9 reduce-scatter.9
  797.9 105.9 reduce-scatter.13
  910.1 118.1 reduce-scatter.7
  1035.8 134.8 reduce-scatter.17
  1177.0 134.6 reduce-scatter.19
where the time goes:
time: 1330 us; the launch traced here: 1320 us
  waiting for transfers between devices  779 us (59%)
  matrix products  151 us (11%)
  blocking collectives  147 us (11%)
  other arithmetic  116 us (9%)
  local copies, waits for them, and re-layouts  91.9 us (7%)
  starting transfers between devices  18 us (1%)
  between operations  15.2 us (1%)
    unnamed x2, blocking collectives  147 us
    reduce_scatter x1, waiting for transfers between devices, shards(): lax.psum_scatter(up_grad, ('dp', 'fsdp'), scatter_dimension=1, tiled=True)  142 us
    reduce_scatter x1, waiting for transfers between devices, shards(): lax.psum_scatter(down_grad, ('dp', 'fsdp'), scatter_dimension=0, tiled=True)  141 us
    reduce_scatter x1, waiting for transfers between devices, shards(): lax.psum_scatter(qkv_grad, ('dp', 'fsdp'), scatter_dimension=1, tiled=True)  124 us
    reduce_scatter x1, waiting for transfers between devices, shards(): lax.psum_scatter(ckv_grad, ('dp', 'fsdp'), scatter_dimension=1, tiled=True)  113 us
    all_gather x1, waiting for transfers between devices, shards(): lax.all_gather(w_up, ('dp', 'fsdp'), axis=1, tiled=True)  60.2 us
    all_gather x1, waiting for transfers between devices, shards(): lax.all_gather(w_down, ('dp', 'fsdp'), axis=0, tiled=True)  57 us
    all_gather x1, waiting for transfers between devices, shards(): lax.all_gather(w_cout, ('dp', 'fsdp'), axis=0, tiled=True)  47.5 us
  transfers between devices with their start and end apart: 18, of which 11 were waited for; matrix products, arithmetic and copies ran while one was open for 23% of the time, Pallas kernels for 0%

commit v1 on v0

v1 whole, which is shorter than its diff:
```python
import jax
import jax.numpy as jnp
from jax import lax
from jax.sharding import PartitionSpec as P

HEADS = 12
HEAD = 64
CORE = 1
f32 = jnp.float32
bf16 = jnp.bfloat16


def norm_rows(values, gain):
    centre = jnp.mean(values, axis=-1, keepdims=True)
    shifted = values - centre
    spread = jnp.mean(shifted * shifted, axis=-1, keepdims=True)
    return shifted * lax.rsqrt(spread + 1e-06) * gain


def exact_gelu(values):
    return jax.nn.gelu(values, approximate=False)


def swap(values, mask):
    count = lax.axis_size("dp")
    return lax.ppermute(values, "dp", [(i, i ^ mask) for i in range(count)])


def shift(values, step):
    count = lax.axis_size("fsdp")
    return lax.ppermute(values, "fsdp", [(i, (i + step) % count) for i in range(count)])


def link_masks(first):
    masks = []
    mask = 2
    while mask < lax.axis_size("dp"):
        masks.append(mask)
        mask *= 2
    return masks if first else masks[::-1]


def gather_inner(shard):
    count = lax.axis_size("fsdp")
    me = lax.axis_index("fsdp")
    came = [shard] + [shift(shard, step) for step in range(1, count)]
    line = [came[count - 1 - k] for k in range(count)] + [came[count - k] for k in range(1, count)]
    stacked = jnp.stack(line)
    part = lax.dynamic_slice_in_dim(stacked, count - 1 - me, count, 0)
    return part.reshape((count * shard.shape[0],) + shard.shape[1:])


def gather_outer(block, first):
    pieces = {0: block}
    for mask in link_masks(first):
        for e in list(pieces):
            pieces[e | mask] = swap(pieces[e], mask)
    for e in list(pieces):
        pieces[e | CORE] = swap(pieces[e], CORE)
    return pieces


def scatter_outer(pieces, first):
    now = dict(pieces)
    for e in list(now):
        if e & CORE:
            gone = now.pop(e)
            now[e ^ CORE] = now[e ^ CORE].astype(f32) + swap(gone.astype(bf16), CORE).astype(f32)
    for mask in link_masks(first)[::-1]:
        for e in list(now):
            if e & mask:
                gone = now.pop(e)
                now[e ^ mask] = now[e ^ mask].astype(f32) + swap(gone.astype(bf16), mask).astype(f32)
    return now[0]


def scatter_inner(block):
    count = lax.axis_size("fsdp")
    me = lax.axis_index("fsdp")
    parts = block.reshape((count, block.shape[0] // count) + block.shape[1:])
    low = parts.astype(bf16)
    total = lax.dynamic_index_in_dim(parts, me, 0, keepdims=False)
    for step in range(1, count):
        going = lax.dynamic_index_in_dim(low, (me + step) % count, 0, keepdims=False)
        total = total + shift(going, step).astype(f32)
    return total


def true_order(pieces):
    me = lax.axis_index("dp")
    stacked = jnp.stack([pieces[e] for e in range(len(pieces))])
    return jnp.concatenate(
        [lax.dynamic_index_in_dim(stacked, me ^ d, 0, keepdims=False) for d in range(len(pieces))]
    )


def relative_parts(values):
    count = lax.axis_size("dp")
    me = lax.axis_index("dp")
    rows = values.shape[0] // count
    return {e: lax.dynamic_slice_in_dim(values, (me ^ e) * rows, rows, 0) for e in range(count)}


def all_sum(values):
    mask = 1
    while mask < lax.axis_size("dp"):
        values = values + swap(values, mask)
        mask *= 2
    count = lax.axis_size("fsdp")
    mask = 1
    while mask < count:
        values = values + lax.ppermute(values, "fsdp", [(i, i ^ mask) for i in range(count)])
        mask *= 2
    return values


def masked_scores(query_rows, keys_all, same_video):
    scores = jnp.einsum("qhd,khd->hqk", query_rows, keys_all, preferred_element_type=f32)
    return jnp.where(same_video[None, :, :], scores, -1e30)


def attend_rows(queries, keys_all, values_all, same_video):
    row_count = queries.shape[0]
    model_width = queries.shape[1] * queries.shape[2]
    scores = masked_scores(queries, keys_all, same_video)
    largest = jnp.max(scores, axis=-1, keepdims=True)
    raised = jnp.exp(scores - largest)
    total_sum = jnp.sum(raised, axis=-1, keepdims=True)
    soft_low = (raised / total_sum).astype(bf16)
    rows = jnp.einsum("hqk,khd->qhd", soft_low, values_all, preferred_element_type=f32)
    return rows.reshape(row_count, model_width).astype(bf16), largest + jnp.log(total_sum)


def attend_grads(queries, keys_all, values_all, same_video, log_sums, grad_attended):
    row_count = queries.shape[0]
    key_count = keys_all.shape[0]
    model_width = queries.shape[1] * queries.shape[2]
    grad_heads = grad_attended.reshape(queries.shape)
    scores = masked_scores(queries, keys_all, same_video)
    soft_rows = jnp.exp(scores - log_sums)
    soft_low = soft_rows.astype(bf16)
    value_sum = jnp.einsum("hqk,qhd->khd", soft_low, grad_heads, preferred_element_type=f32)
    grad_soft = jnp.einsum("qhd,khd->hqk", grad_heads, values_all, preferred_element_type=f32)
    inner_sum = jnp.sum(soft_rows * grad_soft, axis=-1, keepdims=True)
    grad_scores = (soft_rows * (grad_soft - inner_sum)).astype(bf16)
    query_part = jnp.einsum("hqk,khd->qhd", grad_scores, keys_all, preferred_element_type=f32)
    key_sum = jnp.einsum("hqk,qhd->khd", grad_scores, queries, preferred_element_type=f32)
    return (
        query_part.astype(bf16).reshape(row_count, model_width),
        key_sum.reshape(key_count, model_width).astype(bf16),
        value_sum.reshape(key_count, model_width).astype(bf16),
    )


def dot_nn(a, b):
    return jnp.einsum("td,de->te", a, b, preferred_element_type=f32)


def dot_nt(a, b):
    return jnp.einsum("td,ed->te", a, b, preferred_element_type=f32)


def dot_tn(a, b):
    return jnp.einsum("td,te->de", a, b, preferred_element_type=f32)


def shards(
    tokens,
    coarse_view,
    segment_ids,
    partner_device,
    partner_slot,
    mix_weight,
    ln1_gain,
    w_qkv,
    w_out,
    lnx_gain,
    w_cq,
    w_ckv,
    w_cout,
    ln2_gain,
    w_up,
    w_down,
    cotangent,
):
    row_count, width = tokens.shape
    coarse_rows = coarse_view.shape[0]
    block_count = mix_weight.shape[0]
    clip_rows = row_count // block_count
    dp_count, fsdp_count = lax.axis_size("dp"), lax.axis_size("fsdp")
    dp_me, fsdp_me = lax.axis_index("dp"), lax.axis_index("fsdp")
    part = ln1_gain.shape[0]
    device_me = dp_me * fsdp_count + fsdp_me

    first_rows = (w_qkv.T, w_cq, w_out, w_ckv.T, w_cout)
    sizes = [w.shape[0] for w in first_rows]
    group_a1 = jnp.concatenate([w_qkv.T])
    group_a2 = jnp.concatenate([w_out, w_cq, w_ckv.T, w_cout])
    gains = jnp.stack([ln1_gain, lnx_gain, ln2_gain])
    gains_mine = lax.dynamic_update_slice(
        jnp.zeros((3, width), f32), gains.astype(f32), (0, device_me * part)
    )

    target = partner_device[:, 0]
    own = tokens
    masks = link_masks(True)
    token_pieces = gather_outer(own, True)
    token_stack = jnp.stack(
        [token_pieces[e].reshape(block_count, clip_rows, width) for e in range(dp_count)]
    ).reshape(dp_count * block_count, clip_rows, width)
    partner_at = (target ^ dp_me) * block_count + partner_slot
    partner_rows = jnp.stack(
        [
            lax.dynamic_index_in_dim(token_stack, partner_at[b], 0, keepdims=False)
            for b in range(block_count)
        ]
    ).astype(f32)
    mixing = mix_weight[:, None, None]
    own_blocks = own.reshape(block_count, clip_rows, width).astype(f32)
    blended = (mixing * own_blocks + (1.0 - mixing) * partner_rows).reshape(row_count, width)

    gain_one, gain_cross, gain_two = all_sum(gains_mine)

    qkv_t = true_order(gather_outer(gather_inner(w_qkv.T), True))
    out_full = true_order(gather_outer(gather_inner(w_out), False))
    cq_full = true_order(gather_outer(gather_inner(w_cq), True))
    ckv_t = true_order(gather_outer(gather_inner(w_ckv.T), False))
    cout_full = true_order(gather_outer(gather_inner(w_cout), True))
    up_pieces = gather_outer(gather_inner(w_up.T), True)
    down_pieces = gather_outer(gather_inner(w_down), False)
    up_t = jnp.concatenate([up_pieces[e] for e in range(dp_count)])
    down_full = jnp.concatenate([down_pieces[e] for e in range(dp_count)])

    segments = segment_ids[0]
    coarse_seg = segments.reshape(coarse_rows, row_count // coarse_rows)[:, 0]
    self_same = segments[:, None] == segments[None, :]
    cross_same = segments[:, None] == coarse_seg[None, :]

    normed = norm_rows(blended, gain_one).astype(bf16)
    projected = dot_nt(normed, qkv_t)
    queries = (projected[:, :width] * 0.125).astype(bf16).reshape(row_count, HEADS, HEAD)
    keys_all = projected[:, width : 2 * width].astype(bf16).reshape(row_count, HEADS, HEAD)
    values_all = projected[:, 2 * width :].astype(bf16).reshape(row_count, HEADS, HEAD)
    attended, self_lse = attend_rows(queries, keys_all, values_all, self_same)
    residual = blended + dot_nn(attended, out_full)
    crossed_in = norm_rows(residual, gain_cross).astype(bf16)
    cross_q = (dot_nn(crossed_in, cq_full) * 0.125).astype(bf16).reshape(row_count, HEADS, HEAD)
    coarse_proj = dot_nt(coarse_view, ckv_t)
    cross_k = coarse_proj[:, :width].astype(bf16).reshape(coarse_rows, HEADS, HEAD)
    cross_v = coarse_proj[:, width:].astype(bf16).reshape(coarse_rows, HEADS, HEAD)
    crossed, cross_lse = attend_rows(cross_q, cross_k, cross_v, cross_same)
    joined = residual + dot_nn(crossed, cout_full)
    second = norm_rows(joined, gain_two).astype(bf16)
    pre_act = dot_nt(second, up_t)
    hidden = exact_gelu(pre_act).astype(bf16)
    output = (joined + dot_nn(hidden, down_full)).astype(bf16)

    grad_hidden = dot_nt(cotangent, down_full)
    gelu_value, gelu_pull = jax.vjp(exact_gelu, pre_act)
    grad_pre = gelu_pull(grad_hidden)[0].astype(bf16)
    down_grad = dot_tn(hidden, cotangent)
    up_grad = dot_tn(grad_pre, second)
    grad_second = dot_nn(grad_pre, up_t)
    norm_value, norm_pull = jax.vjp(norm_rows, joined, gain_two)
    grad_joined_norm, ln2_piece = norm_pull(grad_second)
    grad_joined = cotangent.astype(f32) + grad_joined_norm

    rows = up_grad.shape[0] // dp_count
    up_shard = scatter_inner(
        scatter_outer({e: up_grad[e * rows : (e + 1) * rows] for e in range(dp_count)}, True)
    ).T
    down_shard = scatter_inner(
        scatter_outer({e: down_grad[e * rows : (e + 1) * rows] for e in range(dp_count)}, False)
    )

    grad_joined_low = grad_joined.astype(bf16)
    cout_grad = dot_tn(crossed, grad_joined_low)
    grad_crossed = dot_nt(grad_joined_low, cout_full).astype(bf16)
    cq_part, ck_part, cv_part = attend_grads(
        cross_q, cross_k, cross_v, cross_same, cross_lse, grad_crossed
    )
    grad_cq = cq_part * 0.125
    cq_grad = dot_tn(crossed_in, grad_cq)
    grad_crossed_in = dot_nt(grad_cq, cq_full)
    grad_ckv = jnp.concatenate([ck_part, cv_part], axis=1)
    ckv_grad = dot_tn(grad_ckv, coarse_view)
    coarse_grad = dot_nn(grad_ckv, ckv_t)
    cross_value, cross_pull = jax.vjp(norm_rows, residual, gain_cross)
    grad_res_norm, lnx_piece = cross_pull(grad_crossed_in)
    grad_residual = grad_joined + grad_res_norm
    grad_res_low = grad_residual.astype(bf16)
    out_grad = dot_tn(attended, grad_res_low)
    grad_attended = dot_nt(grad_res_low, out_full).astype(bf16)
    query_part, key_part, value_part = attend_grads(
        queries, keys_all, values_all, self_same, self_lse, grad_attended
    )
    grad_projected = jnp.concatenate([query_part * 0.125, key_part, value_part], axis=1)
    qkv_grad = dot_tn(grad_projected, normed)
    grad_normed = dot_nn(grad_projected, qkv_t)
    first_value, first_pull = jax.vjp(norm_rows, blended, gain_one)
    grad_blend_norm, ln1_piece = first_pull(grad_normed)
    grad_blended = grad_residual + grad_blend_norm

    def reduce_shard(values, first):
        return scatter_inner(scatter_outer(relative_parts(values), first))

    cout_shard = reduce_shard(cout_grad, True)
    cq_shard = reduce_shard(cq_grad, True)
    ckv_shard = reduce_shard(ckv_grad, False).T
    out_shard = reduce_shard(out_grad, False)
    qkv_shard = reduce_shard(qkv_grad, True).T

    gain_sums = all_sum(jnp.stack([ln1_piece, lnx_piece, ln2_piece]))
    gain_mine = lax.dynamic_slice(gain_sums, (0, device_me * part), (3, part))

    grad_blocks = grad_blended.reshape(block_count, clip_rows, width)
    send_blocks = ((1.0 - mixing) * grad_blocks).reshape(block_count, clip_rows * width)
    places = jnp.arange(dp_count * block_count, dtype=jnp.int32)
    chosen = (places[:, None] == partner_at[None, :]).astype(bf16)
    outgoing = jnp.dot(chosen, send_blocks.astype(bf16), preferred_element_type=f32)
    outgoing = outgoing.reshape(dp_count, row_count, width)
    incoming = scatter_outer({e: outgoing[e] for e in range(dp_count)}, True)
    token_grad = (mixing * grad_blocks).reshape(row_count, width) + incoming
    return (
        output,
        token_grad,
        coarse_grad,
        gain_mine[0],
        qkv_shard,
        out_shard,
        gain_mine[1],
        cq_shard,
        ckv_shard,
        cout_shard,
        gain_mine[2],
        up_shard,
        down_shard,
    )


def solution(mesh):
    rows = P(("dp", "fsdp"), None)
    columns = P(None, ("dp", "fsdp"))
    line = P(("dp", "fsdp"))
    in_specs = (
        rows, rows, rows, rows, line, line, line, columns, rows,
        line, rows, columns, rows, line, columns, rows, rows,
    )
    out_specs = (
        rows, rows, rows, line, columns, rows, line, rows, columns, rows, line, columns, rows,
    )
    return jax.shard_map(shards, mesh=mesh, in_specs=in_specs, out_specs=out_specs, check_vma=False)
```

time: 1330 us -> 682 us (0.51)
  waiting for transfers between devices: 779 us -> 280 us
  blocking collectives: 147 us -> 0 us
  starting transfers between devices: 18 us -> 138 us
  other arithmetic: 116 us -> 56.7 us
  matrix products: 151 us -> 113 us
  local copies, waits for them, and re-layouts: 91.9 us -> 77.5 us
    reduce_scatter x7 -> x0, waiting for transfers between devices: 568 us -> none  [the longest x1 142 us: shards(): lax.psum_scatter(up_grad, ('dp', 'fsdp'), scatter_dimension=1, tiled=True)]
    ppermute x0 -> x164, waiting for transfers between devices: none -> 280 us  [the longest x118 222 us: swap(): return lax.ppermute(values, 'dp', [(i, i ^ mask) for i in range(count)])]
    all_gather x7 -> x0, waiting for transfers between devices: 203 us -> none  [the longest x1 60.2 us: shards(): lax.all_gather(w_up, ('dp', 'fsdp'), axis=1, tiled=True)]
    unnamed x2 -> x0, blocking collectives: 147 us -> none
    ppermute x0 -> x164, starting transfers between devices: none -> 138 us  [the longest x118 70.6 us: swap(): return lax.ppermute(values, 'dp', [(i, i ^ mask) for i in range(count)])]
    all_to_all x4 -> x0, other arithmetic: 61.2 us -> none  [the longest x2 40.1 us: shards(): lax.all_to_all(reply.reshape(peer_count, CAP * clip_rows * model_width),...]
    dot_general x37 -> x34, matrix products: 151 us -> 113 us  [the longest x7 35.1 us: dot_nt(): return jnp.einsum('td,ed->te', a, b, preferred_element_type=f32)]
    unnamed x205 -> x375, local copies, waits for them, and re-layouts: 47 us -> 14.5 us
  transfers between devices with their start and end apart: 18 -> 164, of which waited for: 11 -> 61; matrix products, arithmetic and copies ran while one was open for 23% -> 14% of each run, Pallas kernels for 0% -> 0%
where the time goes in v1:
time: 682 us; the launch traced here: 676 us
  waiting for transfers between devices  280 us (41%)
  starting transfers between devices  138 us (20%)
  matrix products  113 us (17%)
  local copies, waits for them, and re-layouts  77.5 us (11%)
  other arithmetic  56.7 us (8%)
  between operations  12.1 us (2%)
    ppermute x118, waiting for transfers between devices, swap(): return lax.ppermute(values, 'dp', [(i, i ^ mask) for i in range(count)])  222 us
    ppermute x118, starting transfers between devices, swap(): return lax.ppermute(values, 'dp', [(i, i ^ mask) for i in range(count)])  70.6 us
    ppermute x42, starting transfers between devices, shift(): lax.ppermute(values, 'fsdp', [(i, (i + step) % count) for i in range(coun...  60.6 us
    ppermute x42, waiting for transfers between devices, shift(): lax.ppermute(values, 'fsdp', [(i, (i + step) % count) for i in range(coun...  51 us
    dot_general x7, matrix products, dot_nt(): return jnp.einsum('td,ed->te', a, b, preferred_element_type=f32)  35.1 us
    dot_general x7, matrix products, dot_tn(): return jnp.einsum('td,te->de', a, b, preferred_element_type=f32)  28.3 us
    convert_element_type x9, local copies, waits for them, and re-layouts, scatter_outer(): gone.astype(bf16)  22.9 us
    convert_element_type x17, other arithmetic, scatter_outer(): gone.astype(bf16)  14.8 us
  transfers between devices with their start and end apart: 164, of which 61 were waited for; matrix products, arithmetic and copies ran while one was open for 14% of the time, Pallas kernels for 0%

profile of v1, /device:TPU:0, one launch (start us, length us, event | category | flops | bytes accessed | tf_op | source)
XLA Modules:
  0.0 676.5 jit_solution(16181581382163338181)
XLA Ops:
  101.1 6.1 collective-permute-done.26
  116.7 6.0 collective-permute-done.28
  127.9 10.1 %collective-permute-done.30 = bf16[96,768]{1,0:T(8,128)(2,1)S(1)} collective-permute-done((bf16[96,768]{1,0:T(8,128)(2,1)S(1)}, bf16[96,768]{1,0:T(8,128)(2,1)S(1)}, u32[]{:S(2)}, u32[]{:S(2)}) %collective-permute-start.30) | collective-permute-done | bytes 147488 | tf_op jit(solution)/shard_map/ppermute | solution.py:26
  177.5 10.5 %collective-permute-done.66 = bf16[384,768]{1,0:T(8,128)(2,1)S(1)} collective-permute-done((bf16[384,768]{1,0:T(8,128)(2,1)S(1)}, bf16[384,768]{1,0:T(8,128)(2,1)S(1)}, u32[]{:S(2)}, u32[]{:S(2)}) %collective-permute-start.66) | collective-permute-done | bytes 589856 | tf_op jit(solution)/shard_map/ppermute | solution.py:26
  190.2 24.9 %collective-permute-done.76 = bf16[384,768]{1,0:T(8,128)(2,1)S(1)} collective-permute-done((bf16[384,768]{1,0:T(8,128)(2,1)S(1)}, bf16[384,768]{1,0:T(8,128)(2,1)S(1)}, u32[]{:S(2)}, u32[]{:S(2)}) %collective-permute-start.76) | collective-permute-done | bytes 589856 | tf_op jit(solution)/shard_map/ppermute | solution.py:26
  223.0 8.4 %collective-permute-done.68 = bf16[384,768]{1,0:T(8,128)(2,1)S(1)} collective-permute-done((bf16[384,768]{1,0:T(8,128)(2,1)S(1)}, bf16[384,768]{1,0:T(8,128)(2,1)S(1)}, u32[]{:S(2)}, u32[]{:S(2)}) %collective-permute-start.68) | collective-permute-done | bytes 589856 | tf_op jit(solution)/shard_map/ppermute | solution.py:26
  231.8 9.0 %collective-permute-done.20 = bf16[288,768]{1,0:T(8,128)(2,1)S(1)} collective-permute-done((bf16[288,768]{1,0:T(8,128)(2,1)S(1)}, bf16[288,768]{1,0:T(8,128)(2,1)S(1)}, u32[]{:S(2)}, u32[]{:S(2)}) %collective-permute-start.20) | collective-permute-done | bytes 442400 | tf_op jit(solution)/shard_map/ppermute | solution.py:26
  245.5 12.2 %collective-permute-done.3 = bf16[512,768]{1,0:T(8,128)(2,1)S(1)} collective-permute-done((bf16[512,768]{1,0:T(8,128)(2,1)S(1)}, bf16[512,768]{1,0:T(8,128)(2,1)S(1)}, u32[]{:S(2)}, u32[]{:S(2)}) %collective-permute-start.3) | collective-permute-done | bytes 786464 | tf_op jit(solution)/shard_map/ppermute | solution.py:26
  258.3 12.1 %collective-permute-done.70 = bf16[384,768]{1,0:T(8,128)(2,1)S(1)} collective-permute-done((bf16[384,768]{1,0:T(8,128)(2,1)S(1)}, bf16[384,768]{1,0:T(8,128)(2,1)S(1)}, u32[]{:S(2)}, u32[]{:S(2)}) %collective-permute-start.70) | collective-permute-done | bytes 589856 | tf_op jit(solution)/shard_map/ppermute | solution.py:26
  271.3 15.5 %collective-permute-done.5 = bf16[512,768]{1,0:T(8,128)(2,1)S(1)} collective-permute-done((bf16[512,768]{1,0:T(8,128)(2,1)S(1)}, bf16[512,768]{1,0:T(8,128)(2,1)S(1)}, u32[]{:S(2)}, u32[]{:S(2)}) %collective-permute-start.5) | collective-permute-done | bytes 786464 | tf_op jit(solution)/shard_map/ppermute | solution.py:26
  324.2 19.0 %multiply_convert_fusion.1 = (bf16[512,3072]{1,0:T(8,128)(2,1)}, f32[512,3072]{1,0:T(8,128)S(1)}, f32[512,3072]{1,0:T(8,128)}) fusion(bf16[3072,768]{1,0:T(8,128)(2,1)S(1)} %bitcast.592, f32[512,768]{1,0:T(8,128)S(1)} %get-tuple-element.127, f32[768]{0:T(1024)S(1)} %get-tuple-element.19, f32[512]{0:T(512)S(1)} %fusion.86, f32[512]{0:T(512)S(1)} %broadcast_multiply_fusion), kind=kOutput, calls=%fused_computation.21 | convolution fusion | flops 2519728128 | bytes 22027264 | tf_op jit(solution)/shard_map/td,ed->te/dot_general | solution.py:160
  343.3 6.3 fusion.10
  382.2 6.6 fusion.117
  392.4 6.5 fusion.118
  400.3 8.4 %fusion.33 = bf16[12,64,512]{2,1,0:T(8,128)(2,1)} fusion(bf16[512,12,64]{0,2,1:T(8,128)(2,1)S(1)} %bitcast.512, f32[12,512,512]{1,2,0:T(8,128)} %copy-done.1, f32[12,512]{1,0:T(8,128)S(1)} %copy-done.64, pred[512,512]{0,1:T(8,128)(4,1)S(1)} %copy-done.22), kind=kOutput, calls=%fused_computation.88 | convolution fusion | flops 412483584 | bytes 14442496 | tf_op jit(solution)/shard_map/hqk,qhd->khd/dot_general | solution.py:142
  408.7 9.3 %multiply_reduce_fusion = (f32[12,512]{1,0:T(8,128)S(1)}, f32[12,512,512]{1,2,0:T(8,128)}) fusion(f32[12,512,512]{1,2,0:T(8,128)} %copy-done.1, f32[12,512]{1,0:T(8,128)S(1)} %copy-done.64, pred[512,512]{0,1:T(8,128)(4,1)S(1)} %copy-done.22, bf16[512,12,64]{0,2,1:T(8,128)(2,1)S(1)} %bitcast.513, bf16[512,12,64]{0,2,1:T(8,128)(2,1)S(1)} %bitcast.511), kind=kOutput, calls=%fused_computation.1 | convolution fusion | flops 415229952 | bytes 27049984 | tf_op jit(solution)/shard_map/qhd,khd->hqk/dot_general | solution.py:143
  418.0 7.4 %multiply_convert_fusion = bf16[12,512,512]{1,2,0:T(8,128)(2,1)S(1)} fusion(f32[12,512,512]{1,2,0:T(8,128)} %get-tuple-element.134, f32[12,512,512]{1,2,0:T(8,128)S(1)} %bitcast.495, f32[12,512]{1,0:T(8,128)S(1)} %get-tuple-element.133, f32[12,512]{1,0:T(8,128)S(1)} %copy-done.64, pred[512,512]{0,1:T(8,128)(4,1)S(1)} %copy-done.22), kind=kLoop, calls=%fused_computation | loop fusion | flops 15728640 | bytes 31768576 | tf_op jit(solution)/shard_map/convert_element_type | solution.py:145
  571.8 7.9 %collective-permute-done.99 = bf16[288,768]{1,0:T(8,128)(2,1)S(1)} collective-permute-done((bf16[288,768]{1,0:T(8,128)(2,1)S(1)}, bf16[288,768]{1,0:T(8,128)(2,1)S(1)}, u32[]{:S(2)}, u32[]{:S(2)}) %collective-permute-start.99) | collective-permute-done | bytes 442400 | tf_op jit(solution)/shard_map/ppermute | solution.py:26
  593.6 9.9 %collective-permute-done.159 = bf16[384,768]{1,0:T(8,128)(2,1)S(1)} collective-permute-done((bf16[384,768]{1,0:T(8,128)(2,1)S(1)}, bf16[384,768]{1,0:T(8,128)(2,1)S(1)}, u32[]{:S(2)}, u32[]{:S(2)}) %collective-permute-start.159) | collective-permute-done | bytes 589856 | tf_op jit(solution)/shard_map/ppermute | solution.py:26
  613.1 7.0 %collective-permute-done.87 = bf16[512,768]{1,0:T(8,128)(2,1)S(1)} collective-permute-done((bf16[512,768]{1,0:T(8,128)(2,1)S(1)}, bf16[512,768]{1,0:T(8,128)(2,1)S(1)}, u32[]{:S(2)}, u32[]{:S(2)}) %collective-permute-start.87) | collective-permute-done | bytes 786464 | tf_op jit(solution)/shard_map/ppermute | solution.py:26
  622.0 10.8 %collective-permute-done.146 = bf16[384,768]{1,0:T(8,128)(2,1)S(1)} collective-permute-done((bf16[384,768]{1,0:T(8,128)(2,1)S(1)}, bf16[384,768]{1,0:T(8,128)(2,1)S(1)}, u32[]{:S(2)}, u32[]{:S(2)}) %collective-permute-start.146) | collective-permute-done | bytes 589856 | tf_op jit(solution)/shard_map/ppermute | solution.py:26
  637.6 7.3 %collective-permute-done.160 = bf16[384,768]{1,0:T(8,128)(2,1)S(1)} collective-permute-done((bf16[384,768]{1,0:T(8,128)(2,1)S(1)}, bf16[384,768]{1,0:T(8,128)(2,1)S(1)}, u32[]{:S(2)}, u32[]{:S(2)}) %collective-permute-start.160) | collective-permute-done | bytes 589856 | tf_op jit(solution)/shard_map/ppermute | solution.py:26
  653.2 10.7 %collective-permute-done.152 = bf16[96,768]{1,0:T(8,128)(2,1)S(1)} collective-permute-done((bf16[96,768]{1,0:T(8,128)(2,1)S(1)}, bf16[96,768]{1,0:T(8,128)(2,1)S(1)}, u32[]{:S(2)}, u32[]{:S(2)}) %collective-permute-start.152) | collective-permute-done | bytes 147488 | tf_op jit(solution)/shard_map/ppermute | solution.py:31
  664.7 6.2 collective-permute-done.163
  (879 shorter events, 426.2 us)
Async XLA Ops:
  0.7 51.5 %collective-permute-start.23 = (bf16[24,768]{1,0:T(8,128)(2,1)}, bf16[24,768]{1,0:T(8,128)(2,1)S(1)}, u32[]{:S(2)}, u32[]{:S(2)}) collective-permute-start(bf16[24,768]{1,0:T(8,128)(2,1)} %param.25), channel_id=1, source_target_pairs={{0,2},{1,3},{2,0},{3,1},{4,6},{5,7},{6,4},{7,5},{8,10},{9,11},{10,... | collective-permute-start | bytes 110600 | tf_op jit(solution)/shard_map/ppermute | solution.py:31
  4.8 47.3 %collective-permute-start.22 = (bf16[24,768]{1,0:T(8,128)(2,1)}, bf16[24,768]{1,0:T(8,128)(2,1)S(1)}, u32[]{:S(2)}, u32[]{:S(2)}) collective-permute-start(bf16[24,768]{1,0:T(8,128)(2,1)} %param.25), channel_id=1, source_target_pairs={{0,3},{1,0},{2,1},{3,2},{4,7},{5,4},{6,5},{7,6},{8,11},{9,8},{10,9... | collective-permute-start | bytes 110600 | tf_op jit(solution)/shard_map/ppermute | solution.py:31
  6.2 52.0 %collective-permute-start.24 = (bf16[24,768]{1,0:T(8,128)(2,1)}, bf16[24,768]{1,0:T(8,128)(2,1)S(1)}, u32[]{:S(2)}, u32[]{:S(2)}) collective-permute-start(bf16[24,768]{1,0:T(8,128)(2,1)} %param.25), channel_id=1, source_target_pairs={{0,1},{1,2},{2,3},{3,0},{4,5},{5,6},{6,7},{7,4},{8,9},{9,10},{10,1... | collective-permute-start | bytes 110600 | tf_op jit(solution)/shard_map/ppermute | solution.py:31
  68.7 30.8 %collective-permute-start.64 = (bf16[96,768]{1,0:T(8,128)(2,1)S(1)}, bf16[96,768]{1,0:T(8,128)(2,1)S(1)}, u32[]{:S(2)}, u32[]{:S(2)}) collective-permute-start(bf16[96,768]{1,0:T(8,128)(2,1)S(1)} %bitcast.581), channel_id=1, source_target_pairs={{0,1},{1,2},{2,3},{3,0},{4,5},{5,6},{6,7},{7,4},{8,9},{9,10},{10,1... | collective-permute-start | bytes 442376 | tf_op jit(solution)/shard_map/ppermute | solution.py:31
  68.8 30.6 %collective-permute-start.63 = (bf16[96,768]{1,0:T(8,128)(2,1)S(1)}, bf16[96,768]{1,0:T(8,128)(2,1)S(1)}, u32[]{:S(2)}, u32[]{:S(2)}) collective-permute-start(bf16[96,768]{1,0:T(8,128)(2,1)S(1)} %bitcast.582), channel_id=1, source_target_pairs={{0,2},{1,3},{2,0},{3,1},{4,6},{5,7},{6,4},{7,5},{8,10},{9,11},{10,... | collective-permute-start | bytes 442376 | tf_op jit(solution)/shard_map/ppermute | solution.py:31
  92.7 122.5 %collective-permute-start = (bf16[512,768]{1,0:T(8,128)(2,1)S(1)}, bf16[512,768]{1,0:T(8,128)(2,1)S(1)}, u32[]{:S(2)}, u32[]{:S(2)}) collective-permute-start(bf16[512,768]{1,0:T(8,128)(2,1)S(1)} %copy-done.35), channel_id=1, source_target_pairs={{0,4},{4,0},{8,12},{12,8},{16,20},{20,16},{24,28},{28,24},{1,5},{5... | collective-permute-start | bytes 2359304 | tf_op jit(solution)/shard_map/ppermute | solution.py:26
  95.3 45.5 %collective-permute-start.58 = (bf16[96,768]{1,0:T(8,128)(2,1)S(1)}, bf16[96,768]{1,0:T(8,128)(2,1)S(1)}, u32[]{:S(2)}, u32[]{:S(2)}) collective-permute-start(bf16[96,768]{1,0:T(8,128)(2,1)S(1)} %bitcast.567), channel_id=1, source_target_pairs={{0,16},{4,20},{8,24},{12,28},{16,0},{20,4},{24,8},{28,12},{1,17},{... | collective-permute-start | bytes 442376 | tf_op jit(solution)/shard_map/ppermute | solution.py:26
  122.7 39.3 %collective-permute-start.38 = (bf16[192,768]{1,0:T(8,128)(2,1)S(1)}, bf16[192,768]{1,0:T(8,128)(2,1)S(1)}, u32[]{:S(2)}, u32[]{:S(2)}) collective-permute-start(bf16[192,768]{1,0:T(8,128)(2,1)S(1)} %bitcast.550), channel_id=1, source_target_pairs={{0,16},{4,20},{8,24},{12,28},{16,0},{20,4},{24,8},{28,12},{1,17},{... | collective-permute-start | bytes 884744 | tf_op jit(solution)/shard_map/ppermute | solution.py:26
  125.7 29.2 %collective-permute-start.36 = (bf16[192,768]{1,0:T(8,128)(2,1)S(1)}, bf16[192,768]{1,0:T(8,128)(2,1)S(1)}, u32[]{:S(2)}, u32[]{:S(2)}) collective-permute-start(bf16[192,768]{1,0:T(8,128)(2,1)S(1)} %bitcast.551), channel_id=1, source_target_pairs={{0,8},{4,12},{8,0},{12,4},{16,24},{20,28},{24,16},{28,20},{1,9},{5... | collective-permute-start | bytes 884744 | tf_op jit(solution)/shard_map/ppermute | solution.py:26
  159.6 30.3 %collective-permute-start.75 = (bf16[384,768]{1,0:T(8,128)(2,1)S(1)}, bf16[384,768]{1,0:T(8,128)(2,1)S(1)}, u32[]{:S(2)}, u32[]{:S(2)}) collective-permute-start(bf16[384,768]{1,0:T(8,128)(2,1)S(1)} %bitcast.528), channel_id=1, source_target_pairs={{0,4},{4,0},{8,12},{12,8},{16,20},{20,16},{24,28},{28,24},{1,5},{5... | collective-permute-start | bytes 1769480 | tf_op jit(solution)/shard_map/ppermute | solution.py:26
  175.4 41.7 %collective-permute-start.1 = (bf16[512,768]{1,0:T(8,128)(2,1)S(1)}, bf16[512,768]{1,0:T(8,128)(2,1)S(1)}, u32[]{:S(2)}, u32[]{:S(2)}) collective-permute-start(bf16[512,768]{1,0:T(8,128)(2,1)S(1)} %copy-done.35), channel_id=1, source_target_pairs={{0,8},{4,12},{8,0},{12,4},{16,24},{20,28},{24,16},{28,20},{1,9},{5... | collective-permute-start | bytes 2359304 | tf_op jit(solution)/shard_map/ppermute | solution.py:26
  175.4 39.7 %collective-permute-start.76 = (bf16[384,768]{1,0:T(8,128)(2,1)S(1)}, bf16[384,768]{1,0:T(8,128)(2,1)S(1)}, u32[]{:S(2)}, u32[]{:S(2)}) collective-permute-start(bf16[384,768]{1,0:T(8,128)(2,1)S(1)} %bitcast.529), channel_id=1, source_target_pairs={{0,8},{4,12},{8,0},{12,4},{16,24},{20,28},{24,16},{28,20},{1,9},{5... | collective-permute-start | bytes 1769480 | tf_op jit(solution)/shard_map/ppermute | solution.py:26
  188.0 29.4 %collective-permute-start.18 = (bf16[288,768]{1,0:T(8,128)(2,1)S(1)}, bf16[288,768]{1,0:T(8,128)(2,1)S(1)}, u32[]{:S(2)}, u32[]{:S(2)}) collective-permute-start(bf16[288,768]{1,0:T(8,128)(2,1)S(1)} %bitcast.540), channel_id=1, source_target_pairs={{0,16},{4,20},{8,24},{12,28},{16,0},{20,4},{24,8},{28,12},{1,17},{... | collective-permute-start | bytes 1327112 | tf_op jit(solution)/shard_map/ppermute | solution.py:26
  189.8 31.3 %collective-permute-start.78 = (bf16[384,768]{1,0:T(8,128)(2,1)S(1)}, bf16[384,768]{1,0:T(8,128)(2,1)S(1)}, u32[]{:S(2)}, u32[]{:S(2)}) collective-permute-start(bf16[384,768]{1,0:T(8,128)(2,1)S(1)} %bitcast.530), channel_id=1, source_target_pairs={{0,16},{4,20},{8,24},{12,28},{16,0},{20,4},{24,8},{28,12},{1,17},{... | collective-permute-start | bytes 1769480 | tf_op jit(solution)/shard_map/ppermute | solution.py:26
  221.2 36.5 %collective-permute-start.3 = (bf16[512,768]{1,0:T(8,128)(2,1)S(1)}, bf16[512,768]{1,0:T(8,128)(2,1)S(1)}, u32[]{:S(2)}, u32[]{:S(2)}) collective-permute-start(bf16[512,768]{1,0:T(8,128)(2,1)S(1)} %copy-done.35), channel_id=1, source_target_pairs={{0,16},{4,20},{8,24},{12,28},{16,0},{20,4},{24,8},{28,12},{1,17},{... | collective-permute-start | bytes 2359304 | tf_op jit(solution)/shard_map/ppermute | solution.py:26
  241.6 28.8 %collective-permute-start.70 = (bf16[384,768]{1,0:T(8,128)(2,1)S(1)}, bf16[384,768]{1,0:T(8,128)(2,1)S(1)}, u32[]{:S(2)}, u32[]{:S(2)}) collective-permute-start(bf16[384,768]{1,0:T(8,128)(2,1)S(1)} %collective-permute-done.66), channel_id=1, source_target_pairs={{0,16},{4,20},{8,24},{12,28},{16,0},{20,4},{24,8},{28,12},{1,17},{... | collective-permute-start | bytes 1769480 | tf_op jit(solution)/shard_map/ppermute | solution.py:26
  243.7 43.1 %collective-permute-start.5 = (bf16[512,768]{1,0:T(8,128)(2,1)S(1)}, bf16[512,768]{1,0:T(8,128)(2,1)S(1)}, u32[]{:S(2)}, u32[]{:S(2)}) collective-permute-start(bf16[512,768]{1,0:T(8,128)(2,1)S(1)} %collective-permute-done.1), channel_id=1, source_target_pairs={{0,16},{4,20},{8,24},{12,28},{16,0},{20,4},{24,8},{28,12},{1,17},{... | collective-permute-start | bytes 2359304 | tf_op jit(solution)/shard_map/ppermute | solution.py:26
  257.7 29.2 %collective-permute-start.2 = (bf16[512,768]{1,0:T(8,128)(2,1)S(1)}, bf16[512,768]{1,0:T(8,128)(2,1)S(1)}, u32[]{:S(2)}, u32[]{:S(2)}) collective-permute-start(bf16[512,768]{1,0:T(8,128)(2,1)S(1)} %collective-permute-done.1), channel_id=1, source_target_pairs={{0,4},{4,0},{8,12},{12,8},{16,20},{20,16},{24,28},{28,24},{1,5},{5... | collective-permute-start | bytes 2359304 | tf_op jit(solution)/shard_map/ppermute | solution.py:26
  257.7 29.3 %collective-permute-start.4 = (bf16[512,768]{1,0:T(8,128)(2,1)S(1)}, bf16[512,768]{1,0:T(8,128)(2,1)S(1)}, u32[]{:S(2)}, u32[]{:S(2)}) collective-permute-start(bf16[512,768]{1,0:T(8,128)(2,1)S(1)} %collective-permute-done.3), channel_id=1, source_target_pairs={{0,4},{4,0},{8,12},{12,8},{16,20},{20,16},{24,28},{28,24},{1,5},{5... | collective-permute-start | bytes 2359304 | tf_op jit(solution)/shard_map/ppermute | solution.py:26
  439.8 81.9 %collective-permute-start.134 = (bf16[96,768]{1,0:T(8,128)(2,1)}, bf16[96,768]{1,0:T(8,128)(2,1)S(1)}, u32[]{:S(2)}, u32[]{:S(2)}) collective-permute-start(bf16[96,768]{1,0:T(8,128)(2,1)} %get-tuple-element.68), channel_id=1, source_target_pairs={{0,4},{4,0},{8,12},{12,8},{16,20},{20,16},{24,28},{28,24},{1,5},{5... | collective-permute-start | bytes 442376 | tf_op jit(solution)/shard_map/ppermute | solution.py:26
  440.3 57.0 %collective-permute-start.138 = (bf16[96,768]{1,0:T(8,128)(2,1)}, bf16[96,768]{1,0:T(8,128)(2,1)}, u32[]{:S(2)}, u32[]{:S(2)}) collective-permute-start(bf16[96,768]{1,0:T(8,128)(2,1)} %get-tuple-element.69), channel_id=1, source_target_pairs={{0,4},{4,0},{8,12},{12,8},{16,20},{20,16},{24,28},{28,24},{1,5},{5... | collective-permute-start | bytes 442376 | tf_op jit(solution)/shard_map/ppermute | solution.py:26
  440.3 57.4 %collective-permute-start.135 = (bf16[96,768]{1,0:T(8,128)(2,1)}, bf16[96,768]{1,0:T(8,128)(2,1)}, u32[]{:S(2)}, u32[]{:S(2)}) collective-permute-start(bf16[96,768]{1,0:T(8,128)(2,1)} %get-tuple-element.71), channel_id=1, source_target_pairs={{0,4},{4,0},{8,12},{12,8},{16,20},{20,16},{24,28},{28,24},{1,5},{5... | collective-permute-start | bytes 442376 | tf_op jit(solution)/shard_map/ppermute | solution.py:26
  442.8 56.2 %collective-permute-start.118 = (bf16[96,768]{1,0:T(8,128)(2,1)}, bf16[96,768]{1,0:T(8,128)(2,1)}, u32[]{:S(2)}, u32[]{:S(2)}) collective-permute-start(bf16[96,768]{1,0:T(8,128)(2,1)} %get-tuple-element.75), channel_id=1, source_target_pairs={{0,4},{4,0},{8,12},{12,8},{16,20},{20,16},{24,28},{28,24},{1,5},{5... | collective-permute-start | bytes 442376 | tf_op jit(solution)/shard_map/ppermute | solution.py:26
  561.6 28.6 %collective-permute-start.147 = (bf16[384,768]{1,0:T(8,128)(2,1)S(1)}, bf16[384,768]{1,0:T(8,128)(2,1)S(1)}, u32[]{:S(2)}, u32[]{:S(2)}) collective-permute-start(bf16[384,768]{1,0:T(8,128)(2,1)S(1)} %copy-done.51), channel_id=1, source_target_pairs={{0,4},{4,0},{8,12},{12,8},{16,20},{20,16},{24,28},{28,24},{1,5},{5... | collective-permute-start | bytes 1769480 | tf_op jit(solution)/shard_map/ppermute | solution.py:26
  (261 other events, 3605.3 us)

commit v2 on v1

v2 whole, which is shorter than its diff:
```python
import functools

import jax
import jax.numpy as jnp
from jax import lax
from jax.experimental import pallas as pl
from jax.experimental.pallas import tpu as pltpu
from jax.sharding import PartitionSpec as P

HEADS = 12
HEAD = 64
PAIR = 2 * HEAD
CORE = 1
CLIP = 128
WINDOW = 256
TILE = 256
VMEM_BYTES = 56 * 1024 * 1024
f32 = jnp.float32
bf16 = jnp.bfloat16
fence = lax.optimization_barrier


def swap(values, mask):
    count = lax.axis_size("dp")
    return lax.ppermute(values, "dp", [(i, i ^ mask) for i in range(count)])


def shift(values, step):
    count = lax.axis_size("fsdp")
    return lax.ppermute(values, "fsdp", [(i, (i + step) % count) for i in range(count)])


def link_masks():
    masks = []
    mask = 2
    while mask < lax.axis_size("dp"):
        masks.append(mask)
        mask *= 2
    return masks


def relays():
    found = []
    for e in range(2, lax.axis_size("dp"), 2):
        if e & (e - 1):
            found.append((bin(e).count("1"), e, 1 << (e.bit_length() - 1), e & -e))
    return [item[1:] for item in sorted(found)]


def inner_order(came):
    count = len(came)
    me = lax.axis_index("fsdp")
    line = [came[count - 1 - k] for k in range(count)] + [came[count - k] for k in range(1, count)]
    return lax.dynamic_slice_in_dim(jnp.stack(line), count - 1 - me, count, 0)


def inner_start(shard):
    return [shard] + [shift(shard, step) for step in range(1, lax.axis_size("fsdp"))]


def single_steps(block):
    return {mask: swap(block, mask) for mask in link_masks()}


def relay_steps(held, cut):
    def half_of(e, which):
        block = held[e]
        if isinstance(block, tuple):
            return block[which]
        return block[:cut] if which == 0 else block[cut:]

    for e, top, low in relays():
        held[e] = (swap(half_of(e ^ top, 0), top), swap(half_of(e ^ low, 1), low))


def parts_of(pieces, total, cut):
    arrays, places = [], []
    for e in sorted(pieces):
        block = pieces[e]
        if isinstance(block, tuple):
            arrays += [block[0], block[1]]
            places += [(e, 0, cut), (e, cut, total - cut)]
        else:
            arrays.append(block)
            places.append((e, 0, total))
    return arrays, tuple(places)


def core_steps(held):
    out = dict(held)
    for e, block in held.items():
        if isinstance(block, tuple):
            out[e | CORE] = tuple(swap(half, CORE) for half in block)
        else:
            out[e | CORE] = swap(block, CORE)
    return out


def add_low(a, b):
    return (a.astype(f32) + b.astype(f32)).astype(bf16)


def outer_sum(total, cut):
    held = {2 * g: total[g] for g in range(total.shape[0])}
    extra = {e: {0: [], 1: []} for e in held}

    def half_sum(e, which):
        part = held[e][:cut] if which == 0 else held[e][cut:]
        for came in extra[e][which]:
            part = add_low(part, came)
        return part

    for e, top, low in relays()[::-1]:
        extra[e ^ top][0].append(swap(half_sum(e, 0), top))
        extra[e ^ low][1].append(swap(half_sum(e, 1), low))
    came = []
    for mask in link_masks():
        came.append(swap(jnp.concatenate([half_sum(mask, 0), half_sum(mask, 1)]), mask))
    result = held[0].astype(f32)
    for block in came:
        result = result + block.astype(f32)
    return result


def inner_sum(parts):
    count = parts.shape[0]
    me = lax.axis_index("fsdp")
    low = parts.astype(bf16)
    total = lax.dynamic_index_in_dim(parts, me, 0, keepdims=False)
    for step in range(1, count):
        going = lax.dynamic_index_in_dim(low, (me + step) % count, 0, keepdims=False)
        total = total + shift(going, step).astype(f32)
    return total


def nn(a, b):
    return jnp.dot(a, b, preferred_element_type=f32)


def nt(a, b):
    return lax.dot_general(a, b, (((1,), (1,)), ((), ())), preferred_element_type=f32)


def tn(a, b):
    return lax.dot_general(a, b, (((0,), (0,)), ((), ())), preferred_element_type=f32)


def tiles(size):
    step = TILE if size % TILE == 0 else size
    return [(at, step) for at in range(0, size, step)]


def centred(values):
    centre = jnp.mean(values, axis=-1, keepdims=True)
    shifted = values - centre
    spread = jnp.mean(shifted * shifted, axis=-1, keepdims=True)
    r = lax.rsqrt(spread + 1e-06)
    return shifted * r, r


def norm_back(xhat, r, gain, grad):
    c = grad * gain
    first = jnp.mean(c, axis=-1, keepdims=True)
    second = jnp.mean(c * xhat, axis=-1, keepdims=True)
    return r * (c - first - xhat * second), jnp.sum(grad * xhat, axis=0, keepdims=True)


def lower_half(rows):
    return lax.broadcasted_iota(jnp.int32, (rows, PAIR), 1) < HEAD


def two_heads(rows):
    keep = lower_half(rows.shape[0])
    zero = jnp.zeros_like(rows)
    return jnp.concatenate([jnp.where(keep, rows, zero), jnp.where(keep, zero, rows)], axis=0)


def side_by_side(stacked):
    rows = stacked.shape[0] // 2
    return jnp.where(lower_half(rows), stacked[:rows], stacked[rows:])


def softmax_rows(scores):
    raised = jnp.exp(scores - jnp.max(scores, axis=-1, keepdims=True))
    return raised / jnp.sum(raised, axis=-1, keepdims=True)


def bias_of(key_seg, own_seg):
    return jnp.where(key_seg == own_seg, 0.0, -1e30).astype(f32)


def copies(jobs, sems, at):
    made = [pltpu.make_async_copy(src, dst, sems.at[at + i]) for i, (src, dst) in enumerate(jobs)]
    for job in made:
        job.start()
    return made


def whole(shape, dtype):
    return jax.ShapeDtypeStruct(shape, dtype)


VMEM = pl.BlockSpec(memory_space=pltpu.VMEM)
SMEM = pl.BlockSpec(memory_space=pltpu.SMEM)
ANY = pl.BlockSpec(memory_space=pl.ANY)


def params():
    return pltpu.CompilerParams(vmem_limit_bytes=VMEM_BYTES)


def cost(flops, moved, exps=0):
    return pl.CostEstimate(flops=int(flops), bytes_accessed=int(moved), transcendentals=int(exps))


def first_kernel(
    geometry, ints, mix, seg_row, tokens, *refs
):
    dp_count, blocks, token_places, qkv_places, qkv_rows = geometry
    n_tok, n_qkv = len(token_places), len(qkv_places)
    token_refs, qkv_refs = refs[:n_tok], refs[n_tok : n_tok + n_qkv]
    blended_ref, qkv_ref, attended_ref, gains_ref, partner, weight, gain_parts, sems = refs[n_tok + n_qkv :]
    me = ints[0]
    width = tokens.shape[1]

    for b in range(blocks):
        rel, slot = ints[1 + b], ints[1 + blocks + b]
        for ref, (e, start, rows) in zip(token_refs, token_places):
            inside = (rel == e) & (slot * CLIP >= start) & (slot * CLIP < start + rows)

            @pl.when(inside)
            def _(ref=ref, start=start, rows=rows, b=b, slot=slot):
                at = pl.multiple_of(jnp.clip(slot * CLIP - start, 0, rows - CLIP), CLIP)
                pltpu.make_async_copy(ref.at[pl.ds(at, CLIP)], partner.at[b], sems.at[b]).start()

    jobs = []
    for ref, (e, start, rows) in zip(qkv_refs, qkv_places):
        take = min(rows, qkv_rows - start)
        at = pl.multiple_of((me ^ e) * qkv_rows + start, 16)
        jobs.append((ref.at[pl.ds(0, take)], weight.at[pl.ds(at, take)]))
        if start + rows > qkv_rows:
            jobs.append((ref.at[pl.ds(take, rows - take)], gain_parts.at[e]))
    made = copies(jobs, sems, blocks)
    for b in range(blocks):
        pltpu.make_async_copy(tokens.at[pl.ds(0, CLIP)], partner.at[b], sems.at[b]).wait()
    for b in range(blocks):
        rows = slice(b * CLIP, (b + 1) * CLIP)
        share = mix[b]
        blended_ref[rows, :] = share * tokens[rows, :].astype(f32) + (1.0 - share) * partner[b].astype(f32)
    for job in made:
        job.wait()
    gains = gain_parts[0].astype(f32)
    for e in range(1, dp_count):
        gains = gains + gain_parts[e].astype(f32)
    gains_ref[...] = gains[:8]
    xhat, _ = centred(blended_ref[...])
    normed = (xhat * gains[0:1]).astype(bf16)
    for at, step in tiles(3 * width):
        tile = nt(normed, weight[at : at + step, :])
        if at + step <= width:
            tile = tile * 0.125
        qkv_ref[:, at : at + step] = tile.astype(bf16)

    @pl.loop(0, blocks)
    def _(i):
        window = pl.multiple_of(ints[1 + 2 * blocks + i] * CLIP, CLIP)
        bias = bias_of(seg_row[:, pl.ds(window, WINDOW)], ints[1 + 3 * blocks + i])
        rows = pl.ds(pl.multiple_of(i * CLIP, CLIP), CLIP)
        keys = pl.ds(window, WINDOW)
        for at in range(0, width, PAIR):
            queries = two_heads(qkv_ref[rows, at : at + PAIR])
            probs = softmax_rows(nt(queries, qkv_ref[keys, width + at : width + at + PAIR]) + bias).astype(bf16)
            out = nn(probs, qkv_ref[keys, 2 * width + at : 2 * width + at + PAIR])
            attended_ref[rows, at : at + PAIR] = side_by_side(out).astype(bf16)


def load_cross(me, refs, places, layout, weights, sems):
    jobs = []
    for ref, (e, start, rows) in zip(refs, places):
        for (first, size), weight in zip(layout, weights):
            if first >= start and first + size <= start + rows:
                at = pl.multiple_of((me ^ e) * size, 16)
                jobs.append((ref.at[pl.ds(first - start, size)], weight.at[pl.ds(at, size)]))
    return copies(jobs, sems, 0)


def second_kernel(geometry, ints, coarse_seg, coarse, blended, attended, gains, *refs):
    blocks, places, layout = geometry
    weight_refs = refs[: len(places)]
    residual_ref, cq_ref, ckv_ref, crossed_ref, joined_ref, second_ref = refs[len(places) : len(places) + 6]
    w_ckv, w_out, w_cq, w_cout, sems = refs[len(places) + 6 :]
    made = load_cross(ints[0], weight_refs, places, layout, (w_ckv, w_out, w_cq, w_cout), sems)
    for job in made:
        job.wait()
    width = blended.shape[1]
    for at, step in tiles(2 * width):
        ckv_ref[:, at : at + step] = nt(coarse[...], w_ckv[at : at + step, :]).astype(bf16)
    for at, step in tiles(width):
        residual_ref[:, at : at + step] = blended[:, at : at + step] + nn(attended[...], w_out[:, at : at + step])
    xhat, _ = centred(residual_ref[...])
    crossed_in = (xhat * gains[1:2]).astype(bf16)
    for at, step in tiles(width):
        cq_ref[:, at : at + step] = (nn(crossed_in, w_cq[:, at : at + step]) * 0.125).astype(bf16)

    @pl.loop(0, blocks)
    def _(i):
        bias = bias_of(coarse_seg[...], ints[1 + 3 * blocks + i])
        rows = pl.ds(pl.multiple_of(i * CLIP, CLIP), CLIP)
        for at in range(0, width, PAIR):
            queries = two_heads(cq_ref[rows, at : at + PAIR])
            probs = softmax_rows(nt(queries, ckv_ref[:, at : at + PAIR]) + bias).astype(bf16)
            out = nn(probs, ckv_ref[:, width + at : width + at + PAIR])
            crossed_ref[rows, at : at + PAIR] = side_by_side(out).astype(bf16)

    for at, step in tiles(width):
        joined_ref[:, at : at + step] = residual_ref[:, at : at + step] + nn(crossed_ref[...], w_cout[:, at : at + step])
    xhat, _ = centred(joined_ref[...])
    second_ref[...] = (xhat * gains[2:3]).astype(bf16)


def mlp_kernel(geometry, second, cotangent, *refs):
    groups, places, rows, carried = geometry
    weight_refs = refs[: len(places)]
    refs = refs[len(places) :]
    if carried:
        out_in, grad_in = refs[:2]
        refs = refs[2:]
    keep_ref, send_ref, out_ref, grad_ref, w_up, w_down, hidden, grad_pre, sems = refs
    step = pl.program_id(0)

    def jobs_of(group):
        jobs = []
        for ref, (e, which, start) in zip(weight_refs, places):
            if e // 2 == groups[group]:
                for part, weight in ((0, w_up), (1, w_down)):
                    if which is None or which == part:
                        first = part * rows if which is None else 0
                        dst = weight.at[group, pl.ds((e & 1) * rows, rows)]
                        jobs.append((ref.at[pl.ds(first, rows)], dst))
        return jobs

    at = 0
    for group in range(len(groups)):
        jobs = jobs_of(group)
        made = [pltpu.make_async_copy(s, d, sems.at[at + i]) for i, (s, d) in enumerate(jobs)]
        at += len(jobs)

        @pl.when(step == 0)
        def _(made=made):
            for job in made:
                job.start()

        @pl.when(step == group)
        def _(made=made):
            for job in made:
                job.wait()

    @pl.when(step == 0)
    def _():
        if carried:
            out_ref[...] = out_in[...]
            grad_ref[...] = grad_in[...]
        else:
            out_ref[...] = jnp.zeros_like(out_ref)
            grad_ref[...] = jnp.zeros_like(grad_ref)

    up, down = w_up.at[step], w_down.at[step]
    both = 2 * rows
    for first, size in tiles(both):
        pre = nt(second[...], up[first : first + size, :])
        grad_hidden = nt(cotangent[...], down[first : first + size, :])
        cdf = 0.5 * (1.0 + lax.erf(pre * 0.7071067811865476))
        slope = cdf + pre * (jnp.exp(-0.5 * pre * pre) * 0.3989422804014327)
        hidden[:, first : first + size] = (pre * cdf).astype(bf16)
        grad_pre[:, first : first + size] = (grad_hidden * slope).astype(bf16)
    for first, target in ((0, keep_ref), (rows, send_ref)):
        target[0, 0] = tn(grad_pre[:, first : first + rows], second[...]).astype(bf16)
        target[0, 1] = tn(hidden[:, first : first + rows], cotangent[...]).astype(bf16)
    for first, size in tiles(second.shape[1]):
        out_ref[:, first : first + size] += nn(hidden[...], down[:, first : first + size])
        grad_ref[:, first : first + size] += nn(grad_pre[...], up[:, first : first + size])


def grads_out(me, dp_count, layout, sources, keep_ref, send_ref, sems, at):
    jobs = []
    for e in range(dp_count):
        target = send_ref if e & CORE else keep_ref
        for (first, size), source in zip(layout, sources):
            row = pl.multiple_of((me ^ e) * size, 16)
            jobs.append((source.at[pl.ds(row, size)], target.at[e // 2, pl.ds(first, size)]))
    return copies(jobs, sems, at)


def third_kernel(
    geometry, ints, coarse_seg, coarse, gains, mlp_out, grad_second, joined, cotangent, residual, attended, crossed, cq, ckv, *refs
):
    blocks, places, layout, dp_count = geometry
    weight_refs = refs[: len(places)]
    refs = refs[len(places) :]
    output_ref, coarse_ref, grad_res_ref, grad_att_ref, gain_grads_ref, keep_ref, send_ref = refs[:7]
    w_ckv, w_out, w_cq, w_cout, g_ckv, g_out, g_cq, g_cout, crossed_in, grad_cross, grad_cq, key_sum, value_sum, grad_joined, sems = refs[7:]
    me = ints[0]
    width = joined.shape[1]
    made = load_cross(me, weight_refs, places, layout, (w_ckv, w_out, w_cq, w_cout), sems)
    output_ref[...] = (joined[...] + mlp_out[...]).astype(bf16)
    xhat, r = centred(joined[...])
    grad_in, gain_two = norm_back(xhat, r, gains[2:3], grad_second[...])
    grad_joined[...] = cotangent[...].astype(f32) + grad_in
    low = grad_joined[...].astype(bf16)
    for job in made:
        job.wait()
    for at, step in tiles(width):
        grad_cross[:, at : at + step] = nt(low, w_cout[at : at + step, :]).astype(bf16)
    for at, step in tiles(width):
        g_cout[at : at + step, :] = tn(crossed[:, at : at + step], low).astype(bf16)
    key_sum[...] = jnp.zeros_like(key_sum)
    value_sum[...] = jnp.zeros_like(value_sum)

    @pl.loop(0, blocks)
    def _(i):
        bias = bias_of(coarse_seg[...], ints[1 + 3 * blocks + i])
        rows = pl.ds(pl.multiple_of(i * CLIP, CLIP), CLIP)
        for at in range(0, width, PAIR):
            lanes = slice(at, at + PAIR)
            queries = two_heads(cq[rows, lanes])
            grads = two_heads(grad_cross[rows, lanes])
            keys = ckv[:, lanes]
            values = ckv[:, width + at : width + at + PAIR]
            probs = softmax_rows(nt(queries, keys) + bias)
            value_sum[:, lanes] += tn(probs.astype(bf16), grads)
            grad_probs = nt(grads, values)
            inner = jnp.sum(probs * grad_probs, axis=-1, keepdims=True)
            scores = (probs * (grad_probs - inner)).astype(bf16)
            part = side_by_side(nn(scores, keys)).astype(bf16)
            grad_cq[rows, lanes] = part * jnp.asarray(0.125, bf16)
            key_sum[:, lanes] += tn(scores, queries)

    xhat, r = centred(residual[...])
    crossed_in[...] = (xhat * gains[1:2]).astype(bf16)
    for at, step in tiles(width):
        g_cq[at : at + step, :] = tn(crossed_in[:, at : at + step], grad_cq[...]).astype(bf16)
    dk, dv = key_sum[...].astype(bf16), value_sum[...].astype(bf16)
    for at, step in tiles(width):
        g_ckv[at : at + step, :] = tn(dk[:, at : at + step], coarse[...]).astype(bf16)
        g_ckv[width + at : width + at + step, :] = tn(dv[:, at : at + step], coarse[...]).astype(bf16)
        coarse_ref[:, at : at + step] = nn(dk, w_ckv[0:width, at : at + step]) + nn(dv, w_ckv[width : 2 * width, at : at + step])
    pieces = [nt(grad_cq[...], w_cq[at : at + step, :]) for at, step in tiles(width)]
    grad_in, gain_cross = norm_back(xhat, r, gains[1:2], jnp.concatenate(pieces, axis=1))
    grad_res = grad_joined[...] + grad_in
    grad_res_ref[...] = grad_res
    low = grad_res.astype(bf16)
    for at, step in tiles(width):
        g_out[at : at + step, :] = tn(attended[:, at : at + step], low).astype(bf16)
    going = grads_out(me, dp_count, layout, (g_ckv, g_out, g_cq, g_cout), keep_ref, send_ref, sems, sems.shape[0] - 4 * dp_count)
    for at, step in tiles(width):
        grad_att_ref[:, at : at + step] = nt(low, w_out[at : at + step, :]).astype(bf16)
    zero = jnp.zeros_like(gain_two)
    gain_grads_ref[...] = jnp.concatenate([zero, gain_cross, gain_two] + [zero] * 5, axis=0)
    for job in going:
        job.wait()


def fourth_kernel(geometry, ints, mix, seg_row, gains, gain_grads, blended, grad_res, grad_att, qkv, *refs):
    dp_count, blocks, qkv_places, qkv_rows = geometry
    weight_refs = refs[: len(qkv_places)]
    refs = refs[len(qkv_places) :]
    base_ref, keep_ref, send_ref, mix_keep_ref, mix_send_ref = refs[:5]
    weight, grad_w, grad_proj, key_sum, value_sum, going_back, gain_rows, sems = refs[5:]
    me = ints[0]
    width = blended.shape[1]
    jobs = []
    for ref, (e, start, rows) in zip(weight_refs, qkv_places):
        take = min(rows, qkv_rows - start)
        at = pl.multiple_of((me ^ e) * qkv_rows + start, 16)
        jobs.append((ref.at[pl.ds(0, take)], weight.at[pl.ds(at, take)]))
    made = copies(jobs, sems, 0)
    going_back[...] = jnp.zeros_like(going_back)
    key_sum[...] = jnp.zeros_like(key_sum)
    value_sum[...] = jnp.zeros_like(value_sum)

    @pl.loop(0, blocks)
    def _(i):
        window = pl.multiple_of(ints[1 + 2 * blocks + i] * CLIP, CLIP)
        bias = bias_of(seg_row[:, pl.ds(window, WINDOW)], ints[1 + 3 * blocks + i])
        rows = pl.ds(pl.multiple_of(i * CLIP, CLIP), CLIP)
        near = pl.ds(window, WINDOW)
        for at in range(0, width, PAIR):
            lanes = slice(at, at + PAIR)
            queries = two_heads(qkv[rows, lanes])
            grads = two_heads(grad_att[rows, lanes])
            keys = qkv[near, width + at : width + at + PAIR]
            values = qkv[near, 2 * width + at : 2 * width + at + PAIR]
            probs = softmax_rows(nt(queries, keys) + bias)
            value_sum[near, lanes] += tn(probs.astype(bf16), grads)
            grad_probs = nt(grads, values)
            inner = jnp.sum(probs * grad_probs, axis=-1, keepdims=True)
            scores = (probs * (grad_probs - inner)).astype(bf16)
            part = side_by_side(nn(scores, keys)).astype(bf16)
            grad_proj[rows, lanes] = part * jnp.asarray(0.125, bf16)
            key_sum[near, lanes] += tn(scores, queries)

    grad_proj[:, width : 2 * width] = key_sum[...].astype(bf16)
    grad_proj[:, 2 * width : 3 * width] = value_sum[...].astype(bf16)
    xhat, r = centred(blended[...])
    normed = (xhat * gains[0:1]).astype(bf16)
    for at, step in tiles(3 * width):
        grad_w[at : at + step, :] = tn(grad_proj[:, at : at + step], normed).astype(bf16)
    sent = grads_out(me, dp_count, ((0, qkv_rows),), (grad_w,), keep_ref, send_ref, sems, len(jobs))
    for job in made:
        job.wait()
    pieces = [nn(grad_proj[...], weight[:, at : at + step]) for at, step in tiles(width)]
    grad_in, gain_one = norm_back(xhat, r, gains[0:1], jnp.concatenate(pieces, axis=1))
    all_gains = jnp.concatenate([gain_one, gain_grads[1:8], jnp.zeros((8, width), f32)], axis=0)
    gain_rows[...] = all_gains.astype(bf16)
    at = len(jobs) + dp_count
    last = []
    for e in range(dp_count):
        target = send_ref if e & CORE else keep_ref
        last.append((gain_rows, target.at[e // 2, pl.ds(qkv_rows, 16)]))
    sent += copies(last, sems, at)
    at += dp_count
    grad_blend = grad_res[...] + grad_in
    for b in range(blocks):
        rows = slice(b * CLIP, (b + 1) * CLIP)
        share = mix[b]
        part = grad_blend[rows, :]
        base_ref[rows, :] = share * part
        place = ints[1 + b] * blocks + ints[1 + blocks + b]
        going_back[place] = (going_back[place].astype(f32) + (1.0 - share) * part).astype(bf16)
    mixed = []
    for e in range(dp_count):
        target = mix_send_ref if e & CORE else mix_keep_ref
        for s in range(blocks):
            mixed.append((going_back.at[e * blocks + s], target.at[e // 2, pl.ds(s * CLIP, CLIP)]))
    sent += copies(mixed, sems, at)
    for job in sent:
        job.wait()


def shards(
    tokens,
    coarse_view,
    segment_ids,
    partner_device,
    partner_slot,
    mix_weight,
    ln1_gain,
    w_qkv,
    w_out,
    lnx_gain,
    w_cq,
    w_ckv,
    w_cout,
    ln2_gain,
    w_up,
    w_down,
    cotangent,
):
    row_count, width = tokens.shape
    coarse_rows = coarse_view.shape[0]
    blocks = mix_weight.shape[0]
    dp_count, fsdp_count = lax.axis_size("dp"), lax.axis_size("fsdp")
    dp_me, fsdp_me = lax.axis_index("dp"), lax.axis_index("fsdp")
    part = ln1_gain.shape[0]
    device_me = dp_me * fsdp_count + fsdp_me
    pairs = dp_count // 2

    target = partner_device[:, 0]
    segments = segment_ids[0]
    videos = segments.reshape(blocks, row_count // blocks)[:, 0]
    following = jnp.concatenate([videos[1:] == videos[:-1], jnp.zeros((1,), bool)])
    before = jnp.concatenate([jnp.zeros((1,), bool), videos[1:] == videos[:-1]])
    index = jnp.arange(blocks, dtype=jnp.int32)
    window = jnp.where(following, index, jnp.where(before, index - 1, jnp.minimum(index, blocks - 2)))
    ints = jnp.concatenate(
        [dp_me[None].astype(jnp.int32), (target ^ dp_me).astype(jnp.int32), partner_slot, window, videos]
    )
    seg_row = segments[None, :]
    coarse_seg = segments.reshape(coarse_rows, row_count // coarse_rows)[:, 0][None, :]

    gain_rows = lax.dynamic_update_slice(
        jnp.zeros((8, width), bf16), jnp.stack([ln1_gain, lnx_gain, ln2_gain]), (0, device_me * part)
    )
    shard_one = jnp.concatenate([w_qkv.T, gain_rows])
    shard_two = jnp.concatenate([w_ckv.T, w_out, w_cq, w_cout])
    shard_mlp = jnp.concatenate([w_up.T, w_down])
    sizes_two = (w_ckv.shape[1], w_out.shape[0], w_cq.shape[0], w_cout.shape[0])
    qkv_part, up_part = w_qkv.shape[1], w_up.shape[1]
    qkv_rows, up_rows = qkv_part * fsdp_count, up_part * fsdp_count
    layout = []
    at = 0
    for size in sizes_two:
        layout.append((at * fsdp_count, size * fsdp_count))
        at += size
    layout = tuple(layout)
    rows_two = at * fsdp_count

    held_tok = {0: tokens, **single_steps(tokens)}
    held_tok_core = swap(tokens, CORE)
    came_attn = inner_start(jnp.concatenate([shard_one, shard_two]))
    held_tok, held_tok_core, came_attn = fence((held_tok, held_tok_core, came_attn))

    attn = inner_order(came_attn)
    one_rows = qkv_part + 8
    ones, twos = attn[:, :one_rows], attn[:, one_rows:]
    gain_block = jnp.sum(ones[:, qkv_part:].astype(f32), axis=0).astype(bf16)
    block_one = jnp.concatenate(
        [ones[:, :qkv_part].reshape(qkv_rows, width), gain_block, jnp.zeros((8, width), bf16)]
    )
    split = []
    at = 0
    for size in sizes_two:
        split.append(twos[:, at : at + size].reshape(size * fsdp_count, width))
        at += size
    block_two = jnp.concatenate(split)
    cut_tok, cut_one, cut_two, cut_mlp = row_count // 2, qkv_rows // 2, layout[0][1], up_rows

    relay_steps(held_tok, cut_tok)
    core_tok = core_steps({e: b for e, b in held_tok.items() if e and not isinstance(b, tuple)})
    held_one = {0: block_one, **single_steps(block_one)}
    held_tok, core_tok, held_one, shard_mlp, block_two = fence(
        (held_tok, core_tok, held_one, shard_mlp, block_two)
    )
    core_tok.update({1: held_tok_core})
    core_tok.update(core_steps({e: b for e, b in held_tok.items() if isinstance(b, tuple)}))
    pieces_tok = {**held_tok, **core_tok}

    came_mlp = inner_start(shard_mlp)
    relay_steps(held_one, cut_one)
    pieces_one = core_steps(held_one)
    pieces_tok, pieces_one, came_mlp, block_two = fence((pieces_tok, pieces_one, came_mlp, block_two))

    held_two = {0: block_two, **single_steps(block_two)}
    mlp = inner_order(came_mlp)
    block_mlp = jnp.concatenate(
        [mlp[:, :up_part].reshape(up_rows, width), mlp[:, up_part:].reshape(up_rows, width)]
    )
    arrays_tok, places_tok = parts_of(pieces_tok, row_count, cut_tok)
    arrays_one, places_one = parts_of(pieces_one, qkv_rows + 16, cut_one)
    blended, qkv, attended, gains = pl.pallas_call(
        functools.partial(first_kernel, (dp_count, blocks, places_tok, places_one, qkv_rows)),
        out_shape=(
            whole((row_count, width), f32),
            whole((row_count, 3 * width), bf16),
            whole((row_count, width), bf16),
            whole((8, width), f32),
        ),
        in_specs=[SMEM, SMEM, VMEM, VMEM] + [ANY] * (len(arrays_tok) + len(arrays_one)),
        out_specs=(VMEM,) * 4,
        scratch_shapes=[
            pltpu.VMEM((blocks, CLIP, width), bf16),
            pltpu.VMEM((3 * width, width), bf16),
            pltpu.VMEM((dp_count, 16, width), bf16),
            pltpu.SemaphoreType.DMA((blocks + len(arrays_one) + dp_count,)),
        ],
        compiler_params=params(),
        cost_estimate=cost(2e9 * 10, 12e6),
        name="mix_self_attention",
    )(ints, mix_weight, seg_row, tokens, *arrays_tok, *arrays_one)
    held_two, block_mlp = fence((held_two, block_mlp))

    relay_steps(held_two, cut_two)
    pieces_two = core_steps(held_two)
    held_mlp = {0: block_mlp, **single_steps(block_mlp)}
    arrays_two, places_two = parts_of(pieces_two, rows_two, cut_two)
    wide = [pltpu.VMEM((sizes * fsdp_count * dp_count, width), bf16) for sizes in sizes_two]
    n_two = 4 * dp_count
    residual, cq, ckv, crossed, joined, second = pl.pallas_call(
        functools.partial(second_kernel, (blocks, places_two, layout)),
        out_shape=(
            whole((row_count, width), f32),
            whole((row_count, width), bf16),
            whole((coarse_rows, 2 * width), bf16),
            whole((row_count, width), bf16),
            whole((row_count, width), f32),
            whole((row_count, width), bf16),
        ),
        in_specs=[SMEM] + [VMEM] * 5 + [ANY] * len(arrays_two),
        out_specs=(VMEM,) * 6,
        scratch_shapes=wide + [pltpu.SemaphoreType.DMA((n_two,))],
        compiler_params=params(),
        cost_estimate=cost(2e9 * 10, 12e6),
        name="cross_attention",
    )(ints, coarse_seg, coarse_view, blended, attended, gains, *arrays_two)
    held_mlp = fence(held_mlp)

    singles = dict(held_mlp)
    pieces_mlp = core_steps(singles)
    relay_steps(held_mlp, cut_mlp)
    late = core_steps({e: b for e, b in held_mlp.items() if isinstance(b, tuple)})

    def mlp_call(pieces, carried):
        groups = tuple(sorted({e // 2 for e in pieces}))
        arrays, places = [], []
        for e in sorted(pieces):
            block = pieces[e]
            if isinstance(block, tuple):
                arrays += list(block)
                places += [(e, 0, 0), (e, 1, 0)]
            else:
                arrays.append(block)
                places.append((e, None, 0))
        count = len(groups)
        fixed = pl.BlockSpec((row_count, width), lambda g: (0, 0))
        moving = pl.BlockSpec((1, 2, up_rows, width), lambda g: (g, 0, 0, 0))
        keep, send, out, grad = pl.pallas_call(
            functools.partial(mlp_kernel, (groups, tuple(places), up_rows, bool(carried))),
            grid=(count,),
            out_shape=(
                whole((count, 2, up_rows, width), bf16),
                whole((count, 2, up_rows, width), bf16),
                whole((row_count, width), f32),
                whole((row_count, width), f32),
            ),
            in_specs=[fixed, fixed] + [ANY] * len(arrays) + [fixed] * len(carried),
            out_specs=(moving, moving, fixed, fixed),
            scratch_shapes=[
                pltpu.VMEM((count, 2 * up_rows, width), bf16),
                pltpu.VMEM((count, 2 * up_rows, width), bf16),
                pltpu.VMEM((row_count, 2 * up_rows), bf16),
                pltpu.VMEM((row_count, 2 * up_rows), bf16),
                pltpu.SemaphoreType.DMA((4 * count,)),
            ],
            compiler_params=params(),
            cost_estimate=cost(7.2e9 * count, 8e6 * count),
            name="feed_forward",
        )(second, cotangent, *arrays, *carried)
        flat = (count, 2 * up_rows, width)
        return groups, keep.reshape(flat), send.reshape(flat), out, grad

    groups_a, keep_a, send_a, out_a, grad_a = mlp_call(pieces_mlp, ())
    groups_b, keep_b, send_b, mlp_out, grad_second = mlp_call(late, (out_a, grad_a))

    total_b = add_low(keep_b, swap(send_b, CORE))
    total_a = add_low(keep_a, swap(send_a, CORE))
    where = {g: total_a[i] for i, g in enumerate(groups_a)}
    where.update({g: total_b[i] for i, g in enumerate(groups_b)})

    output, coarse_grad, grad_res, grad_att, gain_grads, keep_two, send_two = pl.pallas_call(
        functools.partial(third_kernel, (blocks, places_two, layout, dp_count)),
        out_shape=(
            whole((row_count, width), bf16),
            whole((coarse_rows, width), f32),
            whole((row_count, width), f32),
            whole((row_count, width), bf16),
            whole((8, width), f32),
            whole((pairs, rows_two, width), bf16),
            whole((pairs, rows_two, width), bf16),
        ),
        in_specs=[SMEM] + [VMEM] * 12 + [ANY] * len(arrays_two),
        out_specs=(VMEM,) * 5 + (ANY,) * 2,
        scratch_shapes=wide
        + wide
        + [
            pltpu.VMEM((row_count, width), bf16),
            pltpu.VMEM((row_count, width), bf16),
            pltpu.VMEM((row_count, width), bf16),
            pltpu.VMEM((coarse_rows, width), f32),
            pltpu.VMEM((coarse_rows, width), f32),
            pltpu.VMEM((row_count, width), f32),
            pltpu.SemaphoreType.DMA((n_two + 4 * dp_count,)),
        ],
        compiler_params=params(),
        cost_estimate=cost(2e9 * 12, 30e6),
        name="cross_attention_backward",
    )(
        ints, coarse_seg, coarse_view, gains, mlp_out, grad_second, joined, cotangent, residual, attended, crossed, cq, ckv,
        *arrays_two,
    )

    base, keep_one, send_one, keep_tok, send_tok = pl.pallas_call(
        functools.partial(fourth_kernel, (dp_count, blocks, places_one, qkv_rows)),
        out_shape=(
            whole((row_count, width), f32),
            whole((pairs, qkv_rows + 16, width), bf16),
            whole((pairs, qkv_rows + 16, width), bf16),
            whole((pairs, row_count, width), bf16),
            whole((pairs, row_count, width), bf16),
        ),
        in_specs=[SMEM, SMEM] + [VMEM] * 7 + [ANY] * len(arrays_one),
        out_specs=(VMEM,) + (ANY,) * 4,
        scratch_shapes=[
            pltpu.VMEM((3 * width, width), bf16),
            pltpu.VMEM((3 * width, width), bf16),
            pltpu.VMEM((row_count, 3 * width), bf16),
            pltpu.VMEM((row_count, width), f32),
            pltpu.VMEM((row_count, width), f32),
            pltpu.VMEM((dp_count * blocks, CLIP, width), bf16),
            pltpu.VMEM((16, width), bf16),
            pltpu.SemaphoreType.DMA((len(arrays_one) + 2 * dp_count + dp_count * blocks,)),
        ],
        compiler_params=params(),
        cost_estimate=cost(2e9 * 12, 30e6),
        name="self_attention_backward",
    )(ints, mix_weight, seg_row, gains, gain_grads, blended, grad_res, grad_att, qkv, *arrays_one)

    mlp_sum = outer_sum(jnp.stack([where[g] for g in range(pairs)]), cut_mlp)
    mlp_parts = jnp.concatenate(
        [mlp_sum[:up_rows].reshape(fsdp_count, up_part, width), mlp_sum[up_rows:].reshape(fsdp_count, up_part, width)], axis=1
    )
    mlp_mine = inner_sum(mlp_parts)
    up_shard, down_shard = mlp_mine[:up_part].T, mlp_mine[up_part:]

    two_sum = outer_sum(add_low(keep_two, swap(send_two, CORE)), cut_two)
    two_parts = jnp.concatenate(
        [two_sum[first : first + size].reshape(fsdp_count, size // fsdp_count, width) for first, size in layout], axis=1
    )
    two_mine = inner_sum(two_parts)
    found = []
    at = 0
    for size in sizes_two:
        found.append(two_mine[at : at + size])
        at += size
    ckv_shard, out_shard, cq_shard, cout_shard = found[0].T, found[1], found[2], found[3]

    one_sum = outer_sum(add_low(keep_one, swap(send_one, CORE)), cut_one)
    gain_sum = jnp.broadcast_to(one_sum[qkv_rows : qkv_rows + 8][None], (fsdp_count, 8, width))
    one_parts = jnp.concatenate([one_sum[:qkv_rows].reshape(fsdp_count, qkv_part, width), gain_sum], axis=1)
    one_mine = inner_sum(one_parts)
    qkv_shard = one_mine[:qkv_part].T
    gain_mine = lax.dynamic_slice(one_mine[qkv_part:], (0, device_me * part), (3, part))

    token_grad = base + outer_sum(add_low(keep_tok, swap(send_tok, CORE)), cut_tok)
    return (
        output,
        token_grad,
        coarse_grad,
        gain_mine[0],
        qkv_shard,
        out_shard,
        gain_mine[1],
        cq_shard,
        ckv_shard,
        cout_shard,
        gain_mine[2],
        up_shard,
        down_shard,
    )


def solution(mesh):
    rows = P(("dp", "fsdp"), None)
    columns = P(None, ("dp", "fsdp"))
    line = P(("dp", "fsdp"))
    in_specs = (
        rows, rows, rows, rows, line, line, line, columns, rows,
        line, rows, columns, rows, line, columns, rows, rows,
    )
    out_specs = (
        rows, rows, rows, line, columns, rows, line, rows, columns, rows, line, columns, rows,
    )
    return jax.shard_map(shards, mesh=mesh, in_specs=in_specs, out_specs=out_specs, check_vma=False)
```

time: 682 us -> 425 us (0.62)
  the two profiles are of different devices: /device:TPU:0 before, /device:TPU:28 now
where the time goes in v2:
time: 425 us; the launch traced here: 419 us
  waiting for transfers between devices  196 us (46%)
  Pallas kernels  111 us (26%)
  starting transfers between devices  64.3 us (15%)
  local copies, waits for them, and re-layouts  27.8 us (7%)
  other arithmetic  17.5 us (4%)
    ppermute x57, waiting for transfers between devices, swap(): return lax.ppermute(values, 'dp', [(i, i ^ mask) for i in range(count)])  130 us
    ppermute x15, waiting for transfers between devices, shift(): lax.ppermute(values, 'fsdp', [(i, (i + step) % count) for i in range(coun...  65.9 us
    ppermute x57, starting transfers between devices, swap(): return lax.ppermute(values, 'dp', [(i, i ^ mask) for i in range(count)])  34.3 us
    ppermute x15, starting transfers between devices, shift(): lax.ppermute(values, 'fsdp', [(i, (i + step) % count) for i in range(coun...  30 us
    pallas_call x1, Pallas kernels, shards(): pl.pallas_call(functools.partial(third_kernel, (blocks, places_two, layou...  29.7 us
    pallas_call x1, Pallas kernels, shards(): pl.pallas_call(functools.partial(fourth_kernel, (dp_count, blocks, places...  28.1 us
    pallas_call x2, Pallas kernels, mlp_call(): pl.pallas_call(functools.partial(mlp_kernel, (groups, tuple(places), up_r...  27.2 us
    pallas_call x1, Pallas kernels, shards(): pl.pallas_call(functools.partial(second_kernel, (blocks, places_two, layo...  13.9 us
  transfers between devices with their start and end apart: 72, of which 30 were waited for; matrix products, arithmetic and copies ran while one was open for 9% of the time, Pallas kernels for 10%

profile of v2, /device:TPU:28, one launch (start us, length us, event | category | flops | bytes accessed | tf_op | source)
XLA Modules:
  0.0 418.6 jit_solution(3430035642615919304)
XLA Ops:
  9.9 7.9 %collective-permute-done.3 = bf16[200,768]{1,0:T(8,128)(2,1)S(1)} collective-permute-done((bf16[200,768]{1,0:T(8,128)(2,1)S(1)}, bf16[200,768]{1,0:T(8,128)(2,1)S(1)}, u32[]{:S(2)}, u32[]{:S(2)}) %collective-permute-start.3) | collective-permute-done | bytes 307232 | tf_op jit(solution)/shard_map/ppermute | solution.py:30
  17.8 13.9 %collective-permute-start.5 = (bf16[200,768]{1,0:T(8,128)(2,1)S(1)}, bf16[200,768]{1,0:T(8,128)(2,1)S(1)}, u32[]{:S(2)}, u32[]{:S(2)}) collective-permute-start(bf16[200,768]{1,0:T(8,128)(2,1)S(1)} %constant_dynamic-update-slice_fusion), channel_id=1, source_target_pairs={{0,3},{1,0},{2,1},{3,2},{4,7},{5,4},{6,5},{7,6},{8,11},{9,8},{10,9... | collective-permute-start | bytes 921608 | tf_op jit(solution)/shard_map/ppermute | solution.py:30
  31.7 5.6 %collective-permute-done.4 = bf16[200,768]{1,0:T(8,128)(2,1)S(1)} collective-permute-done((bf16[200,768]{1,0:T(8,128)(2,1)S(1)}, bf16[200,768]{1,0:T(8,128)(2,1)S(1)}, u32[]{:S(2)}, u32[]{:S(2)}) %collective-permute-start.4) | collective-permute-done | bytes 307232 | tf_op jit(solution)/shard_map/ppermute | solution.py:30
  43.8 7.2 %collective-permute-done.6.refs_6_ = bf16[256,768]{1,0:T(8,128)(2,1)S(1)} collective-permute-done((bf16[256,768]{1,0:T(8,128)(2,1)S(1)}, bf16[256,768]{1,0:T(8,128)(2,1)S(1)}, u32[]{:S(2)}, u32[]{:S(2)}) %collective-permute-start.6) | collective-permute-done | bytes 393248 | tf_op jit(solution)/shard_map/ppermute | solution.py:25
  51.9 10.5 %collective-permute-done.7.refs_7_ = bf16[256,768]{1,0:T(8,128)(2,1)} collective-permute-done((bf16[256,768]{1,0:T(8,128)(2,1)}, bf16[256,768]{1,0:T(8,128)(2,1)}, u32[]{:S(2)}, u32[]{:S(2)}) %collective-permute-start.7) | collective-permute-done | bytes 393248 | tf_op jit(solution)/shard_map/ppermute | solution.py:25
  73.8 18.8 %collective-permute-done.22 = bf16[192,768]{1,0:T(8,128)(2,1)S(1)} collective-permute-done((bf16[192,768]{1,0:T(8,128)(2,1)S(1)}, bf16[192,768]{1,0:T(8,128)(2,1)S(1)}, u32[]{:S(2)}, u32[]{:S(2)}) %collective-permute-start.22) | collective-permute-done | bytes 294944 | tf_op jit(solution)/shard_map/ppermute | solution.py:30
  99.6 15.0 %collective-permute-done.24.refs_2_ = bf16[480,768]{1,0:T(8,128)(2,1)} collective-permute-done((bf16[480,768]{1,0:T(8,128)(2,1)S(1)}, bf16[480,768]{1,0:T(8,128)(2,1)}, u32[]{:S(2)}, u32[]{:S(2)}) %collective-permute-start.24) | collective-permute-done | bytes 737312 | tf_op jit(solution)/shard_map/ppermute | solution.py:25
  127.7 21.7 %collective-permute-done.29.refs_6_ = bf16[192,768]{1,0:T(8,128)(2,1)} collective-permute-done((bf16[192,768]{1,0:T(8,128)(2,1)}, bf16[192,768]{1,0:T(8,128)(2,1)}, u32[]{:S(2)}, u32[]{:S(2)}) %collective-permute-start.29) | collective-permute-done | bytes 294944 | tf_op jit(solution)/shard_map/ppermute | solution.py:25
  152.9 12.5 %mix_self_attention.1 = (f32[512,768]{1,0:T(8,128)}, bf16[512,2304]{1,0:T(8,128)(2,1)}, bf16[512,768]{1,0:T(8,128)(2,1)}, f32[8,768]{1,0:T(8,128)}) custom-call(s32[17]{0:T(128)} %concatenate.59.ints, f32[4]{0:T(128)} %mix.3, s32[1,512]{1,0:T(1,128)} %seg_row.3, bf16[512,768]{1,0:T(8,128)(2,1)} %refs_0_, bf16[512,768]{1,0:T(8,128)(2,1)} %refs_0_, ...), custom_call_target="tpu_custom_call" | custom-call | flops 20000000000 | bytes 12000000 | tf_op jit(solution)/shard_map/mix_self_attention/pallas_call | solution.py:640
  170.5 13.9 %cross_attention.1 = (f32[512,768]{1,0:T(8,128)}, bf16[512,768]{1,0:T(8,128)(2,1)}, bf16[128,1536]{1,0:T(8,128)(2,1)}, bf16[512,768]{1,0:T(8,128)(2,1)}, f32[512,768]{1,0:T(8,128)}, /*index=5*/bf16[512,768]{1,0:T(8,128)(2,1)}) custom-call(s32[17]{0:T(128)} %concatenate.59.ints, s32[1,128]{1,0:T(1,128)} %bitcast.230, bf16[128,768]{1,0:T(8,128)(2,1)} %coarse.3, ...), custom_call_target="tpu_custom_call" | custom-call | flops 20000000000 | bytes 12000000 | tf_op jit(solution)/shard_map/cross_attention/pallas_call | solution.py:668
  187.1 17.5 %feed_forward.2 = (bf16[3,2,384,768]{3,2,1,0:T(8,128)(2,1)}, bf16[3,2,384,768]{3,2,1,0:T(8,128)(2,1)}, f32[512,768]{1,0:T(8,128)}, f32[512,768]{1,0:T(8,128)}) custom-call(bf16[512,768]{1,0:T(8,128)(2,1)} %get-tuple-element.146.second, bf16[512,768]{1,0:T(8,128)(2,1)} %cotangent.5, bf16[768,768]{1,0:T(8,128)(2,1)} %copy-done.5, bf16[768,768]{1,0:T(8,128)(2,1)} %copy-done.15, ...), custom_call_target="tpu_custom_call" | custom-call | flops 21600000000 | bytes 24000000 | tf_op jit(solution)/shard_map/feed_forward/pallas_call | solution.py:706
  205.6 9.7 %feed_forward.3 = (bf16[1,2,384,768]{3,2,1,0:T(8,128)(2,1)}, bf16[1,2,384,768]{3,2,1,0:T(8,128)(2,1)}, f32[512,768]{1,0:T(8,128)}, f32[512,768]{1,0:T(8,128)}) custom-call(bf16[512,768]{1,0:T(8,128)(2,1)} %get-tuple-element.146.second, bf16[512,768]{1,0:T(8,128)(2,1)} %cotangent.5, bf16[384,768]{1,0:T(8,128)(2,1)} %collective-permute-done.35.refs_0_, ...), custom_call_target="tpu_custom_call" | custom-call | flops 7200000000 | bytes 8000000 | tf_op jit(solution)/shard_map/feed_forward/pallas_call | solution.py:706
  215.4 29.7 %cross_attention_backward.1 = (bf16[512,768]{1,0:T(8,128)(2,1)}, f32[128,768]{1,0:T(8,128)}, f32[512,768]{1,0:T(8,128)}, bf16[512,768]{1,0:T(8,128)(2,1)}, f32[8...) custom-call(s32[17]{0:T(128)} %concatenate.59.ints, s32[1,128]{1,0:T(1,128)} %bitcast.231, ...), custom_call_target="tpu_custom_call" | custom-call | flops 24000000000 | bytes 30000000 | tf_op jit(solution)/shard_map/cross_attention_backward/pallas_call | solution.py:739
  245.1 28.1 %self_attention_backward.1 = (f32[512,768]{1,0:T(8,128)}, bf16[4,304,768]{2,1,0:T(8,128)(2,1)}, bf16[4,304,768]{2,1,0:T(8,128)(2,1)}, bf16[4,512,768]{2,1,0:T(8,128)(2,1)}, bf16[4,512,768]{2,1,0:T(8,128)(2,1)}) custom-call(s32[17]{0:T(128)} %concatenate.59.ints, f32[4]{0:T(128)} %mix.3, s32[1,512]{1,0:T(1,128)} %seg_row.3, ...), custom_call_target="tpu_custom_call" | custom-call | flops 24000000000 | bytes 30000000 | tf_op jit(solution)/shard_map/self_attention_backward/pallas_call | solution.py:771
  281.0 6.3 %collective-permute-done.48 = bf16[144,768]{1,0:T(8,128)(2,1)S(1)} collective-permute-done((bf16[144,768]{1,0:T(8,128)(2,1)S(1)}, bf16[144,768]{1,0:T(8,128)(2,1)S(1)}, u32[]{:S(2)}, u32[]{:S(2)}) %collective-permute-start.48) | collective-permute-done | bytes 221216 | tf_op jit(solution)/shard_map/ppermute | solution.py:25
  290.6 9.2 %collective-permute-done.49 = bf16[304,768]{1,0:T(8,128)(2,1)} collective-permute-done((bf16[304,768]{1,0:T(8,128)(2,1)S(1)}, bf16[304,768]{1,0:T(8,128)(2,1)}, u32[]{:S(2)}, u32[]{:S(2)}) %collective-permute-start.49) | collective-permute-done | bytes 466976 | tf_op jit(solution)/shard_map/ppermute | solution.py:25
  308.5 4.9 %collective-permute-done.53 = bf16[80,768]{1,0:T(8,128)(2,1)S(1)} collective-permute-done((bf16[80,768]{1,0:T(8,128)(2,1)S(1)}, bf16[80,768]{1,0:T(8,128)(2,1)S(1)}, u32[]{:S(2)}, u32[]{:S(2)}) %collective-permute-start.53) | collective-permute-done | bytes 122912 | tf_op jit(solution)/shard_map/ppermute | solution.py:30
  326.2 8.1 %collective-permute-done.56 = bf16[192,768]{1,0:T(8,128)(2,1)S(1)} collective-permute-done((bf16[192,768]{1,0:T(8,128)(2,1)S(1)}, bf16[192,768]{1,0:T(8,128)(2,1)S(1)}, u32[]{:S(2)}, u32[]{:S(2)}) %collective-permute-start.56) | collective-permute-done | bytes 294944 | tf_op jit(solution)/shard_map/ppermute | solution.py:25
  346.4 3.6 collective-permute-done.45
  350.3 15.5 %collective-permute-done.57 = bf16[480,768]{1,0:T(8,128)(2,1)S(1)} collective-permute-done((bf16[480,768]{1,0:T(8,128)(2,1)S(1)}, bf16[480,768]{1,0:T(8,128)(2,1)S(1)}, u32[]{:S(2)}, u32[]{:S(2)}) %collective-permute-start.57) | collective-permute-done | bytes 737312 | tf_op jit(solution)/shard_map/ppermute | solution.py:25
  373.6 8.8 %collective-permute-done.61 = bf16[120,768]{1,0:T(8,128)(2,1)S(1)} collective-permute-done((bf16[120,768]{1,0:T(8,128)(2,1)S(1)}, bf16[120,768]{1,0:T(8,128)(2,1)S(1)}, u32[]{:S(2)}, u32[]{:S(2)}) %collective-permute-start.61) | collective-permute-done | bytes 184352 | tf_op jit(solution)/shard_map/ppermute | solution.py:30
  383.8 7.3 %collective-permute-done.66 = bf16[768,768]{1,0:T(8,128)(2,1)S(1)} collective-permute-done((bf16[768,768]{1,0:T(8,128)(2,1)S(1)}, bf16[768,768]{1,0:T(8,128)(2,1)S(1)}, u32[]{:S(2)}, u32[]{:S(2)}) %collective-permute-start.66) | collective-permute-done | bytes 1179680 | tf_op jit(solution)/shard_map/ppermute | solution.py:25
  396.9 6.9 %collective-permute-done.44 = bf16[512,768]{1,0:T(8,128)(2,1)S(1)} collective-permute-done((bf16[512,768]{1,0:T(8,128)(2,1)S(1)}, bf16[512,768]{1,0:T(8,128)(2,1)S(1)}, u32[]{:S(2)}, u32[]{:S(2)}) %collective-permute-start.44) | collective-permute-done | bytes 786464 | tf_op jit(solution)/shard_map/ppermute | solution.py:25
  405.3 12.0 %collective-permute-done.70 = bf16[192,768]{1,0:T(8,128)(2,1)S(1)} collective-permute-done((bf16[192,768]{1,0:T(8,128)(2,1)S(1)}, bf16[192,768]{1,0:T(8,128)(2,1)S(1)}, u32[]{:S(2)}, u32[]{:S(2)}) %collective-permute-start.70) | collective-permute-done | bytes 294944 | tf_op jit(solution)/shard_map/ppermute | solution.py:30
  (290 shorter events, 122.0 us)
Async XLA Ops:
  0.6 36.7 %collective-permute-start = (bf16[512,768]{1,0:T(8,128)(2,1)}, bf16[512,768]{1,0:T(8,128)(2,1)}, u32[]{:S(2)}, u32[]{:S(2)}) collective-permute-start(bf16[512,768]{1,0:T(8,128)(2,1)} %refs_0_), channel_id=1, source_target_pairs={{0,8},{4,12},{8,0},{12,4},{16,24},{20,28},{24,16},{28,20},{1,9},{5... | collective-permute-start | bytes 2359304 | tf_op jit(solution)/shard_map/ppermute | solution.py:25
  2.2 35.2 %collective-permute-start.1 = (bf16[512,768]{1,0:T(8,128)(2,1)}, bf16[512,768]{1,0:T(8,128)(2,1)}, u32[]{:S(2)}, u32[]{:S(2)}) collective-permute-start(bf16[512,768]{1,0:T(8,128)(2,1)} %refs_0_), channel_id=1, source_target_pairs={{0,16},{4,20},{8,24},{12,28},{16,0},{20,4},{24,8},{28,12},{1,17},{... | collective-permute-start | bytes 2359304 | tf_op jit(solution)/shard_map/ppermute | solution.py:25
  2.7 34.7 %collective-permute-start.2 = (bf16[512,768]{1,0:T(8,128)(2,1)}, bf16[512,768]{1,0:T(8,128)(2,1)S(1)}, u32[]{:S(2)}, u32[]{:S(2)}) collective-permute-start(bf16[512,768]{1,0:T(8,128)(2,1)} %refs_0_), channel_id=1, source_target_pairs={{0,4},{4,0},{8,12},{12,8},{16,20},{20,16},{24,28},{28,24},{1,5},{5... | collective-permute-start | bytes 2359304 | tf_op jit(solution)/shard_map/ppermute | solution.py:25
  8.1 29.3 %collective-permute-start.4 = (bf16[200,768]{1,0:T(8,128)(2,1)S(1)}, bf16[200,768]{1,0:T(8,128)(2,1)S(1)}, u32[]{:S(2)}, u32[]{:S(2)}) collective-permute-start(bf16[200,768]{1,0:T(8,128)(2,1)S(1)} %constant_dynamic-update-slice_fusion), channel_id=1, source_target_pairs={{0,2},{1,3},{2,0},{3,1},{4,6},{5,7},{6,4},{7,5},{8,10},{9,11},{10,... | collective-permute-start | bytes 921608 | tf_op jit(solution)/shard_map/ppermute | solution.py:30
  38.7 23.8 %collective-permute-start.8 = (bf16[512,768]{1,0:T(8,128)(2,1)}, bf16[512,768]{1,0:T(8,128)(2,1)}, u32[]{:S(2)}, u32[]{:S(2)}) collective-permute-start(bf16[512,768]{1,0:T(8,128)(2,1)} %collective-permute-done.refs_2_), channel_id=1, source_target_pairs={{0,4},{4,0},{8,12},{12,8},{16,20},{20,16},{24,28},{28,24},{1,5},{5... | collective-permute-start | bytes 2359304 | tf_op jit(solution)/shard_map/ppermute | solution.py:25
  65.8 26.7 %collective-permute-start.22 = (bf16[192,768]{1,0:T(8,128)(2,1)S(1)}, bf16[192,768]{1,0:T(8,128)(2,1)S(1)}, u32[]{:S(2)}, u32[]{:S(2)}) collective-permute-start(bf16[192,768]{1,0:T(8,128)(2,1)S(1)} %pad_maximum_fusion.14), channel_id=1, source_target_pairs={{0,2},{1,3},{2,0},{3,1},{4,6},{5,7},{6,4},{7,5},{8,10},{9,11},{10,... | collective-permute-start | bytes 884744 | tf_op jit(solution)/shard_map/ppermute | solution.py:30
  68.5 24.1 %collective-permute-start.23 = (bf16[192,768]{1,0:T(8,128)(2,1)S(1)}, bf16[192,768]{1,0:T(8,128)(2,1)S(1)}, u32[]{:S(2)}, u32[]{:S(2)}) collective-permute-start(bf16[192,768]{1,0:T(8,128)(2,1)S(1)} %pad_maximum_fusion.14), channel_id=1, source_target_pairs={{0,3},{1,0},{2,1},{3,2},{4,7},{5,4},{6,5},{7,6},{8,11},{9,8},{10,9... | collective-permute-start | bytes 884744 | tf_op jit(solution)/shard_map/ppermute | solution.py:30
  115.8 36.4 %collective-permute-start.33 = (bf16[768,768]{1,0:T(8,128)(2,1)S(1)}, bf16[768,768]{1,0:T(8,128)(2,1)S(1)}, u32[]{:S(2)}, u32[]{:S(2)}) collective-permute-start(bf16[768,768]{1,0:T(8,128)(2,1)S(1)} %pad_maximum_fusion.3.refs_0_), channel_id=1, source_target_pairs={{0,8},{4,12},{8,0},{12,4},{16,24},{20,28},{24,16},{28,20},{1,9},{5... | collective-permute-start | bytes 3538952 | tf_op jit(solution)/shard_map/ppermute | solution.py:25
  116.4 36.4 %collective-permute-start.34 = (bf16[768,768]{1,0:T(8,128)(2,1)S(1)}, bf16[768,768]{1,0:T(8,128)(2,1)}, u32[]{:S(2)}, u32[]{:S(2)}) collective-permute-start(bf16[768,768]{1,0:T(8,128)(2,1)S(1)} %pad_maximum_fusion.3.refs_0_), channel_id=1, source_target_pairs={{0,16},{4,20},{8,24},{12,28},{16,0},{20,4},{24,8},{28,12},{1,17},{... | collective-permute-start | bytes 3538952 | tf_op jit(solution)/shard_map/ppermute | solution.py:25
  121.3 31.0 %collective-permute-start.30 = (bf16[288,768]{1,0:T(8,128)(2,1)S(1)}, bf16[288,768]{1,0:T(8,128)(2,1)}, u32[]{:S(2)}, u32[]{:S(2)}) collective-permute-start(bf16[288,768]{1,0:T(8,128)(2,1)S(1)} %slice.321), channel_id=1, source_target_pairs={{0,8},{4,12},{8,0},{12,4},{16,24},{20,28},{24,16},{28,20},{1,9},{5... | collective-permute-start | bytes 1327112 | tf_op jit(solution)/shard_map/ppermute | solution.py:25
  124.6 24.8 %collective-permute-start.29 = (bf16[192,768]{1,0:T(8,128)(2,1)}, bf16[192,768]{1,0:T(8,128)(2,1)}, u32[]{:S(2)}, u32[]{:S(2)}) collective-permute-start(bf16[192,768]{1,0:T(8,128)(2,1)} %slice.320), channel_id=1, source_target_pairs={{0,16},{4,20},{8,24},{12,28},{16,0},{20,4},{24,8},{28,12},{1,17},{... | collective-permute-start | bytes 884744 | tf_op jit(solution)/shard_map/ppermute | solution.py:25
  127.7 40.3 %collective-permute-start.27 = (bf16[480,768]{1,0:T(8,128)(2,1)}, bf16[480,768]{1,0:T(8,128)(2,1)S(1)}, u32[]{:S(2)}, u32[]{:S(2)}) collective-permute-start(bf16[480,768]{1,0:T(8,128)(2,1)} %collective-permute-done.24.refs_2_), channel_id=1, source_target_pairs={{0,4},{4,0},{8,12},{12,8},{16,20},{20,16},{24,28},{28,24},{1,5},{5... | collective-permute-start | bytes 2211848 | tf_op jit(solution)/shard_map/ppermute | solution.py:25
  273.8 28.8 %collective-permute-start.64 = (bf16[1,768,768]{2,1,0:T(8,128)(2,1)}, bf16[1,768,768]{2,1,0:T(8,128)(2,1)S(1)}, u32[]{:S(2)}, u32[]{:S(2)}) collective-permute-start(bf16[1,768,768]{2,1,0:T(8,128)(2,1)} %bitcast.70), channel_id=1, source_target_pairs={{0,4},{4,0},{8,12},{12,8},{16,20},{20,16},{24,28},{28,24},{1,5},{5... | collective-permute-start | bytes 3538952 | tf_op jit(solution)/shard_map/ppermute | solution.py:25
  273.9 44.3 %collective-permute-start.55 = (bf16[4,480,768]{2,1,0:T(8,128)(2,1)}, bf16[4,480,768]{2,1,0:T(8,128)(2,1)}, u32[]{:S(2)}, u32[]{:S(2)}) collective-permute-start(bf16[4,480,768]{2,1,0:T(8,128)(2,1)} %get-tuple-element.172), channel_id=1, source_target_pairs={{0,4},{4,0},{8,12},{12,8},{16,20},{20,16},{24,28},{28,24},{1,5},{5... | collective-permute-start | bytes 8847368 | tf_op jit(solution)/shard_map/ppermute | solution.py:25
  290.6 30.7 %collective-permute-start.42 = (bf16[4,512,768]{2,1,0:T(8,128)(2,1)}, bf16[4,512,768]{2,1,0:T(8,128)(2,1)}, u32[]{:S(2)}, u32[]{:S(2)}) collective-permute-start(bf16[4,512,768]{2,1,0:T(8,128)(2,1)} %get-tuple-element.167), channel_id=1, source_target_pairs={{0,4},{4,0},{8,12},{12,8},{16,20},{20,16},{24,28},{28,24},{1,5},{5... | collective-permute-start | bytes 9437192 | tf_op jit(solution)/shard_map/ppermute | solution.py:25
  299.8 38.7 %collective-permute-start.63 = (bf16[3,768,768]{2,1,0:T(8,128)(2,1)}, bf16[3,768,768]{2,1,0:T(8,128)(2,1)S(1)}, u32[]{:S(2)}, u32[]{:S(2)}) collective-permute-start(bf16[3,768,768]{2,1,0:T(8,128)(2,1)} %bitcast.235), channel_id=1, source_target_pairs={{0,4},{4,0},{8,12},{12,8},{16,20},{20,16},{24,28},{28,24},{1,5},{5... | collective-permute-start | bytes 10616840 | tf_op jit(solution)/shard_map/ppermute | solution.py:25
  313.4 28.1 %collective-permute-start.65 = (bf16[384,768]{1,0:T(8,128)(2,1)S(1)}, bf16[384,768]{1,0:T(8,128)(2,1)S(1)}, u32[]{:S(2)}, u32[]{:S(2)}) collective-permute-start(bf16[384,768]{1,0:T(8,128)(2,1)S(1)} %get-tuple-element.208), channel_id=1, source_target_pairs={{0,16},{4,20},{8,24},{12,28},{16,0},{20,4},{24,8},{28,12},{1,17},{... | collective-permute-start | bytes 1769480 | tf_op jit(solution)/shard_map/ppermute | solution.py:25
  315.0 28.4 %collective-permute-start.67 = (bf16[384,768]{1,0:T(8,128)(2,1)S(1)}, bf16[384,768]{1,0:T(8,128)(2,1)S(1)}, u32[]{:S(2)}, u32[]{:S(2)}) collective-permute-start(bf16[384,768]{1,0:T(8,128)(2,1)S(1)} %get-tuple-element.209), channel_id=1, source_target_pairs={{0,8},{4,12},{8,0},{12,4},{16,24},{20,28},{24,16},{28,20},{1,9},{5... | collective-permute-start | bytes 1769480 | tf_op jit(solution)/shard_map/ppermute | solution.py:25
  338.5 27.4 %collective-permute-start.57 = (bf16[480,768]{1,0:T(8,128)(2,1)S(1)}, bf16[480,768]{1,0:T(8,128)(2,1)S(1)}, u32[]{:S(2)}, u32[]{:S(2)}) collective-permute-start(bf16[480,768]{1,0:T(8,128)(2,1)S(1)} %pad_maximum_fusion.9), channel_id=1, source_target_pairs={{0,8},{4,12},{8,0},{12,4},{16,24},{20,28},{24,16},{28,20},{1,9},{5... | collective-permute-start | bytes 2211848 | tf_op jit(solution)/shard_map/ppermute | solution.py:25
  341.5 24.3 %collective-permute-start.59 = (bf16[480,768]{1,0:T(8,128)(2,1)S(1)}, bf16[480,768]{1,0:T(8,128)(2,1)S(1)}, u32[]{:S(2)}, u32[]{:S(2)}) collective-permute-start(bf16[480,768]{1,0:T(8,128)(2,1)S(1)} %pad_maximum_fusion.10), channel_id=1, source_target_pairs={{0,16},{4,20},{8,24},{12,28},{16,0},{20,4},{24,8},{28,12},{1,17},{... | collective-permute-start | bytes 2211848 | tf_op jit(solution)/shard_map/ppermute | solution.py:25
  343.9 47.2 %collective-permute-start.66 = (bf16[768,768]{1,0:T(8,128)(2,1)S(1)}, bf16[768,768]{1,0:T(8,128)(2,1)S(1)}, u32[]{:S(2)}, u32[]{:S(2)}) collective-permute-start(bf16[768,768]{1,0:T(8,128)(2,1)S(1)} %pad_maximum_fusion.4), channel_id=1, source_target_pairs={{0,8},{4,12},{8,0},{12,4},{16,24},{20,28},{24,16},{28,20},{1,9},{5... | collective-permute-start | bytes 3538952 | tf_op jit(solution)/shard_map/ppermute | solution.py:25
  346.3 44.8 %collective-permute-start.68 = (bf16[768,768]{1,0:T(8,128)(2,1)S(1)}, bf16[768,768]{1,0:T(8,128)(2,1)S(1)}, u32[]{:S(2)}, u32[]{:S(2)}) collective-permute-start(bf16[768,768]{1,0:T(8,128)(2,1)S(1)} %pad_maximum_fusion.5), channel_id=1, source_target_pairs={{0,16},{4,20},{8,24},{12,28},{16,0},{20,4},{24,8},{28,12},{1,17},{... | collective-permute-start | bytes 3538952 | tf_op jit(solution)/shard_map/ppermute | solution.py:25
  373.3 30.5 %collective-permute-start.44 = (bf16[512,768]{1,0:T(8,128)(2,1)S(1)}, bf16[512,768]{1,0:T(8,128)(2,1)S(1)}, u32[]{:S(2)}, u32[]{:S(2)}) collective-permute-start(bf16[512,768]{1,0:T(8,128)(2,1)S(1)} %pad_maximum_fusion.6), channel_id=1, source_target_pairs={{0,8},{4,12},{8,0},{12,4},{16,24},{20,28},{24,16},{28,20},{1,9},{5... | collective-permute-start | bytes 2359304 | tf_op jit(solution)/shard_map/ppermute | solution.py:25
  393.1 24.2 %collective-permute-start.70 = (bf16[192,768]{1,0:T(8,128)(2,1)S(1)}, bf16[192,768]{1,0:T(8,128)(2,1)S(1)}, u32[]{:S(2)}, u32[]{:S(2)}) collective-permute-start(bf16[192,768]{1,0:T(8,128)(2,1)S(1)} %get-tuple-element.207), channel_id=1, source_target_pairs={{0,2},{1,3},{2,0},{3,1},{4,6},{5,7},{6,4},{7,5},{8,10},{9,11},{10,... | collective-permute-start | bytes 884744 | tf_op jit(solution)/shard_map/ppermute | solution.py:30
  (77 other events, 1078.5 us)

commit v3 on v2

--- a/solution.py
+++ b/solution.py
@@ -47,15 +47,28 @@
     return [item[1:] for item in sorted(found)]
 
 
+def inner_gather(shard):
+    count = lax.axis_size("fsdp")
+    me = lax.axis_index("fsdp")
+    held = shard[None]
+    mask = 1
+    while mask < count:
+        came = lax.ppermute(held, "fsdp", [(i, i ^ mask) for i in range(count)])
+        high = (me & mask) != 0
+        held = jnp.concatenate([jnp.where(high, came, held), jnp.where(high, held, came)])
+        mask *= 2
+    return held
+
+
+def inner_start(shard):
+    return [shard] + [shift(shard, step) for step in range(1, lax.axis_size("fsdp"))]
+
+
 def inner_order(came):
     count = len(came)
     me = lax.axis_index("fsdp")
     line = [came[count - 1 - k] for k in range(count)] + [came[count - k] for k in range(1, count)]
     return lax.dynamic_slice_in_dim(jnp.stack(line), count - 1 - me, count, 0)
-
-
-def inner_start(shard):
-    return [shard] + [shift(shard, step) for step in range(1, lax.axis_size("fsdp"))]
 
 
 def single_steps(block):
@@ -100,37 +113,57 @@
     return (a.astype(f32) + b.astype(f32)).astype(bf16)
 
 
-def outer_sum(total, cut):
-    held = {2 * g: total[g] for g in range(total.shape[0])}
-    extra = {e: {0: [], 1: []} for e in held}
-
-    def half_sum(e, which):
-        part = held[e][:cut] if which == 0 else held[e][cut:]
-        for came in extra[e][which]:
+class OuterSum:
+    def __init__(self, total, cut):
+        self.held = {2 * g: block for g, block in enumerate(total)}
+        self.cut = cut
+        self.extra = {e: {0: [], 1: []} for e in self.held}
+        self.came = []
+
+    def half(self, e, which):
+        part = self.held[e][: self.cut] if which == 0 else self.held[e][self.cut :]
+        for came in self.extra[e][which]:
             part = add_low(part, came)
         return part
 
-    for e, top, low in relays()[::-1]:
-        extra[e ^ top][0].append(swap(half_sum(e, 0), top))
-        extra[e ^ low][1].append(swap(half_sum(e, 1), low))
-    came = []
-    for mask in link_masks():
-        came.append(swap(jnp.concatenate([half_sum(mask, 0), half_sum(mask, 1)]), mask))
-    result = held[0].astype(f32)
-    for block in came:
-        result = result + block.astype(f32)
-    return result
-
-
-def inner_sum(parts):
-    count = parts.shape[0]
-    me = lax.axis_index("fsdp")
-    low = parts.astype(bf16)
-    total = lax.dynamic_index_in_dim(parts, me, 0, keepdims=False)
-    for step in range(1, count):
-        going = lax.dynamic_index_in_dim(low, (me + step) % count, 0, keepdims=False)
-        total = total + shift(going, step).astype(f32)
-    return total
+    def relays(self):
+        for e, top, low in relays()[::-1]:
+            self.extra[e ^ top][0].append(swap(self.half(e, 0), top))
+            self.extra[e ^ low][1].append(swap(self.half(e, 1), low))
+
+    def singles(self):
+        self.came = [
+            swap(jnp.concatenate([self.half(mask, 0), self.half(mask, 1)]), mask) for mask in link_masks()
+        ]
+
+    def result(self):
+        total = self.held[0].astype(f32)
+        for block in self.came:
+            total = total + block.astype(f32)
+        return total
+
+    def state(self):
+        return (self.held, self.extra, self.came)
+
+    def put(self, state):
+        self.held, self.extra, self.came = state
+
+
+class InnerSum:
+    def __init__(self, parts):
+        count = parts.shape[0]
+        me = lax.axis_index("fsdp")
+        low = parts.astype(bf16)
+        self.own = lax.dynamic_index_in_dim(parts, me, 0, keepdims=False)
+        self.came = [
+            shift(lax.dynamic_index_in_dim(low, (me + step) % count, 0, keepdims=False), step) for step in range(1, count)
+        ]
+
+    def result(self):
+        total = self.own
+        for block in self.came:
+            total = total + block.astype(f32)
+        return total
 
 
 def nn(a, b):
@@ -187,6 +220,16 @@
 
 def bias_of(key_seg, own_seg):
     return jnp.where(key_seg == own_seg, 0.0, -1e30).astype(f32)
+
+
+def block_bias(key_seg, ints, blocks):
+    return jnp.stack([bias_of(key_seg[...], ints[1 + 3 * blocks + i]) for i in range(blocks)])
+
+
+def biased(scores, bias):
+    blocks, _, keys = bias.shape
+    rows = scores.shape[0] // (2 * blocks)
+    return (scores.reshape(2, blocks, rows, keys) + bias[None]).reshape(scores.shape)
 
 
 def copies(jobs, sems, at):
@@ -278,7 +321,7 @@
     jobs = []
     for ref, (e, start, rows) in zip(refs, places):
         for (first, size), weight in zip(layout, weights):
-            if first >= start and first + size <= start + rows:
+            if weight is not None and first >= start and first + size <= start + rows:
                 at = pl.multiple_of((me ^ e) * size, 16)
                 jobs.append((ref.at[pl.ds(first - start, size)], weight.at[pl.ds(at, size)]))
     return copies(jobs, sems, 0)
@@ -302,15 +345,12 @@
     for at, step in tiles(width):
         cq_ref[:, at : at + step] = (nn(crossed_in, w_cq[:, at : at + step]) * 0.125).astype(bf16)
 
-    @pl.loop(0, blocks)
-    def _(i):
-        bias = bias_of(coarse_seg[...], ints[1 + 3 * blocks + i])
-        rows = pl.ds(pl.multiple_of(i * CLIP, CLIP), CLIP)
-        for at in range(0, width, PAIR):
-            queries = two_heads(cq_ref[rows, at : at + PAIR])
-            probs = softmax_rows(nt(queries, ckv_ref[:, at : at + PAIR]) + bias).astype(bf16)
-            out = nn(probs, ckv_ref[:, width + at : width + at + PAIR])
-            crossed_ref[rows, at : at + PAIR] = side_by_side(out).astype(bf16)
+    bias = block_bias(coarse_seg, ints, blocks)
+    for at in range(0, width, PAIR):
+        queries = two_heads(cq_ref[:, at : at + PAIR])
+        probs = softmax_rows(biased(nt(queries, ckv_ref[:, at : at + PAIR]), bias)).astype(bf16)
+        out = nn(probs, ckv_ref[:, width + at : width + at + PAIR])
+        crossed_ref[:, at : at + PAIR] = side_by_side(out).astype(bf16)
 
     for at, step in tiles(width):
         joined_ref[:, at : at + step] = residual_ref[:, at : at + step] + nn(crossed_ref[...], w_cout[:, at : at + step])
@@ -386,64 +426,79 @@
     for e in range(dp_count):
         target = send_ref if e & CORE else keep_ref
         for (first, size), source in zip(layout, sources):
+            if source is None:
+                continue
             row = pl.multiple_of((me ^ e) * size, 16)
             jobs.append((source.at[pl.ds(row, size)], target.at[e // 2, pl.ds(first, size)]))
     return copies(jobs, sems, at)
 
 
 def third_kernel(
-    geometry, ints, coarse_seg, coarse, gains, mlp_out, grad_second, joined, cotangent, residual, attended, crossed, cq, ckv, *refs
+    geometry, ints, coarse_seg, gains, mlp_out, grad_second, joined, cotangent, crossed, cq, ckv, *refs
 ):
     blocks, places, layout, dp_count = geometry
     weight_refs = refs[: len(places)]
     refs = refs[len(places) :]
-    output_ref, coarse_ref, grad_res_ref, grad_att_ref, gain_grads_ref, keep_ref, send_ref = refs[:7]
-    w_ckv, w_out, w_cq, w_cout, g_ckv, g_out, g_cq, g_cout, crossed_in, grad_cross, grad_cq, key_sum, value_sum, grad_joined, sems = refs[7:]
+    output_ref, grad_joined_ref, grad_cq_ref, grad_ckv_ref, gain_grads_ref, keep_ref, send_ref = refs[:7]
+    w_cout, g_cout, grad_cross, sems = refs[7:]
     me = ints[0]
     width = joined.shape[1]
-    made = load_cross(me, weight_refs, places, layout, (w_ckv, w_out, w_cq, w_cout), sems)
+    made = load_cross(me, weight_refs, places, layout, (None, None, None, w_cout), sems)
     output_ref[...] = (joined[...] + mlp_out[...]).astype(bf16)
     xhat, r = centred(joined[...])
     grad_in, gain_two = norm_back(xhat, r, gains[2:3], grad_second[...])
-    grad_joined[...] = cotangent[...].astype(f32) + grad_in
-    low = grad_joined[...].astype(bf16)
+    grad_joined_ref[...] = cotangent[...].astype(f32) + grad_in
+    low = grad_joined_ref[...].astype(bf16)
     for job in made:
         job.wait()
     for at, step in tiles(width):
         grad_cross[:, at : at + step] = nt(low, w_cout[at : at + step, :]).astype(bf16)
     for at, step in tiles(width):
         g_cout[at : at + step, :] = tn(crossed[:, at : at + step], low).astype(bf16)
-    key_sum[...] = jnp.zeros_like(key_sum)
-    value_sum[...] = jnp.zeros_like(value_sum)
-
-    @pl.loop(0, blocks)
-    def _(i):
-        bias = bias_of(coarse_seg[...], ints[1 + 3 * blocks + i])
-        rows = pl.ds(pl.multiple_of(i * CLIP, CLIP), CLIP)
-        for at in range(0, width, PAIR):
-            lanes = slice(at, at + PAIR)
-            queries = two_heads(cq[rows, lanes])
-            grads = two_heads(grad_cross[rows, lanes])
-            keys = ckv[:, lanes]
-            values = ckv[:, width + at : width + at + PAIR]
-            probs = softmax_rows(nt(queries, keys) + bias)
-            value_sum[:, lanes] += tn(probs.astype(bf16), grads)
-            grad_probs = nt(grads, values)
-            inner = jnp.sum(probs * grad_probs, axis=-1, keepdims=True)
-            scores = (probs * (grad_probs - inner)).astype(bf16)
-            part = side_by_side(nn(scores, keys)).astype(bf16)
-            grad_cq[rows, lanes] = part * jnp.asarray(0.125, bf16)
-            key_sum[:, lanes] += tn(scores, queries)
-
+    going = grads_out(me, dp_count, layout, (None, None, None, g_cout), keep_ref, send_ref, sems, len(made))
+    bias = block_bias(coarse_seg, ints, blocks)
+    for at in range(0, width, PAIR):
+        lanes = slice(at, at + PAIR)
+        queries = two_heads(cq[:, lanes])
+        grads = two_heads(grad_cross[:, lanes])
+        keys = ckv[:, lanes]
+        values = ckv[:, width + at : width + at + PAIR]
+        probs = softmax_rows(biased(nt(queries, keys), bias))
+        grad_ckv_ref[:, width + at : width + at + PAIR] = tn(probs.astype(bf16), grads).astype(bf16)
+        grad_probs = nt(grads, values)
+        inner = jnp.sum(probs * grad_probs, axis=-1, keepdims=True)
+        scores = (probs * (grad_probs - inner)).astype(bf16)
+        part = side_by_side(nn(scores, keys)).astype(bf16)
+        grad_cq_ref[:, lanes] = part * jnp.asarray(0.125, bf16)
+        grad_ckv_ref[:, lanes] = tn(scores, queries).astype(bf16)
+
+    gain_grads_ref[...] = jnp.concatenate([gain_two] * 8, axis=0)
+    for job in going:
+        job.wait()
+
+
+def third_part(geometry, ints, coarse, gains, gain_two, grad_joined, residual, attended, grad_cq, grad_ckv, keep_in, send_in, *refs):
+    places, layout, dp_count = geometry
+    weight_refs = refs[: len(places)]
+    refs = refs[len(places) :]
+    coarse_ref, grad_res_ref, grad_att_ref, gain_grads_ref, keep_ref, send_ref = refs[:6]
+    w_ckv, w_out, w_cq, g_ckv, g_out, g_cq, crossed_in, sems = refs[6:]
+    me = ints[0]
+    width = residual.shape[1]
+    made = load_cross(me, weight_refs, places, layout, (w_ckv, w_out, w_cq, None), sems)
     xhat, r = centred(residual[...])
     crossed_in[...] = (xhat * gains[1:2]).astype(bf16)
     for at, step in tiles(width):
         g_cq[at : at + step, :] = tn(crossed_in[:, at : at + step], grad_cq[...]).astype(bf16)
-    dk, dv = key_sum[...].astype(bf16), value_sum[...].astype(bf16)
+    for at, step in tiles(2 * width):
+        g_ckv[at : at + step, :] = tn(grad_ckv[:, at : at + step], coarse[...]).astype(bf16)
+    for job in made:
+        job.wait()
+    going = grads_out(me, dp_count, layout, (g_ckv, None, g_cq, None), keep_ref, send_ref, sems, 0)
     for at, step in tiles(width):
-        g_ckv[at : at + step, :] = tn(dk[:, at : at + step], coarse[...]).astype(bf16)
-        g_ckv[width + at : width + at + step, :] = tn(dv[:, at : at + step], coarse[...]).astype(bf16)
-        coarse_ref[:, at : at + step] = nn(dk, w_ckv[0:width, at : at + step]) + nn(dv, w_ckv[width : 2 * width, at : at + step])
+        coarse_ref[:, at : at + step] = nn(grad_ckv[:, 0:width], w_ckv[0:width, at : at + step]) + nn(
+            grad_ckv[:, width : 2 * width], w_ckv[width : 2 * width, at : at + step]
+        )
     pieces = [nt(grad_cq[...], w_cq[at : at + step, :]) for at, step in tiles(width)]
     grad_in, gain_cross = norm_back(xhat, r, gains[1:2], jnp.concatenate(pieces, axis=1))
     grad_res = grad_joined[...] + grad_in
@@ -451,30 +506,18 @@
     low = grad_res.astype(bf16)
     for at, step in tiles(width):
         g_out[at : at + step, :] = tn(attended[:, at : at + step], low).astype(bf16)
-    going = grads_out(me, dp_count, layout, (g_ckv, g_out, g_cq, g_cout), keep_ref, send_ref, sems, sems.shape[0] - 4 * dp_count)
+    going += grads_out(me, dp_count, layout, (None, g_out, None, None), keep_ref, send_ref, sems, len(going))
     for at, step in tiles(width):
         grad_att_ref[:, at : at + step] = nt(low, w_out[at : at + step, :]).astype(bf16)
-    zero = jnp.zeros_like(gain_two)
-    gain_grads_ref[...] = jnp.concatenate([zero, gain_cross, gain_two] + [zero] * 5, axis=0)
+    zero = jnp.zeros_like(gain_cross)
+    gain_grads_ref[...] = jnp.concatenate([zero, gain_cross, gain_two[0:1]] + [zero] * 5, axis=0)
     for job in going:
         job.wait()
 
 
-def fourth_kernel(geometry, ints, mix, seg_row, gains, gain_grads, blended, grad_res, grad_att, qkv, *refs):
-    dp_count, blocks, qkv_places, qkv_rows = geometry
-    weight_refs = refs[: len(qkv_places)]
-    refs = refs[len(qkv_places) :]
-    base_ref, keep_ref, send_ref, mix_keep_ref, mix_send_ref = refs[:5]
-    weight, grad_w, grad_proj, key_sum, value_sum, going_back, gain_rows, sems = refs[5:]
-    me = ints[0]
-    width = blended.shape[1]
-    jobs = []
-    for ref, (e, start, rows) in zip(weight_refs, qkv_places):
-        take = min(rows, qkv_rows - start)
-        at = pl.multiple_of((me ^ e) * qkv_rows + start, 16)
-        jobs.append((ref.at[pl.ds(0, take)], weight.at[pl.ds(at, take)]))
-    made = copies(jobs, sems, 0)
-    going_back[...] = jnp.zeros_like(going_back)
+def fourth_kernel(geometry, ints, seg_row, grad_att, qkv, grad_proj, key_sum, value_sum):
+    (blocks,) = geometry
+    width = grad_att.shape[1]
     key_sum[...] = jnp.zeros_like(key_sum)
     value_sum[...] = jnp.zeros_like(value_sum)
 
@@ -501,24 +544,29 @@
 
     grad_proj[:, width : 2 * width] = key_sum[...].astype(bf16)
     grad_proj[:, 2 * width : 3 * width] = value_sum[...].astype(bf16)
+
+
+def fifth_kernel(geometry, ints, mix, gains, blended, grad_res, grad_proj, *refs):
+    dp_count, blocks, qkv_places, qkv_rows = geometry
+    weight_refs = refs[: len(qkv_places)]
+    refs = refs[len(qkv_places) :]
+    base_ref, gain_ref, mix_keep_ref, mix_send_ref = refs[:4]
+    weight, going_back, sems = refs[4:]
+    me = ints[0]
+    width = blended.shape[1]
+    jobs = []
+    for ref, (e, start, rows) in zip(weight_refs, qkv_places):
+        take = min(rows, qkv_rows - start)
+        at = pl.multiple_of((me ^ e) * qkv_rows + start, 16)
+        jobs.append((ref.at[pl.ds(0, take)], weight.at[pl.ds(at, take)]))
+    made = copies(jobs, sems, 0)
+    going_back[...] = jnp.zeros_like(going_back)
     xhat, r = centred(blended[...])
-    normed = (xhat * gains[0:1]).astype(bf16)
-    for at, step in tiles(3 * width):
-        grad_w[at : at + step, :] = tn(grad_proj[:, at : at + step], normed).astype(bf16)
-    sent = grads_out(me, dp_count, ((0, qkv_rows),), (grad_w,), keep_ref, send_ref, sems, len(jobs))
     for job in made:
         job.wait()
     pieces = [nn(grad_proj[...], weight[:, at : at + step]) for at, step in tiles(width)]
     grad_in, gain_one = norm_back(xhat, r, gains[0:1], jnp.concatenate(pieces, axis=1))
-    all_gains = jnp.concatenate([gain_one, gain_grads[1:8], jnp.zeros((8, width), f32)], axis=0)
-    gain_rows[...] = all_gains.astype(bf16)
-    at = len(jobs) + dp_count
-    last = []
-    for e in range(dp_count):
-        target = send_ref if e & CORE else keep_ref
-        last.append((gain_rows, target.at[e // 2, pl.ds(qkv_rows, 16)]))
-    sent += copies(last, sems, at)
-    at += dp_count
+    gain_ref[...] = jnp.concatenate([gain_one] * 8, axis=0)
     grad_blend = grad_res[...] + grad_in
     for b in range(blocks):
         rows = slice(b * CLIP, (b + 1) * CLIP)
@@ -532,7 +580,26 @@
         target = mix_send_ref if e & CORE else mix_keep_ref
         for s in range(blocks):
             mixed.append((going_back.at[e * blocks + s], target.at[e // 2, pl.ds(s * CLIP, CLIP)]))
-    sent += copies(mixed, sems, at)
+    for job in copies(mixed, sems, len(jobs)):
+        job.wait()
+
+
+def sixth_kernel(geometry, ints, gains, gain_grads, gain_one, blended, grad_proj, keep_ref, send_ref, grad_w, gain_rows, sems):
+    dp_count, qkv_rows = geometry
+    me = ints[0]
+    width = blended.shape[1]
+    xhat, _ = centred(blended[...])
+    normed = (xhat * gains[0:1]).astype(bf16)
+    all_gains = jnp.concatenate([gain_one[0:1], gain_grads[1:8], jnp.zeros((8, width), f32)], axis=0)
+    gain_rows[...] = all_gains.astype(bf16)
+    last = []
+    for e in range(dp_count):
+        target = send_ref if e & CORE else keep_ref
+        last.append((gain_rows, target.at[e // 2, pl.ds(qkv_rows, 16)]))
+    sent = copies(last, sems, 0)
+    for at, step in tiles(3 * width):
+        grad_w[at : at + step, :] = tn(grad_proj[:, at : at + step], normed).astype(bf16)
+    sent += grads_out(me, dp_count, ((0, qkv_rows),), (grad_w,), keep_ref, send_ref, sems, dp_count)
     for job in sent:
         job.wait()
 
@@ -595,46 +662,42 @@
     layout = tuple(layout)
     rows_two = at * fsdp_count
 
+    cut_tok, cut_one, cut_two, cut_mlp = row_count // 2, qkv_rows // 2, layout[0][1], up_rows
+
     held_tok = {0: tokens, **single_steps(tokens)}
-    held_tok_core = swap(tokens, CORE)
-    came_attn = inner_start(jnp.concatenate([shard_one, shard_two]))
-    held_tok, held_tok_core, came_attn = fence((held_tok, held_tok_core, came_attn))
-
-    attn = inner_order(came_attn)
-    one_rows = qkv_part + 8
-    ones, twos = attn[:, :one_rows], attn[:, one_rows:]
+    came_one = inner_start(shard_one)
+    held_tok, came_one, shard_two = fence((held_tok, came_one, shard_two))
+
+    ones = inner_order(came_one)
     gain_block = jnp.sum(ones[:, qkv_part:].astype(f32), axis=0).astype(bf16)
     block_one = jnp.concatenate(
         [ones[:, :qkv_part].reshape(qkv_rows, width), gain_block, jnp.zeros((8, width), bf16)]
     )
+    held_one = {0: block_one, **single_steps(block_one)}
+    came_two = inner_start(shard_two)
+    held_tok, held_one, came_two, shard_mlp = fence((held_tok, held_one, came_two, shard_mlp))
+
+    mlp = inner_gather(shard_mlp)
+    core_tok = core_steps({e: b for e, b in held_tok.items()})
+    relay_steps(held_tok, cut_tok)
+    twos = inner_order(came_two)
     split = []
     at = 0
     for size in sizes_two:
         split.append(twos[:, at : at + size].reshape(size * fsdp_count, width))
         at += size
     block_two = jnp.concatenate(split)
-    cut_tok, cut_one, cut_two, cut_mlp = row_count // 2, qkv_rows // 2, layout[0][1], up_rows
-
-    relay_steps(held_tok, cut_tok)
-    core_tok = core_steps({e: b for e, b in held_tok.items() if e and not isinstance(b, tuple)})
-    held_one = {0: block_one, **single_steps(block_one)}
-    held_tok, core_tok, held_one, shard_mlp, block_two = fence(
-        (held_tok, core_tok, held_one, shard_mlp, block_two)
-    )
-    core_tok.update({1: held_tok_core})
-    core_tok.update(core_steps({e: b for e, b in held_tok.items() if isinstance(b, tuple)}))
-    pieces_tok = {**held_tok, **core_tok}
-
-    came_mlp = inner_start(shard_mlp)
+    held_one, core_tok, held_tok, block_two = fence((held_one, core_tok, held_tok, block_two))
+
+    core_one = core_steps({e: b for e, b in held_one.items()})
     relay_steps(held_one, cut_one)
-    pieces_one = core_steps(held_one)
-    pieces_tok, pieces_one, came_mlp, block_two = fence((pieces_tok, pieces_one, came_mlp, block_two))
+    late_tok = core_steps({e: b for e, b in held_tok.items() if isinstance(b, tuple)})
+    held_one, core_one, late_tok, block_two = fence((held_one, core_one, late_tok, block_two))
 
     held_two = {0: block_two, **single_steps(block_two)}
-    mlp = inner_order(came_mlp)
-    block_mlp = jnp.concatenate(
-        [mlp[:, :up_part].reshape(up_rows, width), mlp[:, up_part:].reshape(up_rows, width)]
-    )
+    late_one = core_steps({e: b for e, b in held_one.items() if isinstance(b, tuple)})
+    pieces_tok = {**core_tok, **late_tok}
+    pieces_one = {**core_one, **late_one}
     arrays_tok, places_tok = parts_of(pieces_tok, row_count, cut_tok)
     arrays_one, places_one = parts_of(pieces_one, qkv_rows + 16, cut_one)
     blended, qkv, attended, gains = pl.pallas_call(
@@ -654,14 +717,23 @@
             pltpu.SemaphoreType.DMA((blocks + len(arrays_one) + dp_count,)),
         ],
         compiler_params=params(),
-        cost_estimate=cost(2e9 * 10, 12e6),
+        cost_estimate=cost(1e9, 1e6),
         name="mix_self_attention",
     )(ints, mix_weight, seg_row, tokens, *arrays_tok, *arrays_one)
-    held_two, block_mlp = fence((held_two, block_mlp))
-
+    held_two, attended = fence((held_two, attended))
+
+    core_two = core_steps({e: b for e, b in held_two.items()})
     relay_steps(held_two, cut_two)
-    pieces_two = core_steps(held_two)
+    held_two, core_two, mlp = fence((held_two, core_two, mlp))
+
+    block_mlp = jnp.concatenate(
+        [mlp[:, :up_part].reshape(up_rows, width), mlp[:, up_part:].reshape(up_rows, width)]
+    )
     held_mlp = {0: block_mlp, **single_steps(block_mlp)}
+    late_two = core_steps({e: b for e, b in held_two.items() if isinstance(b, tuple)})
+    pieces_two = {**core_two, **late_two}
+    wide = [pltpu.VMEM((sizes * fsdp_count * dp_count, width), bf16) for sizes in sizes_two]
+    n_two = 4 * dp_count
     arrays_two, places_two = parts_of(pieces_two, rows_two, cut_two)
     wide = [pltpu.VMEM((sizes * fsdp_count * dp_count, width), bf16) for sizes in sizes_two]
     n_two = 4 * dp_count
@@ -679,15 +751,17 @@
         out_specs=(VMEM,) * 6,
         scratch_shapes=wide + [pltpu.SemaphoreType.DMA((n_two,))],
         compiler_params=params(),
-        cost_estimate=cost(2e9 * 10, 12e6),
+        cost_estimate=cost(1e9, 1e6),
         name="cross_attention",
     )(ints, coarse_seg, coarse_view, blended, attended, gains, *arrays_two)
-    held_mlp = fence(held_mlp)
-
-    singles = dict(held_mlp)
-    pieces_mlp = core_steps(singles)
+    held_mlp, second = fence((held_mlp, second))
+
+    core_mlp = core_steps(dict(held_mlp))
+    order = sorted({e & ~CORE for e in core_mlp})
+    early, middle = order[:-1], order[-1:]
+    pieces_early = {e: core_mlp[e] for g in early for e in (g, g | CORE)}
+    pieces_middle = {e: core_mlp[e] for g in middle for e in (g, g | CORE)}
     relay_steps(held_mlp, cut_mlp)
-    late = core_steps({e: b for e, b in held_mlp.items() if isinstance(b, tuple)})
 
     def mlp_call(pieces, carried):
         groups = tuple(sorted({e // 2 for e in pieces}))
@@ -722,24 +796,65 @@
                 pltpu.SemaphoreType.DMA((4 * count,)),
             ],
             compiler_params=params(),
-            cost_estimate=cost(7.2e9 * count, 8e6 * count),
+            cost_estimate=cost(1e9, 1e6),
             name="feed_forward",
         )(second, cotangent, *arrays, *carried)
         flat = (count, 2 * up_rows, width)
         return groups, keep.reshape(flat), send.reshape(flat), out, grad
 
-    groups_a, keep_a, send_a, out_a, grad_a = mlp_call(pieces_mlp, ())
-    groups_b, keep_b, send_b, mlp_out, grad_second = mlp_call(late, (out_a, grad_a))
+    groups_a, keep_a, send_a, out_a, grad_a = mlp_call(pieces_early, ())
+    held_mlp, pieces_middle, keep_a, send_a, out_a, grad_a = fence((held_mlp, pieces_middle, keep_a, send_a, out_a, grad_a))
+
+    late = core_steps({e: b for e, b in held_mlp.items() if isinstance(b, tuple)})
+    came_a = swap(send_a, CORE)
+    groups_m, keep_m, send_m, out_m, grad_m = mlp_call(pieces_middle, (out_a, grad_a))
+    late, came_a, keep_m, send_m, out_m, grad_m = fence((late, came_a, keep_m, send_m, out_m, grad_m))
+
+    came_m = swap(send_m, CORE)
+    groups_b, keep_b, send_b, mlp_out, grad_second = mlp_call(late, (out_m, grad_m))
+    came_m, keep_b, send_b, mlp_out, grad_second = fence((came_m, keep_b, send_b, mlp_out, grad_second))
 
     total_b = add_low(keep_b, swap(send_b, CORE))
-    total_a = add_low(keep_a, swap(send_a, CORE))
-    where = {g: total_a[i] for i, g in enumerate(groups_a)}
-    where.update({g: total_b[i] for i, g in enumerate(groups_b)})
-
-    output, coarse_grad, grad_res, grad_att, gain_grads, keep_two, send_two = pl.pallas_call(
+    total_a = add_low(keep_a, came_a)
+    total_m = add_low(keep_m, came_m)
+    totals = [None] * pairs
+    for groups, total in ((groups_a, total_a), (groups_m, total_m), (groups_b, total_b)):
+        for i, g in enumerate(groups):
+            totals[g] = total[i]
+    totals, mlp_out = fence((totals, mlp_out))
+
+    sum_mlp = OuterSum(totals, cut_mlp)
+    sum_mlp.relays()
+    output, grad_joined, grad_cq, grad_ckv, gain_two, keep_two, send_two = pl.pallas_call(
         functools.partial(third_kernel, (blocks, places_two, layout, dp_count)),
         out_shape=(
             whole((row_count, width), bf16),
+            whole((row_count, width), f32),
+            whole((row_count, width), bf16),
+            whole((coarse_rows, 2 * width), bf16),
+            whole((8, width), f32),
+            whole((pairs, rows_two, width), bf16),
+            whole((pairs, rows_two, width), bf16),
+        ),
+        in_specs=[SMEM] + [VMEM] * 9 + [ANY] * len(arrays_two),
+        out_specs=(VMEM,) * 5 + (ANY,) * 2,
+        scratch_shapes=[
+            wide[3],
+            wide[3],
+            pltpu.VMEM((row_count, width), bf16),
+            pltpu.SemaphoreType.DMA((n_two + dp_count,)),
+        ],
+        compiler_params=params(),
+        cost_estimate=cost(1e9, 1e6),
+        name="cross_attention_backward",
+    )(ints, coarse_seg, gains, mlp_out, grad_second, joined, cotangent, crossed, cq, ckv, *arrays_two)
+    state, grad_joined = fence((sum_mlp.state(), grad_joined))
+    sum_mlp.put(state)
+
+    sum_mlp.singles()
+    coarse_grad, grad_res, grad_att, gain_grads, keep_two, send_two = pl.pallas_call(
+        functools.partial(third_part, (places_two, layout, dp_count)),
+        out_shape=(
             whole((coarse_rows, width), f32),
             whole((row_count, width), f32),
             whole((row_count, width), bf16),
@@ -747,80 +862,130 @@
             whole((pairs, rows_two, width), bf16),
             whole((pairs, rows_two, width), bf16),
         ),
-        in_specs=[SMEM] + [VMEM] * 12 + [ANY] * len(arrays_two),
-        out_specs=(VMEM,) * 5 + (ANY,) * 2,
-        scratch_shapes=wide
-        + wide
-        + [
+        in_specs=[SMEM] + [VMEM] * 8 + [ANY] * (2 + len(arrays_two)),
+        out_specs=(VMEM,) * 4 + (ANY,) * 2,
+        scratch_shapes=[
+            wide[0],
+            wide[1],
+            wide[2],
+            wide[0],
+            wide[1],
+            wide[2],
             pltpu.VMEM((row_count, width), bf16),
-            pltpu.VMEM((row_count, width), bf16),
-            pltpu.VMEM((row_count, width), bf16),
-            pltpu.VMEM((coarse_rows, width), f32),
-            pltpu.VMEM((coarse_rows, width), f32),
-            pltpu.VMEM((row_count, width), f32),
-            pltpu.SemaphoreType.DMA((n_two + 4 * dp_count,)),
+            pltpu.SemaphoreType.DMA((n_two,)),
         ],
+        input_output_aliases={9: 4, 10: 5},
         compiler_params=params(),
-        cost_estimate=cost(2e9 * 12, 30e6),
-        name="cross_attention_backward",
+        cost_estimate=cost(1e9, 1e6),
+        name="cross_attention_weights",
     )(
-        ints, coarse_seg, coarse_view, gains, mlp_out, grad_second, joined, cotangent, residual, attended, crossed, cq, ckv,
-        *arrays_two,
+        ints, coarse_view, gains, gain_two, grad_joined, residual, attended, grad_cq, grad_ckv, keep_two, send_two, *arrays_two
     )
 
-    base, keep_one, send_one, keep_tok, send_tok = pl.pallas_call(
-        functools.partial(fourth_kernel, (dp_count, blocks, places_one, qkv_rows)),
+    (grad_proj,) = pl.pallas_call(
+        functools.partial(fourth_kernel, (blocks,)),
+        out_shape=(whole((row_count, 3 * width), bf16),),
+        in_specs=[SMEM] + [VMEM] * 3,
+        out_specs=(VMEM,),
+        scratch_shapes=[pltpu.VMEM((row_count, width), f32), pltpu.VMEM((row_count, width), f32)],
+        compiler_params=params(),
+        cost_estimate=cost(1e9, 1e6),
+        name="self_attention_backward",
+    )(ints, seg_row, grad_att, qkv)
+    state, grad_proj, keep_two, send_two = fence((sum_mlp.state(), grad_proj, keep_two, send_two))
+    sum_mlp.put(state)
+
+    came_two = swap(send_two, CORE)
+    mlp_sum = sum_mlp.result()
+    mlp_parts = jnp.concatenate(
+        [mlp_sum[:up_rows].reshape(fsdp_count, up_part, width), mlp_sum[up_rows:].reshape(fsdp_count, up_part, width)], axis=1
+    )
+    inner_mlp = InnerSum(mlp_parts)
+    base, gain_one, keep_tok, send_tok = pl.pallas_call(
+        functools.partial(fifth_kernel, (dp_count, blocks, places_one, qkv_rows)),
         out_shape=(
             whole((row_count, width), f32),
-            whole((pairs, qkv_rows + 16, width), bf16),
-            whole((pairs, qkv_rows + 16, width), bf16),
+            whole((8, width), f32),
             whole((pairs, row_count, width), bf16),
             whole((pairs, row_count, width), bf16),
         ),
-        in_specs=[SMEM, SMEM] + [VMEM] * 7 + [ANY] * len(arrays_one),
-        out_specs=(VMEM,) + (ANY,) * 4,
+        in_specs=[SMEM, SMEM] + [VMEM] * 4 + [ANY] * len(arrays_one),
+        out_specs=(VMEM,) * 2 + (ANY,) * 2,
         scratch_shapes=[
             pltpu.VMEM((3 * width, width), bf16),
-            pltpu.VMEM((3 * width, width), bf16),
-            pltpu.VMEM((row_count, 3 * width), bf16),
-            pltpu.VMEM((row_count, width), f32),
-            pltpu.VMEM((row_count, width), f32),
             pltpu.VMEM((dp_count * blocks, CLIP, width), bf16),
-            pltpu.VMEM((16, width), bf16),
-            pltpu.SemaphoreType.DMA((len(arrays_one) + 2 * dp_count + dp_count * blocks,)),
+            pltpu.SemaphoreType.DMA((len(arrays_one) + dp_count * blocks,)),
         ],
         compiler_params=params(),
-        cost_estimate=cost(2e9 * 12, 30e6),
-        name="self_attention_backward",
-    )(ints, mix_weight, seg_row, gains, gain_grads, blended, grad_res, grad_att, qkv, *arrays_one)
-
-    mlp_sum = outer_sum(jnp.stack([where[g] for g in range(pairs)]), cut_mlp)
-    mlp_parts = jnp.concatenate(
-        [mlp_sum[:up_rows].reshape(fsdp_count, up_part, width), mlp_sum[up_rows:].reshape(fsdp_count, up_part, width)], axis=1
-    )
-    mlp_mine = inner_sum(mlp_parts)
-    up_shard, down_shard = mlp_mine[:up_part].T, mlp_mine[up_part:]
-
-    two_sum = outer_sum(add_low(keep_two, swap(send_two, CORE)), cut_two)
+        cost_estimate=cost(1e9, 1e6),
+        name="self_attention_input",
+    )(ints, mix_weight, gains, blended, grad_res, grad_proj, *arrays_one)
+    came_two, keep_tok, send_tok, gain_one = fence((came_two, keep_tok, send_tok, gain_one))
+
+    sum_two = OuterSum(add_low(keep_two, came_two), cut_two)
+    sum_two.relays()
+    came_tok = swap(send_tok, CORE)
+    keep_one, send_one = pl.pallas_call(
+        functools.partial(sixth_kernel, (dp_count, qkv_rows)),
+        out_shape=(
+            whole((pairs, qkv_rows + 16, width), bf16),
+            whole((pairs, qkv_rows + 16, width), bf16),
+        ),
+        in_specs=[SMEM] + [VMEM] * 5,
+        out_specs=(ANY,) * 2,
+        scratch_shapes=[
+            pltpu.VMEM((3 * width, width), bf16),
+            pltpu.VMEM((16, width), bf16),
+            pltpu.SemaphoreType.DMA((2 * dp_count,)),
+        ],
+        compiler_params=params(),
+        cost_estimate=cost(1e9, 1e6),
+        name="self_attention_weights",
+    )(ints, gains, gain_grads, gain_one, blended, grad_proj)
+    state, came_tok, keep_one, send_one, mlp_came = fence((sum_two.state(), came_tok, keep_one, send_one, inner_mlp.came))
+    sum_two.put(state)
+    inner_mlp.came = mlp_came
+
+    sum_two.singles()
+    came_one = swap(send_one, CORE)
+    total_tok = add_low(keep_tok, came_tok)
+    state, came_one, total_tok = fence((sum_two.state(), came_one, total_tok))
+    sum_two.put(state)
+
+    sum_one, sum_tok = OuterSum(add_low(keep_one, came_one), cut_one), OuterSum(total_tok, cut_tok)
+    sum_one.relays()
+    sum_tok.relays()
+    two_sum = sum_two.result()
     two_parts = jnp.concatenate(
         [two_sum[first : first + size].reshape(fsdp_count, size // fsdp_count, width) for first, size in layout], axis=1
     )
-    two_mine = inner_sum(two_parts)
+    inner_two = InnerSum(two_parts)
+    state, state_tok, two_came = fence((sum_one.state(), sum_tok.state(), inner_two.came))
+    sum_one.put(state)
+    sum_tok.put(state_tok)
+    inner_two.came = two_came
+
+    sum_one.singles()
+    state = fence(sum_one.state())
+    sum_one.put(state)
+    sum_tok.singles()
+    one_sum = sum_one.result()
+    gain_sum = jnp.broadcast_to(one_sum[qkv_rows : qkv_rows + 8][None], (fsdp_count, 8, width))
+    one_parts = jnp.concatenate([one_sum[:qkv_rows].reshape(fsdp_count, qkv_part, width), gain_sum], axis=1)
+    one_mine = InnerSum(one_parts).result()
+
+    mlp_mine = inner_mlp.result()
+    up_shard, down_shard = mlp_mine[:up_part].T, mlp_mine[up_part:]
+    two_mine = inner_two.result()
     found = []
     at = 0
     for size in sizes_two:
         found.append(two_mine[at : at + size])
         at += size
     ckv_shard, out_shard, cq_shard, cout_shard = found[0].T, found[1], found[2], found[3]
-
-    one_sum = outer_sum(add_low(keep_one, swap(send_one, CORE)), cut_one)
-    gain_sum = jnp.broadcast_to(one_sum[qkv_rows : qkv_rows + 8][None], (fsdp_count, 8, width))
-    one_parts = jnp.concatenate([one_sum[:qkv_rows].reshape(fsdp_count, qkv_part, width), gain_sum], axis=1)
-    one_mine = inner_sum(one_parts)
     qkv_shard = one_mine[:qkv_part].T
     gain_mine = lax.dynamic_slice(one_mine[qkv_part:], (0, device_me * part), (3, part))
-
-    token_grad = base + outer_sum(add_low(keep_tok, swap(send_tok, CORE)), cut_tok)
+    token_grad = base + sum_tok.result()
     return (
         output,
         token_grad,

time: 425 us -> 378 us (0.89)
  the two profiles are of different devices: /device:TPU:28 before, /device:TPU:0 now
where the time goes in v3:
time: 378 us; the launch traced here: 372 us
  waiting for transfers between devices  127 us (34%)
  Pallas kernels  118 us (31%)
  starting transfers between devices  76.4 us (20%)
  local copies, waits for them, and re-layouts  25.8 us (7%)
  other arithmetic  23.1 us (6%)
    ppermute x58, waiting for transfers between devices, swap(): return lax.ppermute(values, 'dp', [(i, i ^ mask) for i in range(count)])  73.1 us
    ppermute x58, starting transfers between devices, swap(): return lax.ppermute(values, 'dp', [(i, i ^ mask) for i in range(count)])  42.5 us
    ppermute x15, waiting for transfers between devices, shift(): lax.ppermute(values, 'fsdp', [(i, (i + step) % count) for i in range(coun...  39.6 us
    pallas_call x3, Pallas kernels, mlp_call(): pl.pallas_call(functools.partial(mlp_kernel, (groups, tuple(places), up_r...  32.9 us
    ppermute x15, starting transfers between devices, shift(): lax.ppermute(values, 'fsdp', [(i, (i + step) % count) for i in range(coun...  27.8 us
    pallas_call x1, Pallas kernels, shards(): pl.pallas_call(functools.partial(fourth_kernel, (blocks,)), out_shape=(wh...  19.2 us
    ppermute x2, waiting for transfers between devices, inner_gather(): came = lax.ppermute(held, 'fsdp', [(i, i ^ mask) for i in range(count)])  14.2 us
    pallas_call x1, Pallas kernels, shards(): pl.pallas_call(functools.partial(third_kernel, (blocks, places_two, layou...  13.8 us
  transfers between devices with their start and end apart: 75, of which 29 were waited for; matrix products, arithmetic and copies ran while one was open for 9% of the time, Pallas kernels for 32%

profile of v3, /device:TPU:0, one launch (start us, length us, event | category | flops | bytes accessed | tf_op | source)
XLA Modules:
  0.0 372.3 jit_solution(11330543639847146692)
XLA Ops:
  35.4 5.4 %collective-permute-done.8 = bf16[120,768]{1,0:T(8,128)(2,1)S(1)} collective-permute-done((bf16[120,768]{1,0:T(8,128)(2,1)S(1)}, bf16[120,768]{1,0:T(8,128)(2,1)S(1)}, u32[]{:S(2)}, u32[]{:S(2)}) %collective-permute-start.8) | collective-permute-done | bytes 184352 | tf_op jit(solution)/shard_map/ppermute | solution.py:30
  44.8 9.4 %collective-permute-done.13.refs_6_ = bf16[256,768]{1,0:T(8,128)(2,1)} collective-permute-done((bf16[256,768]{1,0:T(8,128)(2,1)S(1)}, bf16[256,768]{1,0:T(8,128)(2,1)}, u32[]{:S(2)}, u32[]{:S(2)}) %collective-permute-start.13) | collective-permute-done | bytes 393248 | tf_op jit(solution)/shard_map/ppermute | solution.py:25
  63.0 4.4 %collective-permute-start.31 = (bf16[1,192,768]{2,1,0:T(8,128)(2,1)S(1)}, bf16[1,192,768]{2,1,0:T(8,128)(2,1)}, u32[]{:S(2)}, u32[]{:S(2)}) collective-permute-start(bf16[1,192,768]{2,1,0:T(8,128)(2,1)S(1)} %bitcast.170), channel_id=1, source_target_pairs={{0,1},{1,0},{2,3},{3,2},{4,5},{5,4},{6,7},{7,6},{8,9},{9,8},{10,11... | collective-permute-start | bytes 884744 | tf_op jit(solution)/shard_map/ppermute | solution.py:56
  70.0 4.7 %collective-permute-done.31 = bf16[1,192,768]{2,1,0:T(8,128)(2,1)} collective-permute-done((bf16[1,192,768]{2,1,0:T(8,128)(2,1)S(1)}, bf16[1,192,768]{2,1,0:T(8,128)(2,1)}, u32[]{:S(2)}, u32[]{:S(2)}) %collective-permute-start.31) | collective-permute-done | bytes 294944 | tf_op jit(solution)/shard_map/ppermute | solution.py:56
  81.5 12.8 %mix_self_attention.1 = (f32[512,768]{1,0:T(8,128)}, bf16[512,2304]{1,0:T(8,128)(2,1)}, bf16[512,768]{1,0:T(8,128)(2,1)}, f32[8,768]{1,0:T(8,128)}) custom-call(s32[17]{0:T(128)} %concatenate.68.ints, f32[4]{0:T(128)} %mix.3, s32[1,512]{1,0:T(1,128)} %seg_row.3, bf16[512,768]{1,0:T(8,128)(2,1)} %refs_0_, bf16[512,768]{1,0:T(8,128)(2,1)} %refs_0_, ...), custom_call_target="tpu_custom_call" | custom-call | flops 1000000000 | bytes 1000000 | tf_op jit(solution)/shard_map/mix_self_attention/pallas_call | solution.py:703
  96.8 9.5 %collective-permute-done.32 = bf16[2,192,768]{2,1,0:T(8,128)(2,1)} collective-permute-done((bf16[2,192,768]{2,1,0:T(8,128)(2,1)}, bf16[2,192,768]{2,1,0:T(8,128)(2,1)}, u32[]{:S(2)}, u32[]{:S(2)}) %collective-permute-start.32) | collective-permute-done | bytes 589856 | tf_op jit(solution)/shard_map/ppermute | solution.py:56
  109.2 5.2 %collective-permute-done.26.refs_6_ = bf16[192,768]{1,0:T(8,128)(2,1)} collective-permute-done((bf16[192,768]{1,0:T(8,128)(2,1)S(1)}, bf16[192,768]{1,0:T(8,128)(2,1)}, u32[]{:S(2)}, u32[]{:S(2)}) %collective-permute-start.26) | collective-permute-done | bytes 294944 | tf_op jit(solution)/shard_map/ppermute | solution.py:25
  120.9 11.1 %cross_attention.1 = (f32[512,768]{1,0:T(8,128)}, bf16[512,768]{1,0:T(8,128)(2,1)}, bf16[128,1536]{1,0:T(8,128)(2,1)}, bf16[512,768]{1,0:T(8,128)(2,1)}, f32[512,768]{1,0:T(8,128)}, /*index=5*/bf16[512,768]{1,0:T(8,128)(2,1)}) custom-call(s32[17]{0:T(128)} %concatenate.68.ints, s32[1,128]{1,0:T(1,128)} %bitcast.180, bf16[128,768]{1,0:T(8,128)(2,1)} %coarse.3, ...), custom_call_target="tpu_custom_call" | custom-call | flops 1000000000 | bytes 1000000 | tf_op jit(solution)/shard_map/cross_attention/pallas_call | solution.py:740
  132.0 9.4 %collective-permute-done.33.refs_2_ = bf16[768,768]{1,0:T(8,128)(2,1)} collective-permute-done((bf16[768,768]{1,0:T(8,128)(2,1)S(1)}, bf16[768,768]{1,0:T(8,128)(2,1)}, u32[]{:S(2)}, u32[]{:S(2)}) %collective-permute-start.33) | collective-permute-done | bytes 1179680 | tf_op jit(solution)/shard_map/ppermute | solution.py:25
  149.4 13.2 %feed_forward.3 = (bf16[2,2,384,768]{3,2,1,0:T(8,128)(2,1)}, bf16[2,2,384,768]{3,2,1,0:T(8,128)(2,1)}, f32[512,768]{1,0:T(8,128)}, f32[512,768]{1,0:T(8,128)}) custom-call(bf16[512,768]{1,0:T(8,128)(2,1)} %get-tuple-element.254.second, bf16[512,768]{1,0:T(8,128)(2,1)} %cotangent.7, bf16[768,768]{1,0:T(8,128)(2,1)} %copy-done.5, bf16[768,768]{1,0:T(8,128)(2,1)} %copy-done.29, ...), custom_call_target="tpu_custom_call" | custom-call | flops 1000000000 | bytes 1000000 | tf_op jit(solution)/shard_map/feed_forward/pallas_call | solution.py:780
  163.8 9.8 %feed_forward.4 = (bf16[1,2,384,768]{3,2,1,0:T(8,128)(2,1)}, bf16[1,2,384,768]{3,2,1,0:T(8,128)(2,1)}, f32[512,768]{1,0:T(8,128)}, f32[512,768]{1,0:T(8,128)}) custom-call(bf16[512,768]{1,0:T(8,128)(2,1)} %get-tuple-element.254.second, bf16[512,768]{1,0:T(8,128)(2,1)} %cotangent.7, bf16[768,768]{1,0:T(8,128)(2,1)} %collective-permute-done.34.refs_0_, ...), custom_call_target="tpu_custom_call" | custom-call | flops 1000000000 | bytes 1000000 | tf_op jit(solution)/shard_map/feed_forward/pallas_call | solution.py:780
  174.6 9.8 %feed_forward.5 = (bf16[1,2,384,768]{3,2,1,0:T(8,128)(2,1)}, bf16[1,2,384,768]{3,2,1,0:T(8,128)(2,1)}, f32[512,768]{1,0:T(8,128)}, f32[512,768]{1,0:T(8,128)}) custom-call(bf16[512,768]{1,0:T(8,128)(2,1)} %get-tuple-element.254.second, bf16[512,768]{1,0:T(8,128)(2,1)} %cotangent.7, bf16[384,768]{1,0:T(8,128)(2,1)} %copy-done.35, ...), custom_call_target="tpu_custom_call" | custom-call | flops 1000000000 | bytes 1000000 | tf_op jit(solution)/shard_map/feed_forward/pallas_call | solution.py:780
  189.9 13.8 %cross_attention_backward.1 = (bf16[512,768]{1,0:T(8,128)(2,1)}, f32[512,768]{1,0:T(8,128)}, bf16[512,768]{1,0:T(8,128)(2,1)}, bf16[128,1536]{1,0:T(8,128)(2,1)}...) custom-call(s32[17]{0:T(128)} %concatenate.68.ints, s32[1,128]{1,0:T(1,128)} %bitcast.181, ...), custom_call_target="tpu_custom_call" | custom-call | flops 1000000000 | bytes 1000000 | tf_op jit(solution)/shard_map/cross_attention_backward/pallas_call | solution.py:828
  207.1 10.3 %cross_attention_weights.1 = (f32[128,768]{1,0:T(8,128)}, f32[512,768]{1,0:T(8,128)}, bf16[512,768]{1,0:T(8,128)(2,1)}, f32[8,768]{1,0:T(8,128)}, bf16[4,480,768...) custom-call(s32[17]{0:T(128)} %concatenate.68.ints, ...), custom_call_target="tpu_custom_call", output_to_operand_aliasing={{4}: (9, {}), {5}: (10, {})} | custom-call | flops 1000000000 | bytes 1000000 | tf_op jit(solution)/shard_map/cross_attention_weights/pallas_call | solution.py:855
  217.4 19.2 %self_attention_backward.1.grad_proj = bf16[512,2304]{1,0:T(8,128)(2,1)} custom-call(s32[17]{0:T(128)} %concatenate.68.ints, s32[1,512]{1,0:T(1,128)} %seg_row.3, bf16[512,768]{1,0:T(8,128)(2,1)} %get-tuple-element.313.grad_att, bf16[512,2304]{1,0:T(8,128)(2,1)} %get-tuple-element.314.qkv), custom_call_target="tpu_custom_call" | custom-call | flops 1000000000 | bytes 1000000 | tf_op jit(solution)/shard_map/self_attention_backward/pallas_call | solution.py:885
  236.7 11.4 %self_attention_input.1 = (f32[512,768]{1,0:T(8,128)}, f32[8,768]{1,0:T(8,128)}, bf16[4,512,768]{2,1,0:T(8,128)(2,1)}, bf16[4,512,768]{2,1,0:T(8,128)(2,1)}) custom-call(s32[17]{0:T(128)} %concatenate.68.ints, f32[4]{0:T(128)} %mix.3, f32[8,768]{1,0:T(8,128)} %get-tuple-element.232.gains, f32[512,768]{1,0:T(8,128)} %get-tuple-element.240.blended, ...), custom_call_target="tpu_custom_call" | custom-call | flops 1000000000 | bytes 1000000 | tf_op jit(solution)/shard_map/self_attention_input/pallas_call | solution.py:904
  260.7 6.5 %self_attention_weights.1 = (bf16[4,304,768]{2,1,0:T(8,128)(2,1)}, bf16[4,304,768]{2,1,0:T(8,128)(2,1)}) custom-call(s32[17]{0:T(128)} %concatenate.68.ints, f32[8,768]{1,0:T(8,128)} %get-tuple-element.232.gains, f32[8,768]{1,0:T(8,128)} %get-tuple-element.326.gain_grads, f32[8,768]{1,0:T(8,128)} %get-tuple-element.327.gain_one, ...), custom_call_target="tpu_custom_call" | custom-call | flops 1000000000 | bytes 1000000 | tf_op jit(solution)/shard_map/self_attention_weights/pallas_call | solution.py:928
  269.8 5.5 %collective-permute-done.56 = bf16[192,768]{1,0:T(8,128)(2,1)S(1)} collective-permute-done((bf16[192,768]{1,0:T(8,128)(2,1)S(1)}, bf16[192,768]{1,0:T(8,128)(2,1)S(1)}, u32[]{:S(2)}, u32[]{:S(2)}) %collective-permute-start.56) | collective-permute-done | bytes 294944 | tf_op jit(solution)/shard_map/ppermute | solution.py:30
  286.4 11.9 %collective-permute-done.58 = bf16[480,768]{1,0:T(8,128)(2,1)S(1)} collective-permute-done((bf16[480,768]{1,0:T(8,128)(2,1)S(1)}, bf16[480,768]{1,0:T(8,128)(2,1)S(1)}, u32[]{:S(2)}, u32[]{:S(2)}) %collective-permute-start.58) | collective-permute-done | bytes 737312 | tf_op jit(solution)/shard_map/ppermute | solution.py:25
  305.2 6.0 %collective-permute-start.65 = (bf16[120,768]{1,0:T(8,128)(2,1)S(1)}, bf16[120,768]{1,0:T(8,128)(2,1)S(1)}, u32[]{:S(2)}, u32[]{:S(2)}) collective-permute-start(bf16[120,768]{1,0:T(8,128)(2,1)S(1)} %get-tuple-element.399), channel_id=1, source_target_pairs={{0,1},{1,2},{2,3},{3,0},{4,5},{5,6},{6,7},{7,4},{8,9},{9,10},{10,1... | collective-permute-start | bytes 552968 | tf_op jit(solution)/shard_map/ppermute | solution.py:30
  311.3 4.4 %collective-permute-done.65 = bf16[120,768]{1,0:T(8,128)(2,1)S(1)} collective-permute-done((bf16[120,768]{1,0:T(8,128)(2,1)S(1)}, bf16[120,768]{1,0:T(8,128)(2,1)S(1)}, u32[]{:S(2)}, u32[]{:S(2)}) %collective-permute-start.65) | collective-permute-done | bytes 184352 | tf_op jit(solution)/shard_map/ppermute | solution.py:30
  316.9 4.7 %collective-permute-done.66 = bf16[120,768]{1,0:T(8,128)(2,1)S(1)} collective-permute-done((bf16[120,768]{1,0:T(8,128)(2,1)S(1)}, bf16[120,768]{1,0:T(8,128)(2,1)S(1)}, u32[]{:S(2)}, u32[]{:S(2)}) %collective-permute-start.66) | collective-permute-done | bytes 184352 | tf_op jit(solution)/shard_map/ppermute | solution.py:30
  333.9 24.0 %collective-permute-done.70 = bf16[304,768]{1,0:T(8,128)(2,1)S(1)} collective-permute-done((bf16[304,768]{1,0:T(8,128)(2,1)S(1)}, bf16[304,768]{1,0:T(8,128)(2,1)S(1)}, u32[]{:S(2)}, u32[]{:S(2)}) %collective-permute-start.70) | collective-permute-done | bytes 466976 | tf_op jit(solution)/shard_map/ppermute | solution.py:25
  363.4 5.8 %collective-permute-done.73 = bf16[80,768]{1,0:T(8,128)(2,1)S(1)} collective-permute-done((bf16[80,768]{1,0:T(8,128)(2,1)S(1)}, bf16[80,768]{1,0:T(8,128)(2,1)S(1)}, u32[]{:S(2)}, u32[]{:S(2)}) %collective-permute-start.73) | collective-permute-done | bytes 122912 | tf_op jit(solution)/shard_map/ppermute | solution.py:30
  (356 shorter events, 142.0 us)
Async XLA Ops:
  0.6 20.8 %collective-permute-start = (bf16[512,768]{1,0:T(8,128)(2,1)}, bf16[512,768]{1,0:T(8,128)(2,1)S(1)}, u32[]{:S(2)}, u32[]{:S(2)}) collective-permute-start(bf16[512,768]{1,0:T(8,128)(2,1)} %refs_0_), channel_id=1, source_target_pairs={{0,8},{4,12},{8,0},{12,4},{16,24},{20,28},{24,16},{28,20},{1,9},{5... | collective-permute-start | bytes 2359304 | tf_op jit(solution)/shard_map/ppermute | solution.py:25
  3.6 19.2 %collective-permute-start.1 = (bf16[512,768]{1,0:T(8,128)(2,1)}, bf16[512,768]{1,0:T(8,128)(2,1)S(1)}, u32[]{:S(2)}, u32[]{:S(2)}) collective-permute-start(bf16[512,768]{1,0:T(8,128)(2,1)} %refs_0_), channel_id=1, source_target_pairs={{0,16},{4,20},{8,24},{12,28},{16,0},{20,4},{24,8},{28,12},{1,17},{... | collective-permute-start | bytes 2359304 | tf_op jit(solution)/shard_map/ppermute | solution.py:25
  67.4 26.9 %collective-permute-start.24 = (bf16[480,768]{1,0:T(8,128)(2,1)S(1)}, bf16[480,768]{1,0:T(8,128)(2,1)S(1)}, u32[]{:S(2)}, u32[]{:S(2)}) collective-permute-start(bf16[480,768]{1,0:T(8,128)(2,1)S(1)} %pad_maximum_fusion.9.refs_0_), channel_id=1, source_target_pairs={{0,8},{4,12},{8,0},{12,4},{16,24},{20,28},{24,16},{28,20},{1,9},{5... | collective-permute-start | bytes 2211848 | tf_op jit(solution)/shard_map/ppermute | solution.py:25
  68.4 26.0 %collective-permute-start.25 = (bf16[480,768]{1,0:T(8,128)(2,1)S(1)}, bf16[480,768]{1,0:T(8,128)(2,1)S(1)}, u32[]{:S(2)}, u32[]{:S(2)}) collective-permute-start(bf16[480,768]{1,0:T(8,128)(2,1)S(1)} %pad_maximum_fusion.9.refs_0_), channel_id=1, source_target_pairs={{0,16},{4,20},{8,24},{12,28},{16,0},{20,4},{24,8},{28,12},{1,17},{... | collective-permute-start | bytes 2211848 | tf_op jit(solution)/shard_map/ppermute | solution.py:25
  77.3 29.0 %collective-permute-start.32 = (bf16[2,192,768]{2,1,0:T(8,128)(2,1)}, bf16[2,192,768]{2,1,0:T(8,128)(2,1)}, u32[]{:S(2)}, u32[]{:S(2)}) collective-permute-start(bf16[2,192,768]{2,1,0:T(8,128)(2,1)} %pad_maximum_fusion.12), channel_id=1, source_target_pairs={{0,2},{1,3},{2,0},{3,1},{4,6},{5,7},{6,4},{7,5},{8,10},{9,11},{10,... | collective-permute-start | bytes 1769480 | tf_op jit(solution)/shard_map/ppermute | solution.py:56
  94.4 20.0 %collective-permute-start.28 = (bf16[480,768]{1,0:T(8,128)(2,1)S(1)}, bf16[480,768]{1,0:T(8,128)(2,1)S(1)}, u32[]{:S(2)}, u32[]{:S(2)}) collective-permute-start(bf16[480,768]{1,0:T(8,128)(2,1)S(1)} %pad_maximum_fusion.9.refs_0_), channel_id=1, source_target_pairs={{0,4},{4,0},{8,12},{12,8},{16,20},{20,16},{24,28},{28,24},{1,5},{5... | collective-permute-start | bytes 2211848 | tf_op jit(solution)/shard_map/ppermute | solution.py:25
  94.6 19.8 %collective-permute-start.29 = (bf16[480,768]{1,0:T(8,128)(2,1)S(1)}, bf16[480,768]{1,0:T(8,128)(2,1)}, u32[]{:S(2)}, u32[]{:S(2)}) collective-permute-start(bf16[480,768]{1,0:T(8,128)(2,1)S(1)} %collective-permute-done.24.refs_2_), channel_id=1, source_target_pairs={{0,4},{4,0},{8,12},{12,8},{16,20},{20,16},{24,28},{28,24},{1,5},{5... | collective-permute-start | bytes 2211848 | tf_op jit(solution)/shard_map/ppermute | solution.py:25
  95.0 19.4 %collective-permute-start.30 = (bf16[480,768]{1,0:T(8,128)(2,1)S(1)}, bf16[480,768]{1,0:T(8,128)(2,1)}, u32[]{:S(2)}, u32[]{:S(2)}) collective-permute-start(bf16[480,768]{1,0:T(8,128)(2,1)S(1)} %collective-permute-done.25.refs_4_), channel_id=1, source_target_pairs={{0,4},{4,0},{8,12},{12,8},{16,20},{20,16},{24,28},{28,24},{1,5},{5... | collective-permute-start | bytes 2211848 | tf_op jit(solution)/shard_map/ppermute | solution.py:25
  115.3 26.1 %collective-permute-start.33 = (bf16[768,768]{1,0:T(8,128)(2,1)S(1)}, bf16[768,768]{1,0:T(8,128)(2,1)}, u32[]{:S(2)}, u32[]{:S(2)}) collective-permute-start(bf16[768,768]{1,0:T(8,128)(2,1)S(1)} %pad_maximum_fusion.4.refs_0_), channel_id=1, source_target_pairs={{0,8},{4,12},{8,0},{12,4},{16,24},{20,28},{24,16},{28,20},{1,9},{5... | collective-permute-start | bytes 3538952 | tf_op jit(solution)/shard_map/ppermute | solution.py:25
  116.2 25.8 %collective-permute-start.34 = (bf16[768,768]{1,0:T(8,128)(2,1)S(1)}, bf16[768,768]{1,0:T(8,128)(2,1)}, u32[]{:S(2)}, u32[]{:S(2)}) collective-permute-start(bf16[768,768]{1,0:T(8,128)(2,1)S(1)} %pad_maximum_fusion.4.refs_0_), channel_id=1, source_target_pairs={{0,16},{4,20},{8,24},{12,28},{16,0},{20,4},{24,8},{28,12},{1,17},{... | collective-permute-start | bytes 3538952 | tf_op jit(solution)/shard_map/ppermute | solution.py:25
  142.5 20.2 %collective-permute-start.39 = (bf16[768,768]{1,0:T(8,128)(2,1)}, bf16[768,768]{1,0:T(8,128)(2,1)S(1)}, u32[]{:S(2)}, u32[]{:S(2)}) collective-permute-start(bf16[768,768]{1,0:T(8,128)(2,1)} %collective-permute-done.34.refs_0_), channel_id=1, source_target_pairs={{0,4},{4,0},{8,12},{12,8},{16,20},{20,16},{24,28},{28,24},{1,5},{5... | collective-permute-start | bytes 3538952 | tf_op jit(solution)/shard_map/ppermute | solution.py:25
  204.4 32.2 %collective-permute-start.49 = (bf16[768,768]{1,0:T(8,128)(2,1)S(1)}, bf16[768,768]{1,0:T(8,128)(2,1)S(1)}, u32[]{:S(2)}, u32[]{:S(2)}) collective-permute-start(bf16[768,768]{1,0:T(8,128)(2,1)S(1)} %pad_maximum_fusion.5), channel_id=1, source_target_pairs={{0,8},{4,12},{8,0},{12,4},{16,24},{20,28},{24,16},{28,20},{1,9},{5... | collective-permute-start | bytes 3538952 | tf_op jit(solution)/shard_map/ppermute | solution.py:25
  205.8 30.8 %collective-permute-start.50 = (bf16[768,768]{1,0:T(8,128)(2,1)S(1)}, bf16[768,768]{1,0:T(8,128)(2,1)}, u32[]{:S(2)}, u32[]{:S(2)}) collective-permute-start(bf16[768,768]{1,0:T(8,128)(2,1)S(1)} %pad_maximum_fusion.6), channel_id=1, source_target_pairs={{0,16},{4,20},{8,24},{12,28},{16,0},{20,4},{24,8},{28,12},{1,17},{... | collective-permute-start | bytes 3538952 | tf_op jit(solution)/shard_map/ppermute | solution.py:25
  248.1 28.2 %collective-permute-start.54 = (bf16[4,512,768]{2,1,0:T(8,128)(2,1)}, bf16[4,512,768]{2,1,0:T(8,128)(2,1)}, u32[]{:S(2)}, u32[]{:S(2)}) collective-permute-start(bf16[4,512,768]{2,1,0:T(8,128)(2,1)} %get-tuple-element.325), channel_id=1, source_target_pairs={{0,4},{4,0},{8,12},{12,8},{16,20},{20,16},{24,28},{28,24},{1,5},{5... | collective-permute-start | bytes 9437192 | tf_op jit(solution)/shard_map/ppermute | solution.py:25
  252.5 22.8 %collective-permute-start.56 = (bf16[192,768]{1,0:T(8,128)(2,1)S(1)}, bf16[192,768]{1,0:T(8,128)(2,1)S(1)}, u32[]{:S(2)}, u32[]{:S(2)}) collective-permute-start(bf16[192,768]{1,0:T(8,128)(2,1)S(1)} %get-tuple-element.389), channel_id=1, source_target_pairs={{0,2},{1,3},{2,0},{3,1},{4,6},{5,7},{6,4},{7,5},{8,10},{9,11},{10,... | collective-permute-start | bytes 884744 | tf_op jit(solution)/shard_map/ppermute | solution.py:30
  255.9 19.4 %collective-permute-start.57 = (bf16[192,768]{1,0:T(8,128)(2,1)S(1)}, bf16[192,768]{1,0:T(8,128)(2,1)S(1)}, u32[]{:S(2)}, u32[]{:S(2)}) collective-permute-start(bf16[192,768]{1,0:T(8,128)(2,1)S(1)} %get-tuple-element.388), channel_id=1, source_target_pairs={{0,3},{1,0},{2,1},{3,2},{4,7},{5,4},{6,5},{7,6},{8,11},{9,8},{10,9... | collective-permute-start | bytes 884744 | tf_op jit(solution)/shard_map/ppermute | solution.py:30
  277.0 22.2 %collective-permute-start.60 = (bf16[4,304,768]{2,1,0:T(8,128)(2,1)}, bf16[4,304,768]{2,1,0:T(8,128)(2,1)}, u32[]{:S(2)}, u32[]{:S(2)}) collective-permute-start(bf16[4,304,768]{2,1,0:T(8,128)(2,1)} %get-tuple-element.339), channel_id=1, source_target_pairs={{0,4},{4,0},{8,12},{12,8},{16,20},{20,16},{24,28},{28,24},{1,5},{5... | collective-permute-start | bytes 5603336 | tf_op jit(solution)/shard_map/ppermute | solution.py:25
  301.7 26.5 %collective-permute-start.61 = (bf16[144,768]{1,0:T(8,128)(2,1)S(1)}, bf16[144,768]{1,0:T(8,128)(2,1)S(1)}, u32[]{:S(2)}, u32[]{:S(2)}) collective-permute-start(bf16[144,768]{1,0:T(8,128)(2,1)S(1)} %slice_bitcast_fusion.18), channel_id=1, source_target_pairs={{0,16},{4,20},{8,24},{12,28},{16,0},{20,4},{24,8},{28,12},{1,17},{... | collective-permute-start | bytes 663560 | tf_op jit(solution)/shard_map/ppermute | solution.py:25
  302.5 25.6 %collective-permute-start.62 = (bf16[160,768]{1,0:T(8,128)(2,1)S(1)}, bf16[160,768]{1,0:T(8,128)(2,1)S(1)}, u32[]{:S(2)}, u32[]{:S(2)}) collective-permute-start(bf16[160,768]{1,0:T(8,128)(2,1)S(1)} %slice_bitcast_fusion.16), channel_id=1, source_target_pairs={{0,8},{4,12},{8,0},{12,4},{16,24},{20,28},{24,16},{28,20},{1,9},{5... | collective-permute-start | bytes 737288 | tf_op jit(solution)/shard_map/ppermute | solution.py:25
  303.5 24.6 %collective-permute-start.63 = (bf16[256,768]{1,0:T(8,128)(2,1)S(1)}, bf16[256,768]{1,0:T(8,128)(2,1)S(1)}, u32[]{:S(2)}, u32[]{:S(2)}) collective-permute-start(bf16[256,768]{1,0:T(8,128)(2,1)S(1)} %get-tuple-element.368), channel_id=1, source_target_pairs={{0,16},{4,20},{8,24},{12,28},{16,0},{20,4},{24,8},{28,12},{1,17},{... | collective-permute-start | bytes 1179656 | tf_op jit(solution)/shard_map/ppermute | solution.py:25
  328.4 42.1 %collective-permute-start.69 = (bf16[512,768]{1,0:T(8,128)(2,1)S(1)}, bf16[512,768]{1,0:T(8,128)(2,1)S(1)}, u32[]{:S(2)}, u32[]{:S(2)}) collective-permute-start(bf16[512,768]{1,0:T(8,128)(2,1)S(1)} %pad_maximum_fusion.8), channel_id=1, source_target_pairs={{0,16},{4,20},{8,24},{12,28},{16,0},{20,4},{24,8},{28,12},{1,17},{... | collective-permute-start | bytes 2359304 | tf_op jit(solution)/shard_map/ppermute | solution.py:25
  329.5 41.1 %collective-permute-start.68 = (bf16[512,768]{1,0:T(8,128)(2,1)S(1)}, bf16[512,768]{1,0:T(8,128)(2,1)S(1)}, u32[]{:S(2)}, u32[]{:S(2)}) collective-permute-start(bf16[512,768]{1,0:T(8,128)(2,1)S(1)} %pad_maximum_fusion.7), channel_id=1, source_target_pairs={{0,8},{4,12},{8,0},{12,4},{16,24},{20,28},{24,16},{28,20},{1,9},{5... | collective-permute-start | bytes 2359304 | tf_op jit(solution)/shard_map/ppermute | solution.py:25
  330.6 27.3 %collective-permute-start.70 = (bf16[304,768]{1,0:T(8,128)(2,1)S(1)}, bf16[304,768]{1,0:T(8,128)(2,1)S(1)}, u32[]{:S(2)}, u32[]{:S(2)}) collective-permute-start(bf16[304,768]{1,0:T(8,128)(2,1)S(1)} %pad_maximum_fusion.14), channel_id=1, source_target_pairs={{0,8},{4,12},{8,0},{12,4},{16,24},{20,28},{24,16},{28,20},{1,9},{5... | collective-permute-start | bytes 1400840 | tf_op jit(solution)/shard_map/ppermute | solution.py:25
  331.9 26.0 %collective-permute-start.71 = (bf16[304,768]{1,0:T(8,128)(2,1)S(1)}, bf16[304,768]{1,0:T(8,128)(2,1)S(1)}, u32[]{:S(2)}, u32[]{:S(2)}) collective-permute-start(bf16[304,768]{1,0:T(8,128)(2,1)S(1)} %pad_maximum_fusion.15), channel_id=1, source_target_pairs={{0,16},{4,20},{8,24},{12,28},{16,0},{20,4},{24,8},{28,12},{1,17},{... | collective-permute-start | bytes 1400840 | tf_op jit(solution)/shard_map/ppermute | solution.py:25
  (101 other events, 975.7 us)

commit v4 on v3

--- a/solution.py
+++ b/solution.py
@@ -119,6 +119,7 @@
         self.cut = cut
         self.extra = {e: {0: [], 1: []} for e in self.held}
         self.came = []
+        self.halves = [[], []]
 
     def half(self, e, which):
         part = self.held[e][: self.cut] if which == 0 else self.held[e][self.cut :]
@@ -132,21 +133,26 @@
             self.extra[e ^ low][1].append(swap(self.half(e, 1), low))
 
     def singles(self):
-        self.came = [
+        self.came += [
             swap(jnp.concatenate([self.half(mask, 0), self.half(mask, 1)]), mask) for mask in link_masks()
         ]
+
+    def singles_half(self, which):
+        self.halves[which] = [swap(self.half(mask, which), mask) for mask in link_masks()]
 
     def result(self):
         total = self.held[0].astype(f32)
         for block in self.came:
             total = total + block.astype(f32)
+        for first, second in zip(self.halves[0], self.halves[1]):
+            total = total + jnp.concatenate([first, second]).astype(f32)
         return total
 
     def state(self):
-        return (self.held, self.extra, self.came)
+        return (self.held, self.extra, self.came, self.halves)
 
     def put(self, state):
-        self.held, self.extra, self.came = state
+        self.held, self.extra, self.came, self.halves = state
 
 
 class InnerSum:
@@ -358,25 +364,32 @@
     second_ref[...] = (xhat * gains[2:3]).astype(bf16)
 
 
-def mlp_kernel(geometry, second, cotangent, *refs):
-    groups, places, rows, carried = geometry
+def mlp_kernel(geometry, second, second_near, cotangent, cotangent_near, *refs):
+    groups, places, rows, carried, last = geometry
     weight_refs = refs[: len(places)]
     refs = refs[len(places) :]
     if carried:
-        out_in, grad_in = refs[:2]
-        refs = refs[2:]
-    keep_ref, send_ref, out_ref, grad_ref, w_up, w_down, hidden, grad_pre, sems = refs
+        held = refs[:4]
+        refs = refs[4:]
+    keep_ref = refs[0]
+    if last:
+        going_ref, out_near, grad_near = refs[3:6]
+        sums = (refs[1], refs[2], out_near, grad_near)
+        refs = refs[6:]
+    else:
+        sums = refs[1:5]
+        refs = refs[5:]
+    w_up, w_down, hidden, grad_pre, sems = refs
     step = pl.program_id(0)
 
     def jobs_of(group):
         jobs = []
-        for ref, (e, which, start) in zip(weight_refs, places):
-            if e // 2 == groups[group]:
+        for ref, (e, which) in zip(weight_refs, places):
+            if e == groups[group]:
                 for part, weight in ((0, w_up), (1, w_down)):
                     if which is None or which == part:
                         first = part * rows if which is None else 0
-                        dst = weight.at[group, pl.ds((e & 1) * rows, rows)]
-                        jobs.append((ref.at[pl.ds(first, rows)], dst))
+                        jobs.append((ref.at[pl.ds(first, rows)], weight.at[group]))
         return jobs
 
     at = 0
@@ -397,28 +410,29 @@
 
     @pl.when(step == 0)
     def _():
-        if carried:
-            out_ref[...] = out_in[...]
-            grad_ref[...] = grad_in[...]
-        else:
-            out_ref[...] = jnp.zeros_like(out_ref)
-            grad_ref[...] = jnp.zeros_like(grad_ref)
+        for i, ref in enumerate(sums):
+            ref[...] = held[i][...] if carried else jnp.zeros_like(ref)
 
     up, down = w_up.at[step], w_down.at[step]
-    both = 2 * rows
-    for first, size in tiles(both):
-        pre = nt(second[...], up[first : first + size, :])
-        grad_hidden = nt(cotangent[...], down[first : first + size, :])
+    for half, (inputs, upstream) in enumerate(((second, cotangent), (second_near, cotangent_near))):
+        pre = nt(inputs[...], up[...])
+        grad_hidden = nt(upstream[...], down[...])
         cdf = 0.5 * (1.0 + lax.erf(pre * 0.7071067811865476))
         slope = cdf + pre * (jnp.exp(-0.5 * pre * pre) * 0.3989422804014327)
-        hidden[:, first : first + size] = (pre * cdf).astype(bf16)
-        grad_pre[:, first : first + size] = (grad_hidden * slope).astype(bf16)
-    for first, target in ((0, keep_ref), (rows, send_ref)):
-        target[0, 0] = tn(grad_pre[:, first : first + rows], second[...]).astype(bf16)
-        target[0, 1] = tn(hidden[:, first : first + rows], cotangent[...]).astype(bf16)
-    for first, size in tiles(second.shape[1]):
-        out_ref[:, first : first + size] += nn(hidden[...], down[:, first : first + size])
-        grad_ref[:, first : first + size] += nn(grad_pre[...], up[:, first : first + size])
+        hidden[half] = (pre * cdf).astype(bf16)
+        grad_pre[half] = (grad_hidden * slope).astype(bf16)
+        for first, size in tiles(second.shape[1]):
+            columns = slice(first, first + size)
+            sums[2 * half][:, columns] += nn(hidden[half], down[:, columns])
+            sums[2 * half + 1][:, columns] += nn(grad_pre[half], up[:, columns])
+    keep_ref[0, 0] = (tn(grad_pre[0], second[...]) + tn(grad_pre[1], second_near[...])).astype(bf16)
+    keep_ref[0, 1] = (tn(hidden[0], cotangent[...]) + tn(hidden[1], cotangent_near[...])).astype(bf16)
+    if last:
+
+        @pl.when(step == len(groups) - 1)
+        def _():
+            going_ref[0] = out_near[...].astype(bf16)
+            going_ref[1] = grad_near[...].astype(bf16)
 
 
 def grads_out(me, dp_count, layout, sources, keep_ref, send_ref, sems, at):
@@ -434,7 +448,7 @@
 
 
 def third_kernel(
-    geometry, ints, coarse_seg, gains, mlp_out, grad_second, joined, cotangent, crossed, cq, ckv, *refs
+    geometry, ints, coarse_seg, gains, mlp_out, grad_second, mlp_came, joined, cotangent, crossed, cq, ckv, *refs
 ):
     blocks, places, layout, dp_count = geometry
     weight_refs = refs[: len(places)]
@@ -444,9 +458,9 @@
     me = ints[0]
     width = joined.shape[1]
     made = load_cross(me, weight_refs, places, layout, (None, None, None, w_cout), sems)
-    output_ref[...] = (joined[...] + mlp_out[...]).astype(bf16)
+    output_ref[...] = (joined[...] + (mlp_out[...] + mlp_came[0].astype(f32))).astype(bf16)
     xhat, r = centred(joined[...])
-    grad_in, gain_two = norm_back(xhat, r, gains[2:3], grad_second[...])
+    grad_in, gain_two = norm_back(xhat, r, gains[2:3], grad_second[...] + mlp_came[1].astype(f32))
     grad_joined_ref[...] = cotangent[...].astype(f32) + grad_in
     low = grad_joined_ref[...].astype(bf16)
     for job in made:
@@ -666,7 +680,8 @@
 
     held_tok = {0: tokens, **single_steps(tokens)}
     came_one = inner_start(shard_one)
-    held_tok, came_one, shard_two = fence((held_tok, came_one, shard_two))
+    cotangent_near = swap(cotangent, CORE)
+    held_tok, came_one, shard_two, cotangent_near = fence((held_tok, came_one, shard_two, cotangent_near))
 
     ones = inner_order(came_one)
     gain_block = jnp.sum(ones[:, qkv_part:].astype(f32), axis=0).astype(bf16)
@@ -677,7 +692,7 @@
     came_two = inner_start(shard_two)
     held_tok, held_one, came_two, shard_mlp = fence((held_tok, held_one, came_two, shard_mlp))
 
-    mlp = inner_gather(shard_mlp)
+    mlp = lax.all_gather(shard_mlp, "fsdp", axis=0, tiled=False)
     core_tok = core_steps({e: b for e, b in held_tok.items()})
     relay_steps(held_tok, cut_tok)
     twos = inner_order(came_two)
@@ -754,74 +769,66 @@
         cost_estimate=cost(1e9, 1e6),
         name="cross_attention",
     )(ints, coarse_seg, coarse_view, blended, attended, gains, *arrays_two)
-    held_mlp, second = fence((held_mlp, second))
-
-    core_mlp = core_steps(dict(held_mlp))
-    order = sorted({e & ~CORE for e in core_mlp})
-    early, middle = order[:-1], order[-1:]
-    pieces_early = {e: core_mlp[e] for g in early for e in (g, g | CORE)}
-    pieces_middle = {e: core_mlp[e] for g in middle for e in (g, g | CORE)}
+    second_near = swap(second, CORE)
+    held_mlp, second, second_near = fence((held_mlp, second, second_near))
+
+    early = {e: b for e, b in held_mlp.items()}
     relay_steps(held_mlp, cut_mlp)
 
-    def mlp_call(pieces, carried):
-        groups = tuple(sorted({e // 2 for e in pieces}))
+    def mlp_call(pieces, carried, last):
+        groups = tuple(sorted(pieces))
         arrays, places = [], []
-        for e in sorted(pieces):
+        for e in groups:
             block = pieces[e]
             if isinstance(block, tuple):
                 arrays += list(block)
-                places += [(e, 0, 0), (e, 1, 0)]
+                places += [(e, 0), (e, 1)]
             else:
                 arrays.append(block)
-                places.append((e, None, 0))
+                places.append((e, None))
         count = len(groups)
         fixed = pl.BlockSpec((row_count, width), lambda g: (0, 0))
         moving = pl.BlockSpec((1, 2, up_rows, width), lambda g: (g, 0, 0, 0))
-        keep, send, out, grad = pl.pallas_call(
-            functools.partial(mlp_kernel, (groups, tuple(places), up_rows, bool(carried))),
+        table = whole((row_count, width), f32)
+        out_shape = [whole((count, 2, up_rows, width), bf16), table, table]
+        out_specs = [moving, fixed, fixed]
+        scratch = []
+        if last:
+            out_shape.append(whole((2, row_count, width), bf16))
+            out_specs.append(pl.BlockSpec((2, row_count, width), lambda g: (0, 0, 0)))
+            scratch += [pltpu.VMEM((row_count, width), f32)] * 2
+        else:
+            out_shape += [table, table]
+            out_specs += [fixed, fixed]
+        made = pl.pallas_call(
+            functools.partial(mlp_kernel, (groups, tuple(places), up_rows, bool(carried), last)),
             grid=(count,),
-            out_shape=(
-                whole((count, 2, up_rows, width), bf16),
-                whole((count, 2, up_rows, width), bf16),
-                whole((row_count, width), f32),
-                whole((row_count, width), f32),
-            ),
-            in_specs=[fixed, fixed] + [ANY] * len(arrays) + [fixed] * len(carried),
-            out_specs=(moving, moving, fixed, fixed),
-            scratch_shapes=[
-                pltpu.VMEM((count, 2 * up_rows, width), bf16),
-                pltpu.VMEM((count, 2 * up_rows, width), bf16),
-                pltpu.VMEM((row_count, 2 * up_rows), bf16),
-                pltpu.VMEM((row_count, 2 * up_rows), bf16),
-                pltpu.SemaphoreType.DMA((4 * count,)),
+            out_shape=tuple(out_shape),
+            in_specs=[fixed] * 4 + [ANY] * len(arrays) + [fixed] * len(carried),
+            out_specs=tuple(out_specs),
+            scratch_shapes=scratch
+            + [
+                pltpu.VMEM((count, up_rows, width), bf16),
+                pltpu.VMEM((count, up_rows, width), bf16),
+                pltpu.VMEM((2, row_count, up_rows), bf16),
+                pltpu.VMEM((2, row_count, up_rows), bf16),
+                pltpu.SemaphoreType.DMA((2 * count,)),
             ],
             compiler_params=params(),
             cost_estimate=cost(1e9, 1e6),
             name="feed_forward",
-        )(second, cotangent, *arrays, *carried)
-        flat = (count, 2 * up_rows, width)
-        return groups, keep.reshape(flat), send.reshape(flat), out, grad
-
-    groups_a, keep_a, send_a, out_a, grad_a = mlp_call(pieces_early, ())
-    held_mlp, pieces_middle, keep_a, send_a, out_a, grad_a = fence((held_mlp, pieces_middle, keep_a, send_a, out_a, grad_a))
-
-    late = core_steps({e: b for e, b in held_mlp.items() if isinstance(b, tuple)})
-    came_a = swap(send_a, CORE)
-    groups_m, keep_m, send_m, out_m, grad_m = mlp_call(pieces_middle, (out_a, grad_a))
-    late, came_a, keep_m, send_m, out_m, grad_m = fence((late, came_a, keep_m, send_m, out_m, grad_m))
-
-    came_m = swap(send_m, CORE)
-    groups_b, keep_b, send_b, mlp_out, grad_second = mlp_call(late, (out_m, grad_m))
-    came_m, keep_b, send_b, mlp_out, grad_second = fence((came_m, keep_b, send_b, mlp_out, grad_second))
-
-    total_b = add_low(keep_b, swap(send_b, CORE))
-    total_a = add_low(keep_a, came_a)
-    total_m = add_low(keep_m, came_m)
+        )(second, second_near, cotangent, cotangent_near, *arrays, *carried)
+        return groups, made[0].reshape(count, 2 * up_rows, width), made[1:]
+
+    groups_a, keep_a, sums = mlp_call(early, (), False)
+    late, keep_a, sums = fence(({e: b for e, b in held_mlp.items() if isinstance(b, tuple)}, keep_a, sums))
+    groups_b, keep_b, (mlp_out, grad_second, mlp_going) = mlp_call(late, sums, True)
+    mlp_came = swap(mlp_going, CORE)
     totals = [None] * pairs
-    for groups, total in ((groups_a, total_a), (groups_m, total_m), (groups_b, total_b)):
-        for i, g in enumerate(groups):
-            totals[g] = total[i]
-    totals, mlp_out = fence((totals, mlp_out))
+    for groups, keep in ((groups_a, keep_a), (groups_b, keep_b)):
+        for i, e in enumerate(groups):
+            totals[e // 2] = keep[i]
+    totals, mlp_came = fence((totals, mlp_came))
 
     sum_mlp = OuterSum(totals, cut_mlp)
     sum_mlp.relays()
@@ -836,7 +843,7 @@
             whole((pairs, rows_two, width), bf16),
             whole((pairs, rows_two, width), bf16),
         ),
-        in_specs=[SMEM] + [VMEM] * 9 + [ANY] * len(arrays_two),
+        in_specs=[SMEM] + [VMEM] * 10 + [ANY] * len(arrays_two),
         out_specs=(VMEM,) * 5 + (ANY,) * 2,
         scratch_shapes=[
             wide[3],
@@ -847,11 +854,11 @@
         compiler_params=params(),
         cost_estimate=cost(1e9, 1e6),
         name="cross_attention_backward",
-    )(ints, coarse_seg, gains, mlp_out, grad_second, joined, cotangent, crossed, cq, ckv, *arrays_two)
+    )(ints, coarse_seg, gains, mlp_out, grad_second, mlp_came, joined, cotangent, crossed, cq, ckv, *arrays_two)
     state, grad_joined = fence((sum_mlp.state(), grad_joined))
     sum_mlp.put(state)
 
-    sum_mlp.singles()
+    sum_mlp.singles_half(0)
     coarse_grad, grad_res, grad_att, gain_grads, keep_two, send_two = pl.pallas_call(
         functools.partial(third_part, (places_two, layout, dp_count)),
         out_shape=(
@@ -882,6 +889,11 @@
         ints, coarse_view, gains, gain_two, grad_joined, residual, attended, grad_cq, grad_ckv, keep_two, send_two, *arrays_two
     )
 
+    state, grad_att, keep_two, send_two = fence((sum_mlp.state(), grad_att, keep_two, send_two))
+    sum_mlp.put(state)
+
+    sum_mlp.singles_half(1)
+    came_two = swap(send_two, CORE)
     (grad_proj,) = pl.pallas_call(
         functools.partial(fourth_kernel, (blocks,)),
         out_shape=(whole((row_count, 3 * width), bf16),),
@@ -892,10 +904,11 @@
         cost_estimate=cost(1e9, 1e6),
         name="self_attention_backward",
     )(ints, seg_row, grad_att, qkv)
-    state, grad_proj, keep_two, send_two = fence((sum_mlp.state(), grad_proj, keep_two, send_two))
+    state, grad_proj, came_two = fence((sum_mlp.state(), grad_proj, came_two))
     sum_mlp.put(state)
 
-    came_two = swap(send_two, CORE)
+    sum_two = OuterSum(add_low(keep_two, came_two), cut_two)
+    sum_two.relays()
     mlp_sum = sum_mlp.result()
     mlp_parts = jnp.concatenate(
         [mlp_sum[:up_rows].reshape(fsdp_count, up_part, width), mlp_sum[up_rows:].reshape(fsdp_count, up_part, width)], axis=1
@@ -920,10 +933,10 @@
         cost_estimate=cost(1e9, 1e6),
         name="self_attention_input",
     )(ints, mix_weight, gains, blended, grad_res, grad_proj, *arrays_one)
-    came_two, keep_tok, send_tok, gain_one = fence((came_two, keep_tok, send_tok, gain_one))
-
-    sum_two = OuterSum(add_low(keep_two, came_two), cut_two)
-    sum_two.relays()
+    state, keep_tok, send_tok, gain_one = fence((sum_two.state(), keep_tok, send_tok, gain_one))
+    sum_two.put(state)
+
+    sum_two.singles()
     came_tok = swap(send_tok, CORE)
     keep_one, send_one = pl.pallas_call(
         functools.partial(sixth_kernel, (dp_count, qkv_rows)),
@@ -946,28 +959,25 @@
     sum_two.put(state)
     inner_mlp.came = mlp_came
 
-    sum_two.singles()
+    sum_tok = OuterSum(add_low(keep_tok, came_tok), cut_tok)
+    sum_tok.relays()
     came_one = swap(send_one, CORE)
-    total_tok = add_low(keep_tok, came_tok)
-    state, came_one, total_tok = fence((sum_two.state(), came_one, total_tok))
-    sum_two.put(state)
-
-    sum_one, sum_tok = OuterSum(add_low(keep_one, came_one), cut_one), OuterSum(total_tok, cut_tok)
-    sum_one.relays()
-    sum_tok.relays()
     two_sum = sum_two.result()
     two_parts = jnp.concatenate(
         [two_sum[first : first + size].reshape(fsdp_count, size // fsdp_count, width) for first, size in layout], axis=1
     )
+    state, came_one, two_parts = fence((sum_tok.state(), came_one, two_parts))
+    sum_tok.put(state)
+
+    sum_one = OuterSum(add_low(keep_one, came_one), cut_one)
+    sum_one.relays()
     inner_two = InnerSum(two_parts)
-    state, state_tok, two_came = fence((sum_one.state(), sum_tok.state(), inner_two.came))
-    sum_one.put(state)
-    sum_tok.put(state_tok)
-    inner_two.came = two_came
-
-    sum_one.singles()
     state = fence(sum_one.state())
     sum_one.put(state)
+    sum_one.singles()
+    state, two_came = fence((sum_one.state(), inner_two.came))
+    sum_one.put(state)
+    inner_two.came = two_came
     sum_tok.singles()
     one_sum = sum_one.result()
     gain_sum = jnp.broadcast_to(one_sum[qkv_rows : qkv_rows + 8][None], (fsdp_count, 8, width))

time: 378 us -> 356 us (0.942)
  waiting for transfers between devices: 127 us -> 99.6 us
  between operations: 2.12 us -> 15.5 us
    ppermute x58 -> x55, waiting for transfers between devices: 73.1 us -> 58.6 us  [swap(): return lax.ppermute(values, 'dp', [(i, i ^ mask) for i in range(count)])]
    ppermute x2 -> x0, waiting for transfers between devices: 14.2 us -> none  [inner_gather(): came = lax.ppermute(held, 'fsdp', [(i, i ^ mask) for i in range(count)])]
    ppermute x2 -> x0, starting transfers between devices: 6.04 us -> none  [inner_gather(): came = lax.ppermute(held, 'fsdp', [(i, i ^ mask) for i in range(count)])]
    all_gather x0 -> x1, waiting for transfers between devices: none -> 5.94 us  [shards(): mlp = lax.all_gather(shard_mlp, 'fsdp', axis=0, tiled=False)]
    ppermute x15, waiting for transfers between devices: 39.6 us -> 35.1 us  [shift(): lax.ppermute(values, 'fsdp', [(i, (i + step) % count) for i in range(coun...]
    convert_element_type x12 -> x11, other arithmetic: 9.88 us -> 6.45 us  [add_low(): return (a.astype(f32) + b.astype(f32)).astype(bf16)]
    pallas_call x3 -> x2, Pallas kernels: 32.9 us -> 29.9 us  [mlp_call(): pl.pallas_call(functools.partial(mlp_kernel, (groups, tuple(places), up_r...]
    unnamed x116 -> x102, local copies, waits for them, and re-layouts: 11.7 us -> 10.2 us
  transfers between devices with their start and end apart: 75 -> 71, of which waited for: 29 -> 31; matrix products, arithmetic and copies ran while one was open for 9% -> 9% of each run, Pallas kernels for 32% -> 30%
where the time goes in v4:
time: 356 us; the launch traced here: 351 us
  Pallas kernels  116 us (33%)
  waiting for transfers between devices  99.6 us (28%)
  starting transfers between devices  72.7 us (20%)
  local copies, waits for them, and re-layouts  26 us (7%)
  other arithmetic  21.2 us (6%)
  between operations  15.5 us (4%)
    ppermute x55, waiting for transfers between devices, swap(): return lax.ppermute(values, 'dp', [(i, i ^ mask) for i in range(count)])  58.6 us
    ppermute x55, starting transfers between devices, swap(): return lax.ppermute(values, 'dp', [(i, i ^ mask) for i in range(count)])  42 us
    ppermute x15, waiting for transfers between devices, shift(): lax.ppermute(values, 'fsdp', [(i, (i + step) % count) for i in range(coun...  35.1 us
    ppermute x15, starting transfers between devices, shift(): lax.ppermute(values, 'fsdp', [(i, (i + step) % count) for i in range(coun...  30.7 us
    pallas_call x2, Pallas kernels, mlp_call(): pl.pallas_call(functools.partial(mlp_kernel, (groups, tuple(places), up_r...  29.9 us
    pallas_call x1, Pallas kernels, shards(): pl.pallas_call(functools.partial(fourth_kernel, (blocks,)), out_shape=(wh...  19.1 us
    pallas_call x1, Pallas kernels, shards(): pl.pallas_call(functools.partial(third_kernel, (blocks, places_two, layou...  14.5 us
    pallas_call x1, Pallas kernels, shards(): pl.pallas_call(functools.partial(first_kernel, (dp_count, blocks, places_...  13 us
  transfers between devices with their start and end apart: 71, of which 31 were waited for; matrix products, arithmetic and copies ran while one was open for 9% of the time, Pallas kernels for 30%

profile of v4, /device:TPU:0, one launch (start us, length us, event | category | flops | bytes accessed | tf_op | source)
XLA Modules:
  0.0 350.8 jit_solution(11357393575801649974)
XLA Ops:
  18.1 3.7 %collective-permute-done.2 = bf16[80,768]{1,0:T(8,128)(2,1)S(1)} collective-permute-done((bf16[80,768]{1,0:T(8,128)(2,1)S(1)}, bf16[80,768]{1,0:T(8,128)(2,1)S(1)}, u32[]{:S(2)}, u32[]{:S(2)}) %collective-permute-start.2) | collective-permute-done | bytes 122912 | tf_op jit(solution)/shard_map/ppermute | solution.py:30
  42.4 5.4 %collective-permute-done.9 = bf16[120,768]{1,0:T(8,128)(2,1)S(1)} collective-permute-done((bf16[120,768]{1,0:T(8,128)(2,1)}, bf16[120,768]{1,0:T(8,128)(2,1)S(1)}, u32[]{:S(2)}, u32[]{:S(2)}) %collective-permute-start.9) | collective-permute-done | bytes 184352 | tf_op jit(solution)/shard_map/ppermute | solution.py:30
  54.9 7.3 %collective-permute-done.14.refs_6_ = bf16[256,768]{1,0:T(8,128)(2,1)} collective-permute-done((bf16[256,768]{1,0:T(8,128)(2,1)S(1)}, bf16[256,768]{1,0:T(8,128)(2,1)}, u32[]{:S(2)}, u32[]{:S(2)}) %collective-permute-start.14) | collective-permute-done | bytes 393248 | tf_op jit(solution)/shard_map/ppermute | solution.py:25
  66.1 5.2 %collective-permute-done.16.refs_16_.refs_6_ = bf16[144,768]{1,0:T(8,128)(2,1)} collective-permute-done((bf16[144,768]{1,0:T(8,128)(2,1)S(1)}, bf16[144,768]{1,0:T(8,128)(2,1)}, u32[]{:S(2)}, u32[]{:S(2)}) %collective-permute-start.16) | collective-permute-done | bytes 221216 | tf_op jit(solution)/shard_map/ppermute | solution.py:25
  79.6 13.0 %mix_self_attention.1 = (f32[512,768]{1,0:T(8,128)}, bf16[512,2304]{1,0:T(8,128)(2,1)}, bf16[512,768]{1,0:T(8,128)(2,1)}, f32[8,768]{1,0:T(8,128)}) custom-call(s32[17]{0:T(128)} %concatenate.62.ints, f32[4]{0:T(128)} %mix.3, s32[1,512]{1,0:T(1,128)} %seg_row.3, bf16[512,768]{1,0:T(8,128)(2,1)} %refs_0_, bf16[512,768]{1,0:T(8,128)(2,1)} %refs_0_, ...), custom_call_target="tpu_custom_call" | custom-call | flops 1000000000 | bytes 1000000 | tf_op jit(solution)/shard_map/mix_self_attention/pallas_call | solution.py:718
  97.9 5.9 %all-gather.3.cloned.1.call-done = bf16[768,768]{1,0:T(8,128)(2,1)} async-done(((bf16[192,768]{1,0:T(8,128)(2,1)}), bf16[768,768]{1,0:T(8,128)(2,1)}) %all-gather.3.cloned.1.call-update) | async-done | bytes 1179664 | tf_op jit(solution)/shard_map/all_gather | solution.py:695
  114.2 11.1 %cross_attention.1 = (f32[512,768]{1,0:T(8,128)}, bf16[512,768]{1,0:T(8,128)(2,1)}, bf16[128,1536]{1,0:T(8,128)(2,1)}, bf16[512,768]{1,0:T(8,128)(2,1)}, f32[512,768]{1,0:T(8,128)}, /*index=5*/bf16[512,768]{1,0:T(8,128)(2,1)}) custom-call(s32[17]{0:T(128)} %concatenate.62.ints, s32[1,128]{1,0:T(1,128)} %bitcast.167, bf16[128,768]{1,0:T(8,128)(2,1)} %coarse.3, ...), custom_call_target="tpu_custom_call" | custom-call | flops 1000000000 | bytes 1000000 | tf_op jit(solution)/shard_map/cross_attention/pallas_call | solution.py:755
  125.9 11.6 %collective-permute-done.32.refs_1_ = bf16[768,768]{1,0:T(8,128)(2,1)} collective-permute-done((bf16[768,768]{1,0:T(8,128)(2,1)S(1)}, bf16[768,768]{1,0:T(8,128)(2,1)}, u32[]{:S(2)}, u32[]{:S(2)}) %collective-permute-start.32) | collective-permute-done | bytes 1179680 | tf_op jit(solution)/shard_map/ppermute | solution.py:25
  141.7 19.0 %feed_forward.2 = (bf16[3,2,384,768]{3,2,1,0:T(8,128)(2,1)}, f32[512,768]{1,0:T(8,128)}, f32[512,768]{1,0:T(8,128)}, f32[512,768]{1,0:T(8,128)}, f32[512,768]{1,0:T(8,128)}) custom-call(bf16[512,768]{1,0:T(8,128)(2,1)} %get-tuple-element.244.second, bf16[512,768]{1,0:T(8,128)(2,1)} %copy-done.12, bf16[512,768]{1,0:T(8,128)(2,1)} %cotangent.5, ...), custom_call_target="tpu_custom_call" | custom-call | flops 1000000000 | bytes 1000000 | tf_op jit(solution)/shard_map/feed_forward/pallas_call | solution.py:803
  161.8 10.9 %feed_forward.3 = (bf16[1,2,384,768]{3,2,1,0:T(8,128)(2,1)}, f32[512,768]{1,0:T(8,128)}, f32[512,768]{1,0:T(8,128)}, bf16[2,512,768]{2,1,0:T(8,128)(2,1)}) custom-call(bf16[512,768]{1,0:T(8,128)(2,1)} %get-tuple-element.244.second, bf16[512,768]{1,0:T(8,128)(2,1)} %copy-done.12, bf16[512,768]{1,0:T(8,128)(2,1)} %cotangent.5, bf16[512,768]{1,0:T(8,128)(2,1)} %copy-done.11, ...), custom_call_target="tpu_custom_call" | custom-call | flops 1000000000 | bytes 1000000 | tf_op jit(solution)/shard_map/feed_forward/pallas_call | solution.py:803
  179.5 14.5 %cross_attention_backward.1 = (bf16[512,768]{1,0:T(8,128)(2,1)}, f32[512,768]{1,0:T(8,128)}, bf16[512,768]{1,0:T(8,128)(2,1)}, bf16[128,1536]{1,0:T(8,128)(2,1)}...) custom-call(s32[17]{0:T(128)} %concatenate.62.ints, s32[1,128]{1,0:T(1,128)} %bitcast.168, ...), custom_call_target="tpu_custom_call" | custom-call | flops 1000000000 | bytes 1000000 | tf_op jit(solution)/shard_map/cross_attention_backward/pallas_call | solution.py:835
  195.6 10.2 %cross_attention_weights.1 = (f32[128,768]{1,0:T(8,128)}, f32[512,768]{1,0:T(8,128)}, bf16[512,768]{1,0:T(8,128)(2,1)}, f32[8,768]{1,0:T(8,128)}, bf16[4,480,768...) custom-call(s32[17]{0:T(128)} %concatenate.62.ints, ...), custom_call_target="tpu_custom_call", output_to_operand_aliasing={{4}: (9, {}), {5}: (10, {})} | custom-call | flops 1000000000 | bytes 1000000 | tf_op jit(solution)/shard_map/cross_attention_weights/pallas_call | solution.py:862
  211.8 19.1 %self_attention_backward.1.grad_proj = bf16[512,2304]{1,0:T(8,128)(2,1)} custom-call(s32[17]{0:T(128)} %concatenate.62.ints, s32[1,512]{1,0:T(1,128)} %seg_row.3, bf16[512,768]{1,0:T(8,128)(2,1)} %get-tuple-element.299.grad_att, bf16[512,2304]{1,0:T(8,128)(2,1)} %get-tuple-element.300.qkv), custom_call_target="tpu_custom_call" | custom-call | flops 1000000000 | bytes 1000000 | tf_op jit(solution)/shard_map/self_attention_backward/pallas_call | solution.py:897
  237.2 11.3 %self_attention_input.1 = (f32[512,768]{1,0:T(8,128)}, f32[8,768]{1,0:T(8,128)}, bf16[4,512,768]{2,1,0:T(8,128)(2,1)}, bf16[4,512,768]{2,1,0:T(8,128)(2,1)}) custom-call(s32[17]{0:T(128)} %concatenate.62.ints, f32[4]{0:T(128)} %mix.3, f32[8,768]{1,0:T(8,128)} %get-tuple-element.225.gains, f32[512,768]{1,0:T(8,128)} %get-tuple-element.233.blended, ...), custom_call_target="tpu_custom_call" | custom-call | flops 1000000000 | bytes 1000000 | tf_op jit(solution)/shard_map/self_attention_input/pallas_call | solution.py:917
  258.9 4.3 %collective-permute-start.52 = (bf16[192,768]{1,0:T(8,128)(2,1)S(1)}, bf16[192,768]{1,0:T(8,128)(2,1)S(1)}, u32[]{:S(2)}, u32[]{:S(2)}) collective-permute-start(bf16[192,768]{1,0:T(8,128)(2,1)S(1)} %get-tuple-element.377), channel_id=1, source_target_pairs={{0,1},{1,2},{2,3},{3,0},{4,5},{5,6},{6,7},{7,4},{8,9},{9,10},{10,1... | collective-permute-start | bytes 884744 | tf_op jit(solution)/shard_map/ppermute | solution.py:30
  264.7 7.4 %collective-permute-done.52 = bf16[192,768]{1,0:T(8,128)(2,1)S(1)} collective-permute-done((bf16[192,768]{1,0:T(8,128)(2,1)S(1)}, bf16[192,768]{1,0:T(8,128)(2,1)S(1)}, u32[]{:S(2)}, u32[]{:S(2)}) %collective-permute-start.52) | collective-permute-done | bytes 294944 | tf_op jit(solution)/shard_map/ppermute | solution.py:30
  273.6 6.6 %self_attention_weights.1 = (bf16[4,304,768]{2,1,0:T(8,128)(2,1)}, bf16[4,304,768]{2,1,0:T(8,128)(2,1)}) custom-call(s32[17]{0:T(128)} %concatenate.62.ints, f32[8,768]{1,0:T(8,128)} %get-tuple-element.225.gains, f32[8,768]{1,0:T(8,128)} %get-tuple-element.316.gain_grads, f32[8,768]{1,0:T(8,128)} %get-tuple-element.317.gain_one, ...), custom_call_target="tpu_custom_call" | custom-call | flops 1000000000 | bytes 1000000 | tf_op jit(solution)/shard_map/self_attention_weights/pallas_call | solution.py:941
  280.3 3.9 %collective-permute-done.53 = bf16[192,768]{1,0:T(8,128)(2,1)} collective-permute-done((bf16[192,768]{1,0:T(8,128)(2,1)}, bf16[192,768]{1,0:T(8,128)(2,1)}, u32[]{:S(2)}, u32[]{:S(2)}) %collective-permute-start.53) | collective-permute-done | bytes 294944 | tf_op jit(solution)/shard_map/ppermute | solution.py:30
  294.5 6.0 %collective-permute-done.55 = bf16[256,768]{1,0:T(8,128)(2,1)S(1)} collective-permute-done((bf16[256,768]{1,0:T(8,128)(2,1)S(1)}, bf16[256,768]{1,0:T(8,128)(2,1)S(1)}, u32[]{:S(2)}, u32[]{:S(2)}) %collective-permute-start.55) | collective-permute-done | bytes 393248 | tf_op jit(solution)/shard_map/ppermute | solution.py:25
  304.1 4.8 %collective-permute-start.64 = (bf16[120,768]{1,0:T(8,128)(2,1)S(1)}, bf16[120,768]{1,0:T(8,128)(2,1)S(1)}, u32[]{:S(2)}, u32[]{:S(2)}) collective-permute-start(bf16[120,768]{1,0:T(8,128)(2,1)S(1)} %get-tuple-element.384), channel_id=1, source_target_pairs={{0,1},{1,2},{2,3},{3,0},{4,5},{5,6},{6,7},{7,4},{8,9},{9,10},{10,1... | collective-permute-start | bytes 552968 | tf_op jit(solution)/shard_map/ppermute | solution.py:30
  316.4 4.8 %collective-permute-done.65 = bf16[120,768]{1,0:T(8,128)(2,1)S(1)} collective-permute-done((bf16[120,768]{1,0:T(8,128)(2,1)S(1)}, bf16[120,768]{1,0:T(8,128)(2,1)S(1)}, u32[]{:S(2)}, u32[]{:S(2)}) %collective-permute-start.65) | collective-permute-done | bytes 184352 | tf_op jit(solution)/shard_map/ppermute | solution.py:30
  322.6 4.1 %collective-permute-done.63 = bf16[304,768]{1,0:T(8,128)(2,1)S(1)} collective-permute-done((bf16[304,768]{1,0:T(8,128)(2,1)S(1)}, bf16[304,768]{1,0:T(8,128)(2,1)S(1)}, u32[]{:S(2)}, u32[]{:S(2)}) %collective-permute-start.63) | collective-permute-done | bytes 466976 | tf_op jit(solution)/shard_map/ppermute | solution.py:25
  327.0 3.8 %collective-permute-start.69 = (bf16[80,768]{1,0:T(8,128)(2,1)S(1)}, bf16[80,768]{1,0:T(8,128)(2,1)S(1)}, u32[]{:S(2)}, u32[]{:S(2)}) collective-permute-start(bf16[80,768]{1,0:T(8,128)(2,1)S(1)} %get-tuple-element.388), channel_id=1, source_target_pairs={{0,3},{1,0},{2,1},{3,2},{4,7},{5,4},{6,5},{7,6},{8,11},{9,8},{10,9... | collective-permute-start | bytes 368648 | tf_op jit(solution)/shard_map/ppermute | solution.py:30
  333.0 7.4 %collective-permute-done.59 = bf16[512,768]{1,0:T(8,128)(2,1)S(1)} collective-permute-done((bf16[512,768]{1,0:T(8,128)(2,1)S(1)}, bf16[512,768]{1,0:T(8,128)(2,1)S(1)}, u32[]{:S(2)}, u32[]{:S(2)}) %collective-permute-start.59) | collective-permute-done | bytes 786464 | tf_op jit(solution)/shard_map/ppermute | solution.py:25
  (325 shorter events, 133.9 us)
Async XLA Ops:
  7.2 96.6 %all-gather.3.cloned.1.call-start = ((), (), s32[]{:S(2)}) async-start(), calls=%async_computation | async-start | bytes 1474560 | tf_op jit(solution)/shard_map/all_gather | solution.py:695
  7.2 22.0 %collective-permute-start = (bf16[512,768]{1,0:T(8,128)(2,1)}, bf16[512,768]{1,0:T(8,128)(2,1)S(1)}, u32[]{:S(2)}, u32[]{:S(2)}) collective-permute-start(bf16[512,768]{1,0:T(8,128)(2,1)} %refs_0_), channel_id=1, source_target_pairs={{0,8},{4,12},{8,0},{12,4},{16,24},{20,28},{24,16},{28,20},{1,9},{5... | collective-permute-start | bytes 2359304 | tf_op jit(solution)/shard_map/ppermute | solution.py:25
  10.2 19.2 %collective-permute-start.1 = (bf16[512,768]{1,0:T(8,128)(2,1)}, bf16[512,768]{1,0:T(8,128)(2,1)S(1)}, u32[]{:S(2)}, u32[]{:S(2)}) collective-permute-start(bf16[512,768]{1,0:T(8,128)(2,1)} %refs_0_), channel_id=1, source_target_pairs={{0,16},{4,20},{8,24},{12,28},{16,0},{20,4},{24,8},{28,12},{1,17},{... | collective-permute-start | bytes 2359304 | tf_op jit(solution)/shard_map/ppermute | solution.py:25
  11.7 17.7 %collective-permute-start.5 = (bf16[512,768]{1,0:T(8,128)(2,1)}, bf16[512,768]{1,0:T(8,128)(2,1)S(1)}, u32[]{:S(2)}, u32[]{:S(2)}) collective-permute-start(bf16[512,768]{1,0:T(8,128)(2,1)} %cotangent.5), channel_id=1, source_target_pairs={{0,4},{4,0},{8,12},{12,8},{16,20},{20,16},{24,28},{28,24},{1,5},{5... | collective-permute-start | bytes 2359304 | tf_op jit(solution)/shard_map/ppermute | solution.py:25
  30.6 17.2 %collective-permute-start.6 = (bf16[304,768]{1,0:T(8,128)(2,1)S(1)}, bf16[304,768]{1,0:T(8,128)(2,1)S(1)}, u32[]{:S(2)}, u32[]{:S(2)}) collective-permute-start(bf16[304,768]{1,0:T(8,128)(2,1)S(1)} %pad_maximum_fusion.9.refs_10_.refs_0_), channel_id=1, source_target_pairs={{0,8},{4,12},{8,0},{12,4},{16,24},{20,28},{24,16},{28,20},{1,9},{5... | collective-permute-start | bytes 1400840 | tf_op jit(solution)/shard_map/ppermute | solution.py:25
  31.2 16.6 %collective-permute-start.7 = (bf16[304,768]{1,0:T(8,128)(2,1)S(1)}, bf16[304,768]{1,0:T(8,128)(2,1)S(1)}, u32[]{:S(2)}, u32[]{:S(2)}) collective-permute-start(bf16[304,768]{1,0:T(8,128)(2,1)S(1)} %pad_maximum_fusion.9.refs_10_.refs_0_), channel_id=1, source_target_pairs={{0,16},{4,20},{8,24},{12,28},{16,0},{20,4},{24,8},{28,12},{1,17},{... | collective-permute-start | bytes 1400840 | tf_op jit(solution)/shard_map/ppermute | solution.py:25
  47.8 15.2 %collective-permute-start.12 = (bf16[512,768]{1,0:T(8,128)(2,1)}, bf16[512,768]{1,0:T(8,128)(2,1)S(1)}, u32[]{:S(2)}, u32[]{:S(2)}) collective-permute-start(bf16[512,768]{1,0:T(8,128)(2,1)} %copy-done.21), channel_id=1, source_target_pairs={{0,4},{4,0},{8,12},{12,8},{16,20},{20,16},{24,28},{28,24},{1,5},{5... | collective-permute-start | bytes 2359304 | tf_op jit(solution)/shard_map/ppermute | solution.py:25
  74.6 18.5 %collective-permute-start.25 = (bf16[480,768]{1,0:T(8,128)(2,1)S(1)}, bf16[480,768]{1,0:T(8,128)(2,1)S(1)}, u32[]{:S(2)}, u32[]{:S(2)}) collective-permute-start(bf16[480,768]{1,0:T(8,128)(2,1)S(1)} %pad_maximum_fusion.6.refs_0_), channel_id=1, source_target_pairs={{0,8},{4,12},{8,0},{12,4},{16,24},{20,28},{24,16},{28,20},{1,9},{5... | collective-permute-start | bytes 2211848 | tf_op jit(solution)/shard_map/ppermute | solution.py:25
  75.0 18.2 %collective-permute-start.26 = (bf16[480,768]{1,0:T(8,128)(2,1)S(1)}, bf16[480,768]{1,0:T(8,128)(2,1)S(1)}, u32[]{:S(2)}, u32[]{:S(2)}) collective-permute-start(bf16[480,768]{1,0:T(8,128)(2,1)S(1)} %pad_maximum_fusion.6.refs_0_), channel_id=1, source_target_pairs={{0,16},{4,20},{8,24},{12,28},{16,0},{20,4},{24,8},{28,12},{1,17},{... | collective-permute-start | bytes 2211848 | tf_op jit(solution)/shard_map/ppermute | solution.py:25
  109.3 28.2 %collective-permute-start.32 = (bf16[768,768]{1,0:T(8,128)(2,1)S(1)}, bf16[768,768]{1,0:T(8,128)(2,1)}, u32[]{:S(2)}, u32[]{:S(2)}) collective-permute-start(bf16[768,768]{1,0:T(8,128)(2,1)S(1)} %pad_maximum_fusion.3.refs_0_), channel_id=1, source_target_pairs={{0,8},{4,12},{8,0},{12,4},{16,24},{20,28},{24,16},{28,20},{1,9},{5... | collective-permute-start | bytes 3538952 | tf_op jit(solution)/shard_map/ppermute | solution.py:25
  111.0 27.8 %collective-permute-start.33 = (bf16[768,768]{1,0:T(8,128)(2,1)S(1)}, bf16[768,768]{1,0:T(8,128)(2,1)S(1)}, u32[]{:S(2)}, u32[]{:S(2)}) collective-permute-start(bf16[768,768]{1,0:T(8,128)(2,1)S(1)} %pad_maximum_fusion.3.refs_0_), channel_id=1, source_target_pairs={{0,16},{4,20},{8,24},{12,28},{16,0},{20,4},{24,8},{28,12},{1,17},{... | collective-permute-start | bytes 3538952 | tf_op jit(solution)/shard_map/ppermute | solution.py:25
  140.3 20.4 %collective-permute-start.37 = (bf16[384,768]{1,0:T(8,128)(2,1)S(1)}, bf16[384,768]{1,0:T(8,128)(2,1)S(1)}, u32[]{:S(2)}, u32[]{:S(2)}) collective-permute-start(bf16[384,768]{1,0:T(8,128)(2,1)S(1)} %slice.246), channel_id=1, source_target_pairs={{0,16},{4,20},{8,24},{12,28},{16,0},{20,4},{24,8},{28,12},{1,17},{... | collective-permute-start | bytes 1769480 | tf_op jit(solution)/shard_map/ppermute | solution.py:25
  141.0 19.7 %collective-permute-start.38 = (bf16[384,768]{1,0:T(8,128)(2,1)S(1)}, bf16[384,768]{1,0:T(8,128)(2,1)S(1)}, u32[]{:S(2)}, u32[]{:S(2)}) collective-permute-start(bf16[384,768]{1,0:T(8,128)(2,1)S(1)} %slice.247), channel_id=1, source_target_pairs={{0,8},{4,12},{8,0},{12,4},{16,24},{20,28},{24,16},{28,20},{1,9},{5... | collective-permute-start | bytes 1769480 | tf_op jit(solution)/shard_map/ppermute | solution.py:25
  176.6 17.4 %collective-permute-start.40 = (bf16[384,768]{1,0:T(8,128)(2,1)S(1)}, bf16[384,768]{1,0:T(8,128)(2,1)S(1)}, u32[]{:S(2)}, u32[]{:S(2)}) collective-permute-start(bf16[384,768]{1,0:T(8,128)(2,1)S(1)} %get-tuple-element.379), channel_id=1, source_target_pairs={{0,16},{4,20},{8,24},{12,28},{16,0},{20,4},{24,8},{28,12},{1,17},{... | collective-permute-start | bytes 1769480 | tf_op jit(solution)/shard_map/ppermute | solution.py:25
  177.9 16.1 %collective-permute-start.41 = (bf16[384,768]{1,0:T(8,128)(2,1)S(1)}, bf16[384,768]{1,0:T(8,128)(2,1)S(1)}, u32[]{:S(2)}, u32[]{:S(2)}) collective-permute-start(bf16[384,768]{1,0:T(8,128)(2,1)S(1)} %get-tuple-element.378), channel_id=1, source_target_pairs={{0,8},{4,12},{8,0},{12,4},{16,24},{20,28},{24,16},{28,20},{1,9},{5... | collective-permute-start | bytes 1769480 | tf_op jit(solution)/shard_map/ppermute | solution.py:25
  209.3 23.3 %collective-permute-start.46 = (bf16[4,480,768]{2,1,0:T(8,128)(2,1)}, bf16[4,480,768]{2,1,0:T(8,128)(2,1)}, u32[]{:S(2)}, u32[]{:S(2)}) collective-permute-start(bf16[4,480,768]{2,1,0:T(8,128)(2,1)} %get-tuple-element.301), channel_id=1, source_target_pairs={{0,4},{4,0},{8,12},{12,8},{16,20},{20,16},{24,28},{28,24},{1,5},{5... | collective-permute-start | bytes 8847368 | tf_op jit(solution)/shard_map/ppermute | solution.py:25
  209.3 21.6 %collective-permute-start.44 = (bf16[384,768]{1,0:T(8,128)(2,1)S(1)}, bf16[384,768]{1,0:T(8,128)(2,1)S(1)}, u32[]{:S(2)}, u32[]{:S(2)}) collective-permute-start(bf16[384,768]{1,0:T(8,128)(2,1)S(1)} %slice.255), channel_id=1, source_target_pairs={{0,8},{4,12},{8,0},{12,4},{16,24},{20,28},{24,16},{28,20},{1,9},{5... | collective-permute-start | bytes 1769480 | tf_op jit(solution)/shard_map/ppermute | solution.py:25
  211.1 19.8 %collective-permute-start.45 = (bf16[384,768]{1,0:T(8,128)(2,1)S(1)}, bf16[384,768]{1,0:T(8,128)(2,1)S(1)}, u32[]{:S(2)}, u32[]{:S(2)}) collective-permute-start(bf16[384,768]{1,0:T(8,128)(2,1)S(1)} %add_convert_fusion.3), channel_id=1, source_target_pairs={{0,16},{4,20},{8,24},{12,28},{16,0},{20,4},{24,8},{28,12},{1,17},{... | collective-permute-start | bytes 1769480 | tf_op jit(solution)/shard_map/ppermute | solution.py:25
  250.5 35.6 %collective-permute-start.51 = (bf16[4,512,768]{2,1,0:T(8,128)(2,1)}, bf16[4,512,768]{2,1,0:T(8,128)(2,1)}, u32[]{:S(2)}, u32[]{:S(2)}) collective-permute-start(bf16[4,512,768]{2,1,0:T(8,128)(2,1)} %get-tuple-element.315), channel_id=1, source_target_pairs={{0,4},{4,0},{8,12},{12,8},{16,20},{20,16},{24,28},{28,24},{1,5},{5... | collective-permute-start | bytes 9437192 | tf_op jit(solution)/shard_map/ppermute | solution.py:25
  254.7 31.5 %collective-permute-start.49 = (bf16[480,768]{1,0:T(8,128)(2,1)}, bf16[480,768]{1,0:T(8,128)(2,1)}, u32[]{:S(2)}, u32[]{:S(2)}) collective-permute-start(bf16[480,768]{1,0:T(8,128)(2,1)} %pad_maximum_fusion.7), channel_id=1, source_target_pairs={{0,8},{4,12},{8,0},{12,4},{16,24},{20,28},{24,16},{28,20},{1,9},{5... | collective-permute-start | bytes 2211848 | tf_op jit(solution)/shard_map/ppermute | solution.py:25
  257.3 28.9 %collective-permute-start.50 = (bf16[480,768]{1,0:T(8,128)(2,1)}, bf16[480,768]{1,0:T(8,128)(2,1)}, u32[]{:S(2)}, u32[]{:S(2)}) collective-permute-start(bf16[480,768]{1,0:T(8,128)(2,1)} %pad_maximum_fusion.8), channel_id=1, source_target_pairs={{0,16},{4,20},{8,24},{12,28},{16,0},{20,4},{24,8},{28,12},{1,17},{... | collective-permute-start | bytes 2211848 | tf_op jit(solution)/shard_map/ppermute | solution.py:25
  263.2 20.9 %collective-permute-start.53 = (bf16[192,768]{1,0:T(8,128)(2,1)}, bf16[192,768]{1,0:T(8,128)(2,1)}, u32[]{:S(2)}, u32[]{:S(2)}) collective-permute-start(bf16[192,768]{1,0:T(8,128)(2,1)} %get-tuple-element.376), channel_id=1, source_target_pairs={{0,2},{1,3},{2,0},{3,1},{4,6},{5,7},{6,4},{7,5},{8,10},{9,11},{10,... | collective-permute-start | bytes 884744 | tf_op jit(solution)/shard_map/ppermute | solution.py:30
  315.3 25.2 %collective-permute-start.59 = (bf16[512,768]{1,0:T(8,128)(2,1)S(1)}, bf16[512,768]{1,0:T(8,128)(2,1)S(1)}, u32[]{:S(2)}, u32[]{:S(2)}) collective-permute-start(bf16[512,768]{1,0:T(8,128)(2,1)S(1)} %pad_maximum_fusion.5), channel_id=1, source_target_pairs={{0,16},{4,20},{8,24},{12,28},{16,0},{20,4},{24,8},{28,12},{1,17},{... | collective-permute-start | bytes 2359304 | tf_op jit(solution)/shard_map/ppermute | solution.py:25
  321.2 19.4 %collective-permute-start.58 = (bf16[512,768]{1,0:T(8,128)(2,1)S(1)}, bf16[512,768]{1,0:T(8,128)(2,1)S(1)}, u32[]{:S(2)}, u32[]{:S(2)}) collective-permute-start(bf16[512,768]{1,0:T(8,128)(2,1)S(1)} %pad_maximum_fusion.4), channel_id=1, source_target_pairs={{0,8},{4,12},{8,0},{12,4},{16,24},{20,28},{24,16},{28,20},{1,9},{5... | collective-permute-start | bytes 2359304 | tf_op jit(solution)/shard_map/ppermute | solution.py:25
  (90 other events, 858.7 us)
Sparse Core Ops, SparseCore 0:
  72.0 31.7 all-gather.2

commit v5 on v4

v5 whole, which is shorter than its diff:
```python
import functools

import jax
import jax.numpy as jnp
from jax import lax
from jax.experimental import pallas as pl
from jax.experimental.pallas import tpu as pltpu
from jax.sharding import PartitionSpec as P

HEADS = 12
HEAD = 64
PAIR = 2 * HEAD
CORE = 1
CLIP = 128
WINDOW = 256
TILE = 256
VMEM_BYTES = 56 * 1024 * 1024
f32 = jnp.float32
bf16 = jnp.bfloat16
fence = lax.optimization_barrier


def swap(values, mask):
    count = lax.axis_size("dp")
    return lax.ppermute(values, "dp", [(i, i ^ mask) for i in range(count)])


def shift(values, step):
    count = lax.axis_size("fsdp")
    return lax.ppermute(values, "fsdp", [(i, (i + step) % count) for i in range(count)])


def link_masks():
    masks = []
    mask = 2
    while mask < lax.axis_size("dp"):
        masks.append(mask)
        mask *= 2
    return masks


def inner_swap(values, mask):
    count = lax.axis_size("fsdp")
    return lax.ppermute(values, "fsdp", [(i, i ^ mask) for i in range(count)])


def inner_double(held, mask):
    return inner_join(held, inner_swap(held, mask), mask)


def inner_join(held, came, mask):
    high = (lax.axis_index("fsdp") & mask) != 0
    return jnp.concatenate([jnp.where(high, came, held), jnp.where(high, held, came)])


def inner_rest(held):
    while held.shape[0] < lax.axis_size("fsdp"):
        held = inner_double(held, held.shape[0])
    return held


def inner_start(shard):
    return [shard] + [shift(shard, step) for step in range(1, lax.axis_size("fsdp"))]


def inner_order(came):
    count = len(came)
    me = lax.axis_index("fsdp")
    line = [came[count - 1 - k] for k in range(count)] + [came[count - k] for k in range(1, count)]
    return lax.dynamic_slice_in_dim(jnp.stack(line), count - 1 - me, count, 0)


def mirrored(role):
    masks = link_masks()
    return sum(masks[len(masks) - 1 - i] for i, mask in enumerate(masks) if role & mask)


def step_along(values, mask):
    count = lax.axis_size("dp")
    return lax.ppermute(values, "dp", [(i, i ^ (mirrored(mask) if i & CORE else mask)) for i in range(count)])


def top_bit(role):
    return 1 << (role.bit_length() - 1)


def relayed_roles():
    found = [role for role in range(2, lax.axis_size("dp"), 2) if role & (role - 1)]
    return sorted(found, key=lambda role: bin(role).count("1"))


def device_of(me, role, mirrors):
    holder = me ^ (role & CORE)
    link = role & ~CORE
    return holder ^ (link + lax.rem(holder, 2) * (mirrors[link] - link))


def mirror_table():
    return {role: mirrored(role) for role in range(0, lax.axis_size("dp"), 2)}


def single_steps(block):
    return {mask: step_along(block, mask) for mask in link_masks()}


def relay_steps(held):
    for role in relayed_roles():
        held[role] = step_along(held[role ^ top_bit(role)], top_bit(role))


def parts_of(pieces, total):
    return [pieces[e] for e in sorted(pieces)], tuple((e, 0, total) for e in sorted(pieces))


def core_steps(held):
    return {**held, **{e | CORE: swap(block, CORE) for e, block in held.items()}}


def inner_parts(inner):
    inner.add()
    return inner.parts


def add_low(a, b):
    return (a.astype(f32) + b.astype(f32)).astype(bf16)


class OuterSum:
    def __init__(self, *parts):
        self.parts = {2 * g: [part[g] for part in parts] for g in range(lax.axis_size("dp") // 2)}
        self.came = []

    def value(self, role, rows=slice(None)):
        total = self.parts[role][0][rows].astype(f32)
        for part in self.parts[role][1:]:
            total = total + part[rows].astype(f32)
        return total

    def relays(self):
        for role in relayed_roles()[::-1]:
            came = step_along(self.value(role).astype(bf16), top_bit(role))
            self.parts[role ^ top_bit(role)].append(came)

    def singles(self, rows=slice(None)):
        self.came.append((rows, [step_along(self.value(mask, rows).astype(bf16), mask) for mask in link_masks()]))

    def result(self, index=None):
        chosen = self.came if index is None else [self.came[index]]
        sums = []
        for rows, blocks in chosen:
            total = self.value(0, rows)
            for block in blocks:
                total = total + block.astype(f32)
            sums.append(total)
        return sums[0] if len(sums) == 1 else jnp.concatenate(sums)

    def state(self):
        return (self.parts, [blocks for _, blocks in self.came])

    def put(self, state):
        self.parts = state[0]
        self.came = [(rows, blocks) for (rows, _), blocks in zip(self.came, state[1])]


class InnerSum:
    def __init__(self, parts):
        self.parts = parts
        self.came = None
        self.mask = parts.shape[0]

    def step(self):
        self.add()
        self.mask //= 2
        bit = ((lax.axis_index("fsdp") & self.mask) != 0).astype(jnp.int32)
        halves = self.parts.reshape((2, self.mask) + self.parts.shape[1:])
        self.parts = lax.dynamic_index_in_dim(halves, bit, 0, keepdims=False)
        going = lax.dynamic_index_in_dim(halves, 1 - bit, 0, keepdims=False).astype(bf16)
        self.came = inner_swap(going, self.mask)

    def finish(self, steps=None):
        while self.mask > 1:
            self.step()

    def add(self):
        if self.came is not None:
            self.parts = self.parts + self.came.astype(f32)
            self.came = None

    def result(self):
        self.finish()
        self.add()
        return self.parts[0]


def nn(a, b):
    return jnp.dot(a, b, preferred_element_type=f32)


def nt(a, b):
    return lax.dot_general(a, b, (((1,), (1,)), ((), ())), preferred_element_type=f32)


def tn(a, b):
    return lax.dot_general(a, b, (((0,), (0,)), ((), ())), preferred_element_type=f32)


def tiles(size):
    step = TILE if size % TILE == 0 else size
    return [(at, step) for at in range(0, size, step)]


def centred(values):
    centre = jnp.mean(values, axis=-1, keepdims=True)
    shifted = values - centre
    spread = jnp.mean(shifted * shifted, axis=-1, keepdims=True)
    r = lax.rsqrt(spread + 1e-06)
    return shifted * r, r


def norm_back(xhat, r, gain, grad):
    c = grad * gain
    first = jnp.mean(c, axis=-1, keepdims=True)
    second = jnp.mean(c * xhat, axis=-1, keepdims=True)
    return r * (c - first - xhat * second), jnp.sum(grad * xhat, axis=0, keepdims=True)


def lower_half(rows):
    return lax.broadcasted_iota(jnp.int32, (rows, PAIR), 1) < HEAD


def two_heads(rows):
    keep = lower_half(rows.shape[0])
    zero = jnp.zeros_like(rows)
    return jnp.concatenate([jnp.where(keep, rows, zero), jnp.where(keep, zero, rows)], axis=0)


def side_by_side(stacked):
    rows = stacked.shape[0] // 2
    return jnp.where(lower_half(rows), stacked[:rows], stacked[rows:])


def softmax_rows(scores):
    raised = jnp.exp(scores - jnp.max(scores, axis=-1, keepdims=True))
    return raised / jnp.sum(raised, axis=-1, keepdims=True)


def bias_of(key_seg, own_seg):
    return jnp.where(key_seg == own_seg, 0.0, -1e30).astype(f32)


def block_bias(key_seg, ints, blocks):
    return jnp.stack([bias_of(key_seg[...], ints[1 + 3 * blocks + i]) for i in range(blocks)])


def biased(scores, bias):
    blocks, _, keys = bias.shape
    rows = scores.shape[0] // (2 * blocks)
    return (scores.reshape(2, blocks, rows, keys) + bias[None]).reshape(scores.shape)


def copies(jobs, sems, at):
    made = [pltpu.make_async_copy(src, dst, sems.at[at + i]) for i, (src, dst) in enumerate(jobs)]
    for job in made:
        job.start()
    return made


def whole(shape, dtype):
    return jax.ShapeDtypeStruct(shape, dtype)


VMEM = pl.BlockSpec(memory_space=pltpu.VMEM)
SMEM = pl.BlockSpec(memory_space=pltpu.SMEM)
ANY = pl.BlockSpec(memory_space=pl.ANY)


def params():
    return pltpu.CompilerParams(vmem_limit_bytes=VMEM_BYTES)


def cost(flops, moved, exps=0):
    return pl.CostEstimate(flops=int(flops), bytes_accessed=int(moved), transcendentals=int(exps))


def first_kernel(
    geometry, ints, mix, seg_row, tokens, *refs
):
    dp_count, blocks, token_places, qkv_places, qkv_rows, mirrors = geometry
    n_tok, n_qkv = len(token_places), len(qkv_places)
    token_refs, qkv_refs = refs[:n_tok], refs[n_tok : n_tok + n_qkv]
    blended_ref, qkv_ref, attended_ref, gains_ref, partner, weight, gain_parts, sems = refs[n_tok + n_qkv :]
    me = ints[0]
    width = tokens.shape[1]

    for b in range(blocks):
        holder, slot = ints[1 + b], ints[1 + blocks + b]
        for ref, (role, _, rows) in zip(token_refs, token_places):

            @pl.when(holder == device_of(me, role, mirrors))
            def _(ref=ref, rows=rows, b=b, slot=slot):
                at = pl.multiple_of(slot * CLIP, CLIP)
                pltpu.make_async_copy(ref.at[pl.ds(at, CLIP)], partner.at[b], sems.at[b]).start()

    jobs = []
    for ref, (e, start, rows) in zip(qkv_refs, qkv_places):
        take = min(rows, qkv_rows - start)
        at = pl.multiple_of(device_of(me, e, mirrors) * qkv_rows + start, 16)
        jobs.append((ref.at[pl.ds(0, take)], weight.at[pl.ds(at, take)]))
        if start + rows > qkv_rows:
            jobs.append((ref.at[pl.ds(take, rows - take)], gain_parts.at[e]))
    made = copies(jobs, sems, blocks)
    for b in range(blocks):
        pltpu.make_async_copy(tokens.at[pl.ds(0, CLIP)], partner.at[b], sems.at[b]).wait()
    for b in range(blocks):
        rows = slice(b * CLIP, (b + 1) * CLIP)
        share = mix[b]
        blended_ref[rows, :] = share * tokens[rows, :].astype(f32) + (1.0 - share) * partner[b].astype(f32)
    for job in made:
        job.wait()
    gains = gain_parts[0].astype(f32)
    for e in range(1, dp_count):
        gains = gains + gain_parts[e].astype(f32)
    gains_ref[...] = gains[:8]
    xhat, _ = centred(blended_ref[...])
    normed = (xhat * gains[0:1]).astype(bf16)
    for at, step in tiles(3 * width):
        tile = nt(normed, weight[at : at + step, :])
        if at + step <= width:
            tile = tile * 0.125
        qkv_ref[:, at : at + step] = tile.astype(bf16)

    @pl.loop(0, blocks)
    def _(i):
        window = pl.multiple_of(ints[1 + 2 * blocks + i] * CLIP, CLIP)
        bias = bias_of(seg_row[:, pl.ds(window, WINDOW)], ints[1 + 3 * blocks + i])
        rows = pl.ds(pl.multiple_of(i * CLIP, CLIP), CLIP)
        keys = pl.ds(window, WINDOW)
        for at in range(0, width, PAIR):
            queries = two_heads(qkv_ref[rows, at : at + PAIR])
            probs = softmax_rows(nt(queries, qkv_ref[keys, width + at : width + at + PAIR]) + bias).astype(bf16)
            out = nn(probs, qkv_ref[keys, 2 * width + at : 2 * width + at + PAIR])
            attended_ref[rows, at : at + PAIR] = side_by_side(out).astype(bf16)


def load_cross(me, refs, places, layout, weights, sems, mirrors):
    jobs = []
    for ref, (e, start, rows) in zip(refs, places):
        for (first, size), weight in zip(layout, weights):
            if weight is not None and first >= start and first + size <= start + rows:
                at = pl.multiple_of(device_of(me, e, mirrors) * size, 16)
                jobs.append((ref.at[pl.ds(first - start, size)], weight.at[pl.ds(at, size)]))
    return copies(jobs, sems, 0)


def second_kernel(geometry, ints, coarse_seg, coarse, blended, attended, gains, *refs):
    blocks, places, layout, mirrors = geometry
    weight_refs = refs[: len(places)]
    residual_ref, cq_ref, ckv_ref, crossed_ref, joined_ref, second_ref = refs[len(places) : len(places) + 6]
    w_ckv, w_out, w_cq, w_cout, sems = refs[len(places) + 6 :]
    made = load_cross(ints[0], weight_refs, places, layout, (w_ckv, w_out, w_cq, w_cout), sems, mirrors)
    for job in made:
        job.wait()
    width = blended.shape[1]
    for at, step in tiles(2 * width):
        ckv_ref[:, at : at + step] = nt(coarse[...], w_ckv[at : at + step, :]).astype(bf16)
    for at, step in tiles(width):
        residual_ref[:, at : at + step] = blended[:, at : at + step] + nn(attended[...], w_out[:, at : at + step])
    xhat, _ = centred(residual_ref[...])
    crossed_in = (xhat * gains[1:2]).astype(bf16)
    for at, step in tiles(width):
        cq_ref[:, at : at + step] = (nn(crossed_in, w_cq[:, at : at + step]) * 0.125).astype(bf16)

    bias = block_bias(coarse_seg, ints, blocks)
    for at in range(0, width, PAIR):
        queries = two_heads(cq_ref[:, at : at + PAIR])
        probs = softmax_rows(biased(nt(queries, ckv_ref[:, at : at + PAIR]), bias)).astype(bf16)
        out = nn(probs, ckv_ref[:, width + at : width + at + PAIR])
        crossed_ref[:, at : at + PAIR] = side_by_side(out).astype(bf16)

    for at, step in tiles(width):
        joined_ref[:, at : at + step] = residual_ref[:, at : at + step] + nn(crossed_ref[...], w_cout[:, at : at + step])
    xhat, _ = centred(joined_ref[...])
    second_ref[...] = (xhat * gains[2:3]).astype(bf16)


def mlp_kernel(geometry, second, second_near, cotangent, cotangent_near, *refs):
    groups, places, rows, last = geometry
    weight_refs = refs[: len(places)]
    refs = refs[len(places) :]
    keep_ref, going_ref = refs[:2]
    if last:
        own_ref = refs[2]
        sums = refs[3:7]
        refs = refs[7:]
    else:
        sums = refs[2:6]
        refs = refs[6:]
    w_up, w_down, hidden, grad_pre, sems = refs
    step = pl.program_id(0)

    def jobs_of(group):
        jobs = []
        for ref, (e, which) in zip(weight_refs, places):
            if e == groups[group]:
                for part, weight in ((0, w_up), (1, w_down)):
                    if which is None or which == part:
                        first = part * rows if which is None else 0
                        jobs.append((ref.at[pl.ds(first, rows)], weight.at[group]))
        return jobs

    at = 0
    for group in range(len(groups)):
        jobs = jobs_of(group)
        made = [pltpu.make_async_copy(s, d, sems.at[at + i]) for i, (s, d) in enumerate(jobs)]
        at += len(jobs)

        @pl.when(step == 0)
        def _(made=made):
            for job in made:
                job.start()

        @pl.when(step == group)
        def _(made=made):
            for job in made:
                job.wait()

    @pl.when(step == 0)
    def _():
        for ref in sums:
            ref[...] = jnp.zeros_like(ref)

    up, down = w_up.at[step], w_down.at[step]
    for half, (inputs, upstream) in enumerate(((second, cotangent), (second_near, cotangent_near))):
        pre = nt(inputs[...], up[...])
        grad_hidden = nt(upstream[...], down[...])
        cdf = 0.5 * (1.0 + lax.erf(pre * 0.7071067811865476))
        slope = cdf + pre * (jnp.exp(-0.5 * pre * pre) * 0.3989422804014327)
        hidden[half] = (pre * cdf).astype(bf16)
        grad_pre[half] = (grad_hidden * slope).astype(bf16)
        for first, size in tiles(second.shape[1]):
            columns = slice(first, first + size)
            sums[2 * half][:, columns] += nn(hidden[half], down[:, columns])
            sums[2 * half + 1][:, columns] += nn(grad_pre[half], up[:, columns])
    keep_ref[0, 0] = (tn(grad_pre[0], second[...]) + tn(grad_pre[1], second_near[...])).astype(bf16)
    keep_ref[0, 1] = (tn(hidden[0], cotangent[...]) + tn(hidden[1], cotangent_near[...])).astype(bf16)

    @pl.when(step == len(groups) - 1)
    def _():
        going_ref[0] = sums[2][...].astype(bf16)
        going_ref[1] = sums[3][...].astype(bf16)
        if last:
            own_ref[0] = sums[0][...].astype(bf16)
            own_ref[1] = sums[1][...].astype(bf16)


def grads_out(me, dp_count, layout, sources, keep_ref, send_ref, sems, at, mirrors):
    jobs = []
    for e in range(dp_count):
        target = send_ref if e & CORE else keep_ref
        for (first, size), source in zip(layout, sources):
            if source is None:
                continue
            row = pl.multiple_of(device_of(me, e, mirrors) * size, 16)
            jobs.append((source.at[pl.ds(row, size)], target.at[e // 2, pl.ds(first, size)]))
    return copies(jobs, sems, at)


def third_kernel(
    geometry, ints, coarse_seg, gains, mlp_out, grad_second, own_b, came_a, came_b, joined, cotangent, crossed, cq, ckv, *refs
):
    blocks, places, layout, dp_count, mirrors = geometry
    weight_refs = refs[: len(places)]
    refs = refs[len(places) :]
    output_ref, grad_joined_ref, grad_cq_ref, grad_ckv_ref, gain_grads_ref, keep_ref, send_ref = refs[:7]
    w_cout, g_cout, grad_cross, sems = refs[7:]
    me = ints[0]
    width = joined.shape[1]
    made = load_cross(me, weight_refs, places, layout, (None, None, None, w_cout), sems, mirrors)
    rest = [own_b[i].astype(f32) + came_a[i].astype(f32) + came_b[i].astype(f32) for i in range(2)]
    output_ref[...] = (joined[...] + (mlp_out[...] + rest[0])).astype(bf16)
    xhat, r = centred(joined[...])
    grad_in, gain_two = norm_back(xhat, r, gains[2:3], grad_second[...] + rest[1])
    grad_joined_ref[...] = cotangent[...].astype(f32) + grad_in
    low = grad_joined_ref[...].astype(bf16)
    for job in made:
        job.wait()
    for at, step in tiles(width):
        grad_cross[:, at : at + step] = nt(low, w_cout[at : at + step, :]).astype(bf16)
    for at, step in tiles(width):
        g_cout[at : at + step, :] = tn(crossed[:, at : at + step], low).astype(bf16)
    going = grads_out(me, dp_count, layout, (None, None, None, g_cout), keep_ref, send_ref, sems, len(made), mirrors)
    bias = block_bias(coarse_seg, ints, blocks)
    for at in range(0, width, PAIR):
        lanes = slice(at, at + PAIR)
        queries = two_heads(cq[:, lanes])
        grads = two_heads(grad_cross[:, lanes])
        keys = ckv[:, lanes]
        values = ckv[:, width + at : width + at + PAIR]
        probs = softmax_rows(biased(nt(queries, keys), bias))
        grad_ckv_ref[:, width + at : width + at + PAIR] = tn(probs.astype(bf16), grads).astype(bf16)
        grad_probs = nt(grads, values)
        inner = jnp.sum(probs * grad_probs, axis=-1, keepdims=True)
        scores = (probs * (grad_probs - inner)).astype(bf16)
        part = side_by_side(nn(scores, keys)).astype(bf16)
        grad_cq_ref[:, lanes] = part * jnp.asarray(0.125, bf16)
        grad_ckv_ref[:, lanes] = tn(scores, queries).astype(bf16)

    gain_grads_ref[...] = jnp.concatenate([gain_two] * 8, axis=0)
    for job in going:
        job.wait()


def third_part(geometry, ints, coarse, gains, gain_two, grad_joined, residual, attended, grad_cq, grad_ckv, keep_in, send_in, *refs):
    places, layout, dp_count, mirrors = geometry
    weight_refs = refs[: len(places)]
    refs = refs[len(places) :]
    coarse_ref, grad_res_ref, grad_att_ref, gain_grads_ref, keep_ref, send_ref = refs[:6]
    w_ckv, w_out, w_cq, g_ckv, g_out, g_cq, crossed_in, sems = refs[6:]
    me = ints[0]
    width = residual.shape[1]
    made = load_cross(me, weight_refs, places, layout, (w_ckv, w_out, w_cq, None), sems, mirrors)
    xhat, r = centred(residual[...])
    crossed_in[...] = (xhat * gains[1:2]).astype(bf16)
    for at, step in tiles(width):
        g_cq[at : at + step, :] = tn(crossed_in[:, at : at + step], grad_cq[...]).astype(bf16)
    for at, step in tiles(2 * width):
        g_ckv[at : at + step, :] = tn(grad_ckv[:, at : at + step], coarse[...]).astype(bf16)
    for job in made:
        job.wait()
    going = grads_out(me, dp_count, layout, (g_ckv, None, g_cq, None), keep_ref, send_ref, sems, 0, mirrors)
    for at, step in tiles(width):
        coarse_ref[:, at : at + step] = nn(grad_ckv[:, 0:width], w_ckv[0:width, at : at + step]) + nn(
            grad_ckv[:, width : 2 * width], w_ckv[width : 2 * width, at : at + step]
        )
    pieces = [nt(grad_cq[...], w_cq[at : at + step, :]) for at, step in tiles(width)]
    grad_in, gain_cross = norm_back(xhat, r, gains[1:2], jnp.concatenate(pieces, axis=1))
    grad_res = grad_joined[...] + grad_in
    grad_res_ref[...] = grad_res
    low = grad_res.astype(bf16)
    for at, step in tiles(width):
        g_out[at : at + step, :] = tn(attended[:, at : at + step], low).astype(bf16)
    going += grads_out(me, dp_count, layout, (None, g_out, None, None), keep_ref, send_ref, sems, len(going), mirrors)
    for at, step in tiles(width):
        grad_att_ref[:, at : at + step] = nt(low, w_out[at : at + step, :]).astype(bf16)
    zero = jnp.zeros_like(gain_cross)
    gain_grads_ref[...] = jnp.concatenate([zero, gain_cross, gain_two[0:1]] + [zero] * 5, axis=0)
    for job in going:
        job.wait()


def fourth_kernel(geometry, ints, seg_row, grad_att, qkv, *refs):
    blocks, first, last = geometry
    grad_proj, query_part, key_part, value_part, key_sum, value_sum, sems = refs[-7:]
    width = grad_att.shape[1]
    low, high = first * PAIR, last * PAIR
    key_sum[...] = jnp.zeros_like(key_sum)
    value_sum[...] = jnp.zeros_like(value_sum)

    @pl.loop(0, blocks)
    def _(i):
        window = pl.multiple_of(ints[1 + 2 * blocks + i] * CLIP, CLIP)
        bias = bias_of(seg_row[:, pl.ds(window, WINDOW)], ints[1 + 3 * blocks + i])
        rows = pl.ds(pl.multiple_of(i * CLIP, CLIP), CLIP)
        near = pl.ds(window, WINDOW)
        for at in range(low, high, PAIR):
            lanes = slice(at - low, at - low + PAIR)
            queries = two_heads(qkv[rows, at : at + PAIR])
            grads = two_heads(grad_att[rows, at : at + PAIR])
            keys = qkv[near, width + at : width + at + PAIR]
            values = qkv[near, 2 * width + at : 2 * width + at + PAIR]
            probs = softmax_rows(nt(queries, keys) + bias)
            value_sum[near, lanes] += tn(probs.astype(bf16), grads)
            grad_probs = nt(grads, values)
            inner = jnp.sum(probs * grad_probs, axis=-1, keepdims=True)
            scores = (probs * (grad_probs - inner)).astype(bf16)
            part = side_by_side(nn(scores, keys)).astype(bf16)
            query_part[rows, lanes] = part * jnp.asarray(0.125, bf16)
            key_sum[near, lanes] += tn(scores, queries)

    key_part[...] = key_sum[...].astype(bf16)
    value_part[...] = value_sum[...].astype(bf16)
    jobs = [
        (part, grad_proj.at[:, pl.ds(i * width + low, high - low)])
        for i, part in enumerate((query_part, key_part, value_part))
    ]
    for job in copies(jobs, sems, 0):
        job.wait()


def fifth_kernel(geometry, ints, mix, gains, blended, grad_res, grad_proj, *refs):
    dp_count, blocks, qkv_places, qkv_rows, mirrors = geometry
    weight_refs = refs[: len(qkv_places)]
    refs = refs[len(qkv_places) :]
    base_ref, going_ref = refs[:2]
    weight, sems = refs[2:]
    me = ints[0]
    width = blended.shape[1]
    jobs = []
    for ref, (e, start, rows) in zip(weight_refs, qkv_places):
        take = min(rows, qkv_rows - start)
        at = pl.multiple_of(device_of(me, e, mirrors) * qkv_rows + start, 16)
        jobs.append((ref.at[pl.ds(0, take)], weight.at[pl.ds(at, take)]))
    made = copies(jobs, sems, 0)
    xhat, r = centred(blended[...])
    for job in made:
        job.wait()
    pieces = [nn(grad_proj[...], weight[:, at : at + step]) for at, step in tiles(width)]
    grad_in, _ = norm_back(xhat, r, gains[0:1], jnp.concatenate(pieces, axis=1))
    grad_blend = grad_res[...] + grad_in
    for b in range(blocks):
        rows = slice(b * CLIP, (b + 1) * CLIP)
        share = mix[b]
        part = grad_blend[rows, :]
        base_ref[rows, :] = share * part
        going_ref[rows, :] = ((1.0 - share) * part).astype(bf16)


def place_kernel(geometry, ints, ints_near, blocks_own, blocks_near, out_ref):
    blocks, mirrors = geometry
    me = ints[0]
    out_ref[...] = jnp.zeros_like(out_ref)
    for table, first, source in ((ints, 1, blocks_own), (ints_near, 0, blocks_near)):
        for b in range(blocks):
            holder, slot = table[first + b], table[first + blocks + b]
            group = jnp.int32(0)
            for role in mirrors:
                group = group + jnp.where(device_of(me, role, mirrors) == holder, role // 2, 0)

            @pl.when(lax.rem(holder, 2) == lax.rem(me, 2))
            def _(group=group, slot=slot, source=source, b=b):
                rows = pl.ds(pl.multiple_of(slot * CLIP, CLIP), CLIP)
                part = source[b * CLIP : (b + 1) * CLIP, :].astype(f32)
                out_ref[group, rows, :] = (out_ref[group, rows, :].astype(f32) + part).astype(bf16)


def sixth_kernel(geometry, ints, gains, gain_grads, blended, grad_proj, *refs):
    dp_count, qkv_places, qkv_rows, mirrors = geometry
    weight_refs = refs[: len(qkv_places)]
    keep_ref, send_ref, weight, grad_w, gain_rows, sems = refs[len(qkv_places) :]
    me = ints[0]
    width = blended.shape[1]
    jobs = []
    for ref, (e, start, rows) in zip(weight_refs, qkv_places):
        take = min(rows, qkv_rows - start)
        at = pl.multiple_of(device_of(me, e, mirrors) * qkv_rows + start, 16)
        jobs.append((ref.at[pl.ds(0, take)], weight.at[pl.ds(at, take)]))
    made = copies(jobs, sems, 0)
    xhat, _ = centred(blended[...])
    normed = (xhat * gains[0:1]).astype(bf16)
    for job in made:
        job.wait()
    gain_one = jnp.zeros((1, width), f32)
    for at, step in tiles(3 * width):
        part = tn(grad_proj[:, at : at + step], normed)
        gain_one = gain_one + jnp.sum(part * weight[at : at + step, :].astype(f32), axis=0, keepdims=True)
        grad_w[at : at + step, :] = part.astype(bf16)
    sent = grads_out(me, dp_count, ((0, qkv_rows),), (grad_w,), keep_ref, send_ref, sems, len(jobs), mirrors)
    all_gains = jnp.concatenate([gain_one / gains[0:1], gain_grads[1:8], jnp.zeros((8, width), f32)], axis=0)
    gain_rows[...] = all_gains.astype(bf16)
    last = []
    for e in range(dp_count):
        target = send_ref if e & CORE else keep_ref
        last.append((gain_rows, target.at[e // 2, pl.ds(qkv_rows, 16)]))
    for job in sent + copies(last, sems, len(jobs) + dp_count):
        job.wait()


def shards(
    tokens,
    coarse_view,
    segment_ids,
    partner_device,
    partner_slot,
    mix_weight,
    ln1_gain,
    w_qkv,
    w_out,
    lnx_gain,
    w_cq,
    w_ckv,
    w_cout,
    ln2_gain,
    w_up,
    w_down,
    cotangent,
):
    row_count, width = tokens.shape
    coarse_rows = coarse_view.shape[0]
    blocks = mix_weight.shape[0]
    dp_count, fsdp_count = lax.axis_size("dp"), lax.axis_size("fsdp")
    dp_me, fsdp_me = lax.axis_index("dp"), lax.axis_index("fsdp")
    part = ln1_gain.shape[0]
    device_me = dp_me * fsdp_count + fsdp_me
    pairs = dp_count // 2
    mirrors = mirror_table()

    target = partner_device[:, 0]
    segments = segment_ids[0]
    videos = segments.reshape(blocks, row_count // blocks)[:, 0]
    following = jnp.concatenate([videos[1:] == videos[:-1], jnp.zeros((1,), bool)])
    before = jnp.concatenate([jnp.zeros((1,), bool), videos[1:] == videos[:-1]])
    index = jnp.arange(blocks, dtype=jnp.int32)
    window = jnp.where(following, index, jnp.where(before, index - 1, jnp.minimum(index, blocks - 2)))
    ints = jnp.concatenate(
        [dp_me[None].astype(jnp.int32), target, partner_slot, window, videos]
    )
    ints_near = swap(ints[1 : 1 + 2 * blocks], CORE)
    seg_row = segments[None, :]
    coarse_seg = segments.reshape(coarse_rows, row_count // coarse_rows)[:, 0][None, :]

    gain_rows = lax.dynamic_update_slice(
        jnp.zeros((8, width), bf16), jnp.stack([ln1_gain, lnx_gain, ln2_gain]), (0, device_me * part)
    )
    shard_one = jnp.concatenate([w_qkv.T, gain_rows])
    shard_two = jnp.concatenate([w_ckv.T, w_out, w_cq, w_cout])
    shard_mlp = jnp.concatenate([w_up.T, w_down])
    sizes_two = (w_ckv.shape[1], w_out.shape[0], w_cq.shape[0], w_cout.shape[0])
    qkv_part, up_part = w_qkv.shape[1], w_up.shape[1]
    qkv_rows, up_rows = qkv_part * fsdp_count, up_part * fsdp_count
    layout = []
    at = 0
    for size in sizes_two:
        layout.append((at * fsdp_count, size * fsdp_count))
        at += size
    layout = tuple(layout)
    rows_two = at * fsdp_count

    held_tok = {0: tokens, **single_steps(tokens)}
    came_one = inner_start(shard_one)
    held_tok, came_one, shard_two = fence((held_tok, came_one, shard_two))

    ones = inner_order(came_one)
    gain_block = jnp.sum(ones[:, qkv_part:].astype(f32), axis=0).astype(bf16)
    block_one = jnp.concatenate(
        [ones[:, :qkv_part].reshape(qkv_rows, width), gain_block, jnp.zeros((8, width), bf16)]
    )
    held_one = {0: block_one, **single_steps(block_one)}
    came_two = inner_start(shard_two)
    held_tok, held_one, came_two, shard_mlp = fence((held_tok, held_one, came_two, shard_mlp))

    mlp = inner_double(shard_mlp[None], 1)
    core_tok = core_steps(dict(held_tok))
    near_tok = set(held_tok)
    relay_steps(held_tok)
    twos = inner_order(came_two)
    split = []
    at = 0
    for size in sizes_two:
        split.append(twos[:, at : at + size].reshape(size * fsdp_count, width))
        at += size
    block_two = jnp.concatenate(split)
    held_one, core_tok, held_tok, block_two, mlp = fence((held_one, core_tok, held_tok, block_two, mlp))

    cuts = (0, 2 * up_part // 3, 5 * up_part // 3, 2 * up_part)
    mlp_cut = [mlp[:, first:last] for first, last in zip(cuts, cuts[1:])]
    mlp_came = [inner_swap(mlp_cut[0], 2)]
    core_one = core_steps(dict(held_one))
    relay_steps(held_one)
    late_tok = core_steps({e: b for e, b in held_tok.items() if e not in near_tok})
    held_one, core_one, late_tok, block_two, mlp_cut, mlp_came = fence(
        (held_one, core_one, late_tok, block_two, mlp_cut, mlp_came)
    )

    held_two = {0: block_two, **single_steps(block_two)}
    cotangent_near = swap(cotangent, CORE)
    mlp_came.append(inner_swap(mlp_cut[1], 2))
    late_one = core_steps({e: b for e, b in held_one.items() if e not in near_tok})
    pieces_tok = {**core_tok, **late_tok}
    pieces_one = {**core_one, **late_one}
    arrays_tok, places_tok = parts_of(pieces_tok, row_count)
    arrays_one, places_one = parts_of(pieces_one, qkv_rows + 16)
    blended, qkv, attended, gains = pl.pallas_call(
        functools.partial(first_kernel, (dp_count, blocks, places_tok, places_one, qkv_rows, mirrors)),
        out_shape=(
            whole((row_count, width), f32),
            whole((row_count, 3 * width), bf16),
            whole((row_count, width), bf16),
            whole((8, width), f32),
        ),
        in_specs=[SMEM, SMEM, VMEM, VMEM] + [ANY] * (len(arrays_tok) + len(arrays_one)),
        out_specs=(VMEM,) * 4,
        scratch_shapes=[
            pltpu.VMEM((blocks, CLIP, width), bf16),
            pltpu.VMEM((3 * width, width), bf16),
            pltpu.VMEM((dp_count, 16, width), bf16),
            pltpu.SemaphoreType.DMA((blocks + len(arrays_one) + dp_count,)),
        ],
        compiler_params=params(),
        cost_estimate=cost(1e9, 1e6),
        name="mix_self_attention",
    )(ints, mix_weight, seg_row, tokens, *arrays_tok, *arrays_one)
    held_two, attended, mlp_came, cotangent_near, mlp_cut = fence((held_two, attended, mlp_came, cotangent_near, mlp_cut))

    core_two = core_steps(dict(held_two))
    relay_steps(held_two)
    mlp_came.append(inner_swap(mlp_cut[2], 2))
    held_two, core_two, mlp_came, ints_near = fence((held_two, core_two, mlp_came, ints_near))

    mlp = jnp.concatenate([inner_rest(inner_join(cut, came, 2)) for cut, came in zip(mlp_cut, mlp_came)], axis=1)
    block_mlp = jnp.concatenate([mlp[:, :up_part].reshape(up_rows, width), mlp[:, up_part:].reshape(up_rows, width)])
    held_mlp = {0: block_mlp, **single_steps(block_mlp)}
    late_two = core_steps({e: b for e, b in held_two.items() if e not in near_tok})
    pieces_two = {**core_two, **late_two}
    wide = [pltpu.VMEM((sizes * fsdp_count * dp_count, width), bf16) for sizes in sizes_two]
    n_two = 4 * dp_count
    arrays_two, places_two = parts_of(pieces_two, rows_two)
    wide = [pltpu.VMEM((sizes * fsdp_count * dp_count, width), bf16) for sizes in sizes_two]
    n_two = 4 * dp_count
    residual, cq, ckv, crossed, joined, second = pl.pallas_call(
        functools.partial(second_kernel, (blocks, places_two, layout, mirrors)),
        out_shape=(
            whole((row_count, width), f32),
            whole((row_count, width), bf16),
            whole((coarse_rows, 2 * width), bf16),
            whole((row_count, width), bf16),
            whole((row_count, width), f32),
            whole((row_count, width), bf16),
        ),
        in_specs=[SMEM] + [VMEM] * 5 + [ANY] * len(arrays_two),
        out_specs=(VMEM,) * 6,
        scratch_shapes=wide + [pltpu.SemaphoreType.DMA((n_two,))],
        compiler_params=params(),
        cost_estimate=cost(1e9, 1e6),
        name="cross_attention",
    )(ints, coarse_seg, coarse_view, blended, attended, gains, *arrays_two)
    second_near = swap(second, CORE)
    held_mlp, second, second_near = fence((held_mlp, second, second_near))

    early = dict(held_mlp)
    relay_steps(held_mlp)

    def mlp_call(pieces, last):
        groups = tuple(sorted(pieces))
        count = len(groups)
        fixed = pl.BlockSpec((row_count, width), lambda g: (0, 0))
        moving = pl.BlockSpec((1, 2, up_rows, width), lambda g: (g, 0, 0, 0))
        both = pl.BlockSpec((2, row_count, width), lambda g: (0, 0, 0))
        table = whole((row_count, width), f32)
        out_shape = [whole((count, 2, up_rows, width), bf16), whole((2, row_count, width), bf16)]
        out_specs = [moving, both]
        scratch = [pltpu.VMEM((row_count, width), f32)] * (4 if last else 2)
        if last:
            out_shape.append(whole((2, row_count, width), bf16))
            out_specs.append(both)
        else:
            out_shape += [table, table]
            out_specs += [fixed, fixed]
        made = pl.pallas_call(
            functools.partial(mlp_kernel, (groups, tuple((e, None) for e in groups), up_rows, last)),
            grid=(count,),
            out_shape=tuple(out_shape),
            in_specs=[fixed] * 4 + [ANY] * count,
            out_specs=tuple(out_specs),
            scratch_shapes=scratch
            + [
                pltpu.VMEM((count, up_rows, width), bf16),
                pltpu.VMEM((count, up_rows, width), bf16),
                pltpu.VMEM((2, row_count, up_rows), bf16),
                pltpu.VMEM((2, row_count, up_rows), bf16),
                pltpu.SemaphoreType.DMA((2 * count,)),
            ],
            compiler_params=params(),
            cost_estimate=cost(1e9, 1e6),
            name="feed_forward",
        )(second, second_near, cotangent, cotangent_near, *[pieces[e] for e in groups])
        return groups, made[0].reshape(count, 2 * up_rows, width), made[1], made[2:]

    groups_a, keep_a, going_a, (mlp_out, grad_second) = mlp_call(early, False)
    late = {e: b for e, b in held_mlp.items() if e not in near_tok}
    late, keep_a, going_a, mlp_out, grad_second = fence((late, keep_a, going_a, mlp_out, grad_second))
    came_a = swap(going_a, CORE)
    groups_b, keep_b, going_b, (own_b,) = mlp_call(late, True)
    came_a, keep_b, going_b, own_b = fence((came_a, keep_b, going_b, own_b))
    came_b = swap(going_b, CORE)
    totals = [None] * pairs
    for groups, keep in ((groups_a, keep_a), (groups_b, keep_b)):
        for i, e in enumerate(groups):
            totals[e // 2] = keep[i]
    totals, came_b = fence((totals, came_b))

    sum_mlp = OuterSum(totals)
    sum_mlp.relays()
    output, grad_joined, grad_cq, grad_ckv, gain_two, keep_two, send_two = pl.pallas_call(
        functools.partial(third_kernel, (blocks, places_two, layout, dp_count, mirrors)),
        out_shape=(
            whole((row_count, width), bf16),
            whole((row_count, width), f32),
            whole((row_count, width), bf16),
            whole((coarse_rows, 2 * width), bf16),
            whole((8, width), f32),
            whole((pairs, rows_two, width), bf16),
            whole((pairs, rows_two, width), bf16),
        ),
        in_specs=[SMEM] + [VMEM] * 12 + [ANY] * len(arrays_two),
        out_specs=(VMEM,) * 5 + (ANY,) * 2,
        scratch_shapes=[
            wide[3],
            wide[3],
            pltpu.VMEM((row_count, width), bf16),
            pltpu.SemaphoreType.DMA((n_two + dp_count,)),
        ],
        compiler_params=params(),
        cost_estimate=cost(1e9, 1e6),
        name="cross_attention_backward",
    )(ints, coarse_seg, gains, mlp_out, grad_second, own_b, came_a, came_b, joined, cotangent, crossed, cq, ckv, *arrays_two)
    state, grad_joined = fence((sum_mlp.state(), grad_joined))
    sum_mlp.put(state)

    sum_mlp.singles(slice(0, up_rows))
    coarse_grad, grad_res, grad_att, gain_grads, keep_two, send_two = pl.pallas_call(
        functools.partial(third_part, (places_two, layout, dp_count, mirrors)),
        out_shape=(
            whole((coarse_rows, width), f32),
            whole((row_count, width), f32),
            whole((row_count, width), bf16),
            whole((8, width), f32),
            whole((pairs, rows_two, width), bf16),
            whole((pairs, rows_two, width), bf16),
        ),
        in_specs=[SMEM] + [VMEM] * 8 + [ANY] * (2 + len(arrays_two)),
        out_specs=(VMEM,) * 4 + (ANY,) * 2,
        scratch_shapes=[
            wide[0],
            wide[1],
            wide[2],
            wide[0],
            wide[1],
            wide[2],
            pltpu.VMEM((row_count, width), bf16),
            pltpu.SemaphoreType.DMA((n_two,)),
        ],
        input_output_aliases={9: 4, 10: 5},
        compiler_params=params(),
        cost_estimate=cost(1e9, 1e6),
        name="cross_attention_weights",
    )(
        ints, coarse_view, gains, gain_two, grad_joined, residual, attended, grad_cq, grad_ckv, keep_two, send_two, *arrays_two
    )

    state, grad_att, keep_two, send_two = fence((sum_mlp.state(), grad_att, keep_two, send_two))
    sum_mlp.put(state)

    sum_mlp.singles(slice(up_rows, 2 * up_rows))
    came_two = swap(send_two, CORE)
    def attention_back(first, last, held):
        columns = (last - first) * PAIR
        return pl.pallas_call(
            functools.partial(fourth_kernel, (blocks, first, last)),
            out_shape=whole((row_count, 3 * width), bf16),
            in_specs=[SMEM] + [VMEM] * 3 + [ANY] * len(held),
            out_specs=ANY,
            scratch_shapes=[pltpu.VMEM((row_count, columns), bf16)] * 3
            + [pltpu.VMEM((row_count, columns), f32)] * 2
            + [pltpu.SemaphoreType.DMA((3,))],
            input_output_aliases={4: 0} if held else {},
            compiler_params=params(),
            cost_estimate=cost(1e9, 1e6),
            name="self_attention_backward",
        )(ints, seg_row, grad_att, qkv, *held)

    grad_proj = attention_back(0, HEADS // 2, ())
    state, came_two, grad_proj = fence((sum_mlp.state(), came_two, grad_proj))
    sum_mlp.put(state)

    sum_two = OuterSum(keep_two, came_two)
    sum_two.relays()
    inner_up = InnerSum(sum_mlp.result(0).reshape(fsdp_count, up_part, width))
    inner_up.step()
    keep_one, send_one = pl.pallas_call(
        functools.partial(sixth_kernel, (dp_count, places_one, qkv_rows, mirrors)),
        out_shape=(
            whole((pairs, qkv_rows + 16, width), bf16),
            whole((pairs, qkv_rows + 16, width), bf16),
        ),
        in_specs=[SMEM] + [VMEM] * 4 + [ANY] * len(arrays_one),
        out_specs=(ANY,) * 2,
        scratch_shapes=[
            pltpu.VMEM((3 * width, width), bf16),
            pltpu.VMEM((3 * width, width), bf16),
            pltpu.VMEM((16, width), bf16),
            pltpu.SemaphoreType.DMA((len(arrays_one) + 2 * dp_count,)),
        ],
        compiler_params=params(),
        cost_estimate=cost(1e9, 1e6),
        name="self_attention_weights",
    )(ints, gains, gain_grads, blended, grad_proj, *arrays_one)
    state, keep_one, send_one, up_came = fence((sum_two.state(), keep_one, send_one, inner_up.came))
    sum_two.put(state)
    inner_up.came = up_came

    sum_two.singles()
    inner_down = InnerSum(sum_mlp.result(1).reshape(fsdp_count, up_part, width))
    inner_down.step()
    came_one = swap(send_one, CORE)
    base, going_tok = pl.pallas_call(
        functools.partial(fifth_kernel, (dp_count, blocks, places_one, qkv_rows, mirrors)),
        out_shape=(
            whole((row_count, width), f32),
            whole((row_count, width), bf16),
        ),
        in_specs=[SMEM, SMEM] + [VMEM] * 4 + [ANY] * len(arrays_one),
        out_specs=(VMEM,) * 2,
        scratch_shapes=[
            pltpu.VMEM((3 * width, width), bf16),
            pltpu.SemaphoreType.DMA((len(arrays_one),)),
        ],
        compiler_params=params(),
        cost_estimate=cost(1e9, 1e6),
        name="self_attention_input",
    )(ints, mix_weight, gains, blended, grad_res, grad_proj, *arrays_one)
    state, came_one, going_tok, down_came = fence((sum_two.state(), came_one, going_tok, inner_down.came))
    sum_two.put(state)
    inner_down.came = down_came

    sum_one = OuterSum(keep_one, came_one)
    sum_one.relays()
    came_tok = swap(going_tok, CORE)
    placed = pl.pallas_call(
        functools.partial(place_kernel, (blocks, mirrors)),
        out_shape=whole((pairs, row_count, width), bf16),
        in_specs=[SMEM, SMEM] + [VMEM] * 2,
        out_specs=VMEM,
        compiler_params=params(),
        cost_estimate=cost(1e9, 1e6),
        name="place_partner_gradients",
    )(ints, ints_near, going_tok, came_tok)
    mlp_parts = jnp.concatenate([inner_parts(inner_up), inner_parts(inner_down)], axis=1)
    inner_mlp = InnerSum(mlp_parts)
    inner_mlp.finish()
    state, placed, mlp_came = fence((sum_one.state(), placed, inner_mlp.came))
    sum_one.put(state)
    inner_mlp.came = mlp_came

    sum_one.singles()
    sum_tok = OuterSum(placed)
    sum_tok.relays()
    two_sum = sum_two.result()
    two_parts = jnp.concatenate(
        [two_sum[first : first + size].reshape(fsdp_count, size // fsdp_count, width) for first, size in layout], axis=1
    )
    inner_two = InnerSum(two_parts)
    inner_two.step()
    state, state_tok, two_came = fence((sum_one.state(), sum_tok.state(), inner_two.came))
    sum_one.put(state)
    sum_tok.put(state_tok)
    inner_two.came = two_came

    sum_tok.singles()
    one_sum = sum_one.result()
    gain_sum = jnp.broadcast_to(one_sum[qkv_rows : qkv_rows + 8][None], (fsdp_count, 8, width))
    one_parts = jnp.concatenate([one_sum[:qkv_rows].reshape(fsdp_count, qkv_part, width), gain_sum], axis=1)
    inner_one = InnerSum(one_parts)
    inner_one.step()
    one_mine = inner_one.result()
    mlp_mine = inner_mlp.result()
    up_shard, down_shard = mlp_mine[:up_part].T, mlp_mine[up_part:]
    two_mine = inner_two.result()
    found = []
    at = 0
    for size in sizes_two:
        found.append(two_mine[at : at + size])
        at += size
    ckv_shard, out_shard, cq_shard, cout_shard = found[0].T, found[1], found[2], found[3]
    qkv_shard = one_mine[:qkv_part].T
    gain_mine = lax.dynamic_slice(one_mine[qkv_part:], (0, device_me * part), (3, part))
    token_grad = base + sum_tok.result()
    return (
        output,
        token_grad,
        coarse_grad,
        gain_mine[0],
        qkv_shard,
        out_shard,
        gain_mine[1],
        cq_shard,
        ckv_shard,
        cout_shard,
        gain_mine[2],
        up_shard,
        down_shard,
    )


def solution(mesh):
    rows = P(("dp", "fsdp"), None)
    columns = P(None, ("dp", "fsdp"))
    line = P(("dp", "fsdp"))
    in_specs = (
        rows, rows, rows, rows, line, line, line, columns, rows,
        line, rows, columns, rows, line, columns, rows, rows,
    )
    out_specs = (
        rows, rows, rows, line, columns, rows, line, rows, columns, rows, line, columns, rows,
    )
    return jax.shard_map(shards, mesh=mesh, in_specs=in_specs, out_specs=out_specs, check_vma=False)
```

time: 356 us -> 333 us (0.935)
  between operations: 15.5 us -> 2.23 us
  starting transfers between devices: 72.7 us -> 60.5 us
  waiting for transfers between devices: 99.6 us -> 104 us
  local copies, waits for them, and re-layouts: 26 us -> 22.4 us
    ppermute x0 -> x37, waiting for transfers between devices: none -> 84.5 us  [the longest x11 50.4 us: inner_swap(): return lax.ppermute(values, 'fsdp', [(i, i ^ mask) for i in range(count)])]
    ppermute x55 -> x20, waiting for transfers between devices: 58.6 us -> 3.73 us  [swap(): return lax.ppermute(values, 'dp', [(i, i ^ mask) for i in range(count)])]
    ppermute x0 -> x37, starting transfers between devices: none -> 45.8 us  [the longest x26 32.8 us: step_along(): lax.ppermute(values, 'dp', [(i, i ^ (mirrored(mask) if i & CORE else mask...]
    ppermute x55 -> x20, starting transfers between devices: 42 us -> 3.38 us  [swap(): return lax.ppermute(values, 'dp', [(i, i ^ mask) for i in range(count)])]
    ppermute x15 -> x6, waiting for transfers between devices: 35.1 us -> 15.4 us  [shift(): lax.ppermute(values, 'fsdp', [(i, (i + step) % count) for i in range(coun...]
    ppermute x15 -> x6, starting transfers between devices: 30.7 us -> 11.3 us  [shift(): lax.ppermute(values, 'fsdp', [(i, (i + step) % count) for i in range(coun...]
    slice x24 -> x5, local copies, waits for them, and re-layouts: 7.66 us -> 1.47 us  [the longest x3 1.39 us: shards(): mlp_cut = [mlp[:, first:last] for first, last in zip(cuts, cuts[1:])]]
    all_gather x1 -> x0, waiting for transfers between devices: 5.94 us -> none  [shards(): mlp = lax.all_gather(shard_mlp, 'fsdp', axis=0, tiled=False)]
  transfers between devices with their start and end apart: 71 -> 63, of which waited for: 31 -> 25; matrix products, arithmetic and copies ran while one was open for 9% -> 10% of each run, Pallas kernels for 30% -> 36%
where the time goes in v5:
time: 333 us; the launch traced here: 328 us
  Pallas kernels  119 us (36%)
  waiting for transfers between devices  104 us (31%)
  starting transfers between devices  60.5 us (18%)
  local copies, waits for them, and re-layouts  22.4 us (7%)
  other arithmetic  20.3 us (6%)
    ppermute x11, waiting for transfers between devices, inner_swap(): return lax.ppermute(values, 'fsdp', [(i, i ^ mask) for i in range(count)])  50.4 us
    ppermute x26, waiting for transfers between devices, step_along(): lax.ppermute(values, 'dp', [(i, i ^ (mirrored(mask) if i & CORE else mask...  34.1 us
    ppermute x26, starting transfers between devices, step_along(): lax.ppermute(values, 'dp', [(i, i ^ (mirrored(mask) if i & CORE else mask...  32.8 us
    pallas_call x2, Pallas kernels, mlp_call(): pl.pallas_call(functools.partial(mlp_kernel, (groups, tuple(((e, None) fo...  29.3 us
    pallas_call x1, Pallas kernels, attention_back(): pl.pallas_call(functools.partial(fourth_kernel, (blocks, first, last)), o...  18.8 us
    pallas_call x1, Pallas kernels, shards(): pl.pallas_call(functools.partial(third_kernel, (blocks, places_two, layou...  16 us
    ppermute x6, waiting for transfers between devices, shift(): lax.ppermute(values, 'fsdp', [(i, (i + step) % count) for i in range(coun...  15.4 us
    ppermute x11, starting transfers between devices, inner_swap(): return lax.ppermute(values, 'fsdp', [(i, i ^ mask) for i in range(count)])  13 us
  transfers between devices with their start and end apart: 63, of which 25 were waited for; matrix products, arithmetic and copies ran while one was open for 10% of the time, Pallas kernels for 36%

profile of v5, /device:TPU:0, one launch (start us, length us, event | category | flops | bytes accessed | tf_op | source)
XLA Modules:
  0.0 327.9 jit_solution(913564008301151031)
XLA Ops:
  15.3 3.8 %collective-permute-done.3 = bf16[80,768]{1,0:T(8,128)(2,1)S(1)} collective-permute-done((bf16[80,768]{1,0:T(8,128)(2,1)S(1)}, bf16[80,768]{1,0:T(8,128)(2,1)S(1)}, u32[]{:S(2)}, u32[]{:S(2)}) %collective-permute-start.3) | collective-permute-done | bytes 122912 | tf_op jit(solution)/shard_map/ppermute | solution.py:30
  30.9 3.9 %collective-permute-done.7 = bf16[120,768]{1,0:T(8,128)(2,1)S(1)} collective-permute-done((bf16[120,768]{1,0:T(8,128)(2,1)S(1)}, bf16[120,768]{1,0:T(8,128)(2,1)S(1)}, u32[]{:S(2)}, u32[]{:S(2)}) %collective-permute-start.7) | collective-permute-done | bytes 184352 | tf_op jit(solution)/shard_map/ppermute | solution.py:30
  34.8 6.1 %collective-permute-done.8 = bf16[120,768]{1,0:T(8,128)(2,1)S(1)} collective-permute-done((bf16[120,768]{1,0:T(8,128)(2,1)S(1)}, bf16[120,768]{1,0:T(8,128)(2,1)S(1)}, u32[]{:S(2)}, u32[]{:S(2)}) %collective-permute-start.8) | collective-permute-done | bytes 184352 | tf_op jit(solution)/shard_map/ppermute | solution.py:30
  42.8 4.4 %collective-permute-start.14 = (bf16[1,192,768]{2,1,0:T(8,128)(2,1)S(1)}, bf16[1,192,768]{2,1,0:T(8,128)(2,1)S(1)}, u32[]{:S(2)}, u32[]{:S(2)}) collective-permute-start(bf16[1,192,768]{2,1,0:T(8,128)(2,1)S(1)} %bitcast.168), channel_id=1, source_target_pairs={{0,1},{1,0},{2,3},{3,2},{4,5},{5,4},{6,7},{7,6},{8,9},{9,8},{10,11... | collective-permute-start | bytes 884744 | tf_op jit(solution)/shard_map/ppermute | solution.py:44
  48.1 5.3 %collective-permute-done.14 = bf16[1,192,768]{2,1,0:T(8,128)(2,1)S(1)} collective-permute-done((bf16[1,192,768]{2,1,0:T(8,128)(2,1)S(1)}, bf16[1,192,768]{2,1,0:T(8,128)(2,1)S(1)}, u32[]{:S(2)}, u32[]{:S(2)}) %collective-permute-start.14) | collective-permute-done | bytes 294944 | tf_op jit(solution)/shard_map/ppermute | solution.py:44
  59.0 7.7 %collective-permute-done.20 = bf16[2,64,768]{2,1,0:T(8,128)(2,1)} collective-permute-done((bf16[2,64,768]{2,1,0:T(8,128)(2,1)S(1)}, bf16[2,64,768]{2,1,0:T(8,128)(2,1)}, u32[]{:S(2)}, u32[]{:S(2)}) %collective-permute-start.20) | collective-permute-done | bytes 196640 | tf_op jit(solution)/shard_map/ppermute | solution.py:44
  74.6 12.8 %mix_self_attention.1 = (f32[512,768]{1,0:T(8,128)}, bf16[512,2304]{1,0:T(8,128)(2,1)}, bf16[512,768]{1,0:T(8,128)(2,1)}, f32[8,768]{1,0:T(8,128)}) custom-call(s32[17]{0:T(128)} %concatenate.72.ints, f32[4]{0:T(128)} %mix.3, s32[1,512]{1,0:T(1,128)} %seg_row.3, bf16[512,768]{1,0:T(8,128)(2,1)} %refs_0_, bf16[512,768]{1,0:T(8,128)(2,1)} %refs_0_, ...), custom_call_target="tpu_custom_call" | custom-call | flops 1000000000 | bytes 1000000 | tf_op jit(solution)/shard_map/mix_self_attention/pallas_call | solution.py:772
  93.6 7.5 %collective-permute-done.30 = bf16[2,32,768]{2,1,0:T(8,128)(2,1)S(1)} collective-permute-done((bf16[2,32,768]{2,1,0:T(8,128)(2,1)}, bf16[2,32,768]{2,1,0:T(8,128)(2,1)S(1)}, u32[]{:S(2)}, u32[]{:S(2)}) %collective-permute-start.30) | collective-permute-done | bytes 98336 | tf_op jit(solution)/shard_map/ppermute | solution.py:44
  110.2 11.0 %cross_attention.1 = (f32[512,768]{1,0:T(8,128)}, bf16[512,768]{1,0:T(8,128)(2,1)}, bf16[128,1536]{1,0:T(8,128)(2,1)}, bf16[512,768]{1,0:T(8,128)(2,1)}, f32[512,768]{1,0:T(8,128)}, /*index=5*/bf16[512,768]{1,0:T(8,128)(2,1)}) custom-call(s32[17]{0:T(128)} %concatenate.72.ints, s32[1,128]{1,0:T(1,128)} %bitcast.178, bf16[128,768]{1,0:T(8,128)(2,1)} %coarse.3, ...), custom_call_target="tpu_custom_call" | custom-call | flops 1000000000 | bytes 1000000 | tf_op jit(solution)/shard_map/cross_attention/pallas_call | solution.py:809
  121.3 12.2 %collective-permute-done.32.refs_1_ = bf16[768,768]{1,0:T(8,128)(2,1)} collective-permute-done((bf16[768,768]{1,0:T(8,128)(2,1)S(1)}, bf16[768,768]{1,0:T(8,128)(2,1)}, u32[]{:S(2)}, u32[]{:S(2)}) %collective-permute-start.32) | collective-permute-done | bytes 1179680 | tf_op jit(solution)/shard_map/ppermute | solution.py:80
  134.9 20.5 %feed_forward.2 = (bf16[3,2,384,768]{3,2,1,0:T(8,128)(2,1)}, bf16[2,512,768]{2,1,0:T(8,128)(2,1)}, f32[512,768]{1,0:T(8,128)}, f32[512,768]{1,0:T(8,128)}) custom-call(bf16[512,768]{1,0:T(8,128)(2,1)} %get-tuple-element.257.second, bf16[512,768]{1,0:T(8,128)(2,1)} %copy-done.15, bf16[512,768]{1,0:T(8,128)(2,1)} %cotangent.5, ...), custom_call_target="tpu_custom_call" | custom-call | flops 1000000000 | bytes 1000000 | tf_op jit(solution)/shard_map/feed_forward/pallas_call | solution.py:848
  156.4 8.8 %feed_forward.3 = (bf16[1,2,384,768]{3,2,1,0:T(8,128)(2,1)}, bf16[2,512,768]{2,1,0:T(8,128)(2,1)}, bf16[2,512,768]{2,1,0:T(8,128)(2,1)}) custom-call(bf16[512,768]{1,0:T(8,128)(2,1)} %get-tuple-element.257.second, bf16[512,768]{1,0:T(8,128)(2,1)} %copy-done.15, bf16[512,768]{1,0:T(8,128)(2,1)} %cotangent.5, ...), custom_call_target="tpu_custom_call" | custom-call | flops 1000000000 | bytes 1000000 | tf_op jit(solution)/shard_map/feed_forward/pallas_call | solution.py:848
  170.2 16.0 %cross_attention_backward.1 = (bf16[512,768]{1,0:T(8,128)(2,1)}, f32[512,768]{1,0:T(8,128)}, bf16[512,768]{1,0:T(8,128)(2,1)}, bf16[128,1536]{1,0:T(8,128)(2,1)}...) custom-call(s32[17]{0:T(128)} %concatenate.72.ints, s32[1,128]{1,0:T(1,128)} %bitcast.179, ...), custom_call_target="tpu_custom_call" | custom-call | flops 1000000000 | bytes 1000000 | tf_op jit(solution)/shard_map/cross_attention_backward/pallas_call | solution.py:883
  188.3 10.2 %cross_attention_weights.1 = (f32[128,768]{1,0:T(8,128)}, f32[512,768]{1,0:T(8,128)}, bf16[512,768]{1,0:T(8,128)(2,1)}, f32[8,768]{1,0:T(8,128)}, bf16[4,480,768...) custom-call(s32[17]{0:T(128)} %concatenate.72.ints, ...), custom_call_target="tpu_custom_call", output_to_operand_aliasing={{4}: (9, {}), {5}: (10, {})} | custom-call | flops 1000000000 | bytes 1000000 | tf_op jit(solution)/shard_map/cross_attention_weights/pallas_call | solution.py:910
  198.6 3.8 %collective-permute-done.40 = bf16[384,768]{1,0:T(8,128)(2,1)S(1)} collective-permute-done((bf16[384,768]{1,0:T(8,128)(2,1)S(1)}, bf16[384,768]{1,0:T(8,128)(2,1)S(1)}, u32[]{:S(2)}, u32[]{:S(2)}) %collective-permute-start.40) | collective-permute-done | bytes 589856 | tf_op jit(solution)/shard_map/ppermute | solution.py:80
  204.7 18.8 %self_attention_backward.1.grad_proj = bf16[512,2304]{1,0:T(8,128)(2,1)} custom-call(s32[17]{0:T(128)} %concatenate.72.ints, s32[1,512]{1,0:T(1,128)} %seg_row.3, bf16[512,768]{1,0:T(8,128)(2,1)} %get-tuple-element.311.grad_att, bf16[512,2304]{1,0:T(8,128)(2,1)} %get-tuple-element.312.qkv), custom_call_target="tpu_custom_call" | custom-call | flops 1000000000 | bytes 1000000 | tf_op jit(solution)/shard_map/self_attention_backward/pallas_call | solution.py:947
  230.3 8.3 %self_attention_weights.1 = (bf16[4,304,768]{2,1,0:T(8,128)(2,1)}, bf16[4,304,768]{2,1,0:T(8,128)(2,1)}) custom-call(s32[17]{0:T(128)} %concatenate.72.ints, f32[8,768]{1,0:T(8,128)} %get-tuple-element.228.gains, f32[8,768]{1,0:T(8,128)} %get-tuple-element.317.gain_grads, f32[512,768]{1,0:T(8,128)} %get-tuple-element.246.blended, ...), custom_call_target="tpu_custom_call" | custom-call | flops 1000000000 | bytes 1000000 | tf_op jit(solution)/shard_map/self_attention_weights/pallas_call | solution.py:969
  240.3 5.5 %collective-permute-done.46 = bf16[2,96,768]{2,1,0:T(8,128)(2,1)S(1)} collective-permute-done((bf16[2,96,768]{2,1,0:T(8,128)(2,1)S(1)}, bf16[2,96,768]{2,1,0:T(8,128)(2,1)S(1)}, u32[]{:S(2)}, u32[]{:S(2)}) %collective-permute-start.46) | collective-permute-done | bytes 294944 | tf_op jit(solution)/shard_map/ppermute | solution.py:44
  250.3 8.7 %self_attention_input.1 = (f32[512,768]{1,0:T(8,128)}, bf16[512,768]{1,0:T(8,128)(2,1)}) custom-call(s32[17]{0:T(128)} %concatenate.72.ints, f32[4]{0:T(128)} %mix.3, f32[8,768]{1,0:T(8,128)} %get-tuple-element.228.gains, f32[512,768]{1,0:T(8,128)} %get-tuple-element.246.blended, f32[512,768]{1,0:T(8,128)} %get-tuple-element.296.grad_res, ...), custom_call_target="tpu_custom_call" | custom-call | flops 1000000000 | bytes 1000000 | tf_op jit(solution)/shard_map/self_attention_input/pallas_call | solution.py:995
  259.2 5.7 %collective-permute-done.50 = bf16[2,96,768]{2,1,0:T(8,128)(2,1)S(1)} collective-permute-done((bf16[2,96,768]{2,1,0:T(8,128)(2,1)S(1)}, bf16[2,96,768]{2,1,0:T(8,128)(2,1)S(1)}, u32[]{:S(2)}, u32[]{:S(2)}) %collective-permute-start.50) | collective-permute-done | bytes 294944 | tf_op jit(solution)/shard_map/ppermute | solution.py:44
  285.6 5.7 %collective-permute-done.57 = bf16[2,120,768]{2,1,0:T(8,128)(2,1)S(1)} collective-permute-done((bf16[2,120,768]{2,1,0:T(8,128)(2,1)S(1)}, bf16[2,120,768]{2,1,0:T(8,128)(2,1)S(1)}, u32[]{:S(2)}, u32[]{:S(2)}) %collective-permute-start.57) | collective-permute-done | bytes 368672 | tf_op jit(solution)/shard_map/ppermute | solution.py:44
  291.3 11.9 %collective-permute-done.55 = bf16[304,768]{1,0:T(8,128)(2,1)S(1)} collective-permute-done((bf16[304,768]{1,0:T(8,128)(2,1)S(1)}, bf16[304,768]{1,0:T(8,128)(2,1)S(1)}, u32[]{:S(2)}, u32[]{:S(2)}) %collective-permute-start.55) | collective-permute-done | bytes 466976 | tf_op jit(solution)/shard_map/ppermute | solution.py:80
  313.5 3.7 %collective-permute-done.60 = bf16[2,80,768]{2,1,0:T(8,128)(2,1)S(1)} collective-permute-done((bf16[2,80,768]{2,1,0:T(8,128)(2,1)S(1)}, bf16[2,80,768]{2,1,0:T(8,128)(2,1)S(1)}, u32[]{:S(2)}, u32[]{:S(2)}) %collective-permute-start.60) | collective-permute-done | bytes 245792 | tf_op jit(solution)/shard_map/ppermute | solution.py:44
  318.1 4.2 %collective-permute-done.61 = bf16[1,80,768]{2,1,0:T(8,128)(2,1)S(1)} collective-permute-done((bf16[1,80,768]{2,1,0:T(8,128)(2,1)S(1)}, bf16[1,80,768]{2,1,0:T(8,128)(2,1)S(1)}, u32[]{:S(2)}, u32[]{:S(2)}) %collective-permute-start.61) | collective-permute-done | bytes 122912 | tf_op jit(solution)/shard_map/ppermute | solution.py:44
  (299 shorter events, 119.0 us)
Async XLA Ops:
  0.6 21.1 %collective-permute-start = (bf16[512,768]{1,0:T(8,128)(2,1)}, bf16[512,768]{1,0:T(8,128)(2,1)}, u32[]{:S(2)}, u32[]{:S(2)}) collective-permute-start(bf16[512,768]{1,0:T(8,128)(2,1)} %refs_0_), channel_id=1, source_target_pairs={{0,8},{4,20},{8,0},{12,28},{16,24},{20,4},{24,16},{28,12},{1,9},{5... | collective-permute-start | bytes 2359304 | tf_op jit(solution)/shard_map/ppermute | solution.py:80
  3.6 18.1 %collective-permute-start.1 = (bf16[512,768]{1,0:T(8,128)(2,1)}, bf16[512,768]{1,0:T(8,128)(2,1)}, u32[]{:S(2)}, u32[]{:S(2)}) collective-permute-start(bf16[512,768]{1,0:T(8,128)(2,1)} %refs_0_), channel_id=1, source_target_pairs={{0,16},{4,12},{8,24},{12,4},{16,0},{20,28},{24,8},{28,20},{1,17},{... | collective-permute-start | bytes 2359304 | tf_op jit(solution)/shard_map/ppermute | solution.py:80
  22.1 18.9 %collective-permute-start.5 = (bf16[304,768]{1,0:T(8,128)(2,1)S(1)}, bf16[304,768]{1,0:T(8,128)(2,1)S(1)}, u32[]{:S(2)}, u32[]{:S(2)}) collective-permute-start(bf16[304,768]{1,0:T(8,128)(2,1)S(1)} %pad_maximum_fusion.8.refs_8_.refs_0_), channel_id=1, source_target_pairs={{0,8},{4,20},{8,0},{12,28},{16,24},{20,4},{24,16},{28,12},{1,9},{5... | collective-permute-start | bytes 1400840 | tf_op jit(solution)/shard_map/ppermute | solution.py:80
  66.7 20.6 %collective-permute-start.25 = (bf16[512,768]{1,0:T(8,128)(2,1)S(1)}, bf16[512,768]{1,0:T(8,128)(2,1)}, u32[]{:S(2)}, u32[]{:S(2)}) collective-permute-start(bf16[512,768]{1,0:T(8,128)(2,1)S(1)} %copy-done.3), channel_id=1, source_target_pairs={{0,4},{4,0},{8,12},{12,8},{16,20},{20,16},{24,28},{28,24},{1,5},{5... | collective-permute-start | bytes 2359304 | tf_op jit(solution)/shard_map/ppermute | solution.py:25
  69.5 19.4 %collective-permute-start.22 = (bf16[480,768]{1,0:T(8,128)(2,1)S(1)}, bf16[480,768]{1,0:T(8,128)(2,1)S(1)}, u32[]{:S(2)}, u32[]{:S(2)}) collective-permute-start(bf16[480,768]{1,0:T(8,128)(2,1)S(1)} %pad_maximum_fusion.2.refs_0_), channel_id=1, source_target_pairs={{0,8},{4,20},{8,0},{12,28},{16,24},{20,4},{24,16},{28,12},{1,9},{5... | collective-permute-start | bytes 2211848 | tf_op jit(solution)/shard_map/ppermute | solution.py:80
  70.6 18.3 %collective-permute-start.23 = (bf16[480,768]{1,0:T(8,128)(2,1)S(1)}, bf16[480,768]{1,0:T(8,128)(2,1)S(1)}, u32[]{:S(2)}, u32[]{:S(2)}) collective-permute-start(bf16[480,768]{1,0:T(8,128)(2,1)S(1)} %pad_maximum_fusion.2.refs_0_), channel_id=1, source_target_pairs={{0,16},{4,12},{8,24},{12,4},{16,0},{20,28},{24,8},{28,20},{1,17},{... | collective-permute-start | bytes 2211848 | tf_op jit(solution)/shard_map/ppermute | solution.py:80
  72.0 16.9 %collective-permute-start.24 = (bf16[2,96,768]{2,1,0:T(8,128)(2,1)}, bf16[2,96,768]{2,1,0:T(8,128)(2,1)}, u32[]{:S(2)}, u32[]{:S(2)}) collective-permute-start(bf16[2,96,768]{2,1,0:T(8,128)(2,1)} %slice.235), channel_id=1, source_target_pairs={{0,2},{1,3},{2,0},{3,1},{4,6},{5,7},{6,4},{7,5},{8,10},{9,11},{10,... | collective-permute-start | bytes 884744 | tf_op jit(solution)/shard_map/ppermute | solution.py:44
  104.7 28.8 %collective-permute-start.32 = (bf16[768,768]{1,0:T(8,128)(2,1)S(1)}, bf16[768,768]{1,0:T(8,128)(2,1)}, u32[]{:S(2)}, u32[]{:S(2)}) collective-permute-start(bf16[768,768]{1,0:T(8,128)(2,1)S(1)} %pad_maximum_fusion.1.refs_0_), channel_id=1, source_target_pairs={{0,8},{4,20},{8,0},{12,28},{16,24},{20,4},{24,16},{28,12},{1,9},{5... | collective-permute-start | bytes 3538952 | tf_op jit(solution)/shard_map/ppermute | solution.py:80
  105.7 27.8 %collective-permute-start.33 = (bf16[768,768]{1,0:T(8,128)(2,1)S(1)}, bf16[768,768]{1,0:T(8,128)(2,1)}, u32[]{:S(2)}, u32[]{:S(2)}) collective-permute-start(bf16[768,768]{1,0:T(8,128)(2,1)S(1)} %pad_maximum_fusion.1.refs_0_), channel_id=1, source_target_pairs={{0,16},{4,12},{8,24},{12,4},{16,0},{20,28},{24,8},{28,20},{1,17},{... | collective-permute-start | bytes 3538952 | tf_op jit(solution)/shard_map/ppermute | solution.py:80
  133.5 21.9 %collective-permute-start.36 = (bf16[768,768]{1,0:T(8,128)(2,1)}, bf16[768,768]{1,0:T(8,128)(2,1)S(1)}, u32[]{:S(2)}, u32[]{:S(2)}) collective-permute-start(bf16[768,768]{1,0:T(8,128)(2,1)} %collective-permute-done.32.refs_1_), channel_id=1, source_target_pairs={{0,16},{4,12},{8,24},{12,4},{16,0},{20,28},{24,8},{28,20},{1,17},{... | collective-permute-start | bytes 3538952 | tf_op jit(solution)/shard_map/ppermute | solution.py:80
  169.0 17.2 %collective-permute-start.39 = (bf16[768,768]{1,0:T(8,128)(2,1)}, bf16[768,768]{1,0:T(8,128)(2,1)S(1)}, u32[]{:S(2)}, u32[]{:S(2)}) collective-permute-start(bf16[768,768]{1,0:T(8,128)(2,1)} %bitcast.32), channel_id=1, source_target_pairs={{0,16},{4,12},{8,24},{12,4},{16,0},{20,28},{24,8},{28,20},{1,17},{... | collective-permute-start | bytes 3538952 | tf_op jit(solution)/shard_map/ppermute | solution.py:80
  202.4 22.2 %collective-permute-start.44 = (bf16[4,480,768]{2,1,0:T(8,128)(2,1)}, bf16[4,480,768]{2,1,0:T(8,128)(2,1)}, u32[]{:S(2)}, u32[]{:S(2)}) collective-permute-start(bf16[4,480,768]{2,1,0:T(8,128)(2,1)} %get-tuple-element.310), channel_id=1, source_target_pairs={{0,4},{4,0},{8,12},{12,8},{16,20},{20,16},{24,28},{28,24},{1,5},{5... | collective-permute-start | bytes 8847368 | tf_op jit(solution)/shard_map/ppermute | solution.py:25
  202.6 21.9 %collective-permute-start.42 = (bf16[384,768]{1,0:T(8,128)(2,1)S(1)}, bf16[384,768]{1,0:T(8,128)(2,1)S(1)}, u32[]{:S(2)}, u32[]{:S(2)}) collective-permute-start(bf16[384,768]{1,0:T(8,128)(2,1)S(1)} %add_convert_fusion.4), channel_id=1, source_target_pairs={{0,8},{4,20},{8,0},{12,28},{16,24},{20,4},{24,16},{28,12},{1,9},{5... | collective-permute-start | bytes 1769480 | tf_op jit(solution)/shard_map/ppermute | solution.py:80
  203.7 20.8 %collective-permute-start.43 = (bf16[384,768]{1,0:T(8,128)(2,1)S(1)}, bf16[384,768]{1,0:T(8,128)(2,1)S(1)}, u32[]{:S(2)}, u32[]{:S(2)}) collective-permute-start(bf16[384,768]{1,0:T(8,128)(2,1)S(1)} %slice.247), channel_id=1, source_target_pairs={{0,16},{4,12},{8,24},{12,4},{16,0},{20,28},{24,8},{28,20},{1,17},{... | collective-permute-start | bytes 1769480 | tf_op jit(solution)/shard_map/ppermute | solution.py:80
  227.2 18.6 %collective-permute-start.45 = (bf16[480,768]{1,0:T(8,128)(2,1)}, bf16[480,768]{1,0:T(8,128)(2,1)S(1)}, u32[]{:S(2)}, u32[]{:S(2)}) collective-permute-start(bf16[480,768]{1,0:T(8,128)(2,1)} %add_convert_fusion.3), channel_id=1, source_target_pairs={{0,16},{4,12},{8,24},{12,4},{16,0},{20,28},{24,8},{28,20},{1,17},{... | collective-permute-start | bytes 2211848 | tf_op jit(solution)/shard_map/ppermute | solution.py:80
  245.8 20.3 %collective-permute-start.49 = (bf16[4,304,768]{2,1,0:T(8,128)(2,1)}, bf16[4,304,768]{2,1,0:T(8,128)(2,1)}, u32[]{:S(2)}, u32[]{:S(2)}) collective-permute-start(bf16[4,304,768]{2,1,0:T(8,128)(2,1)} %get-tuple-element.331), channel_id=1, source_target_pairs={{0,4},{4,0},{8,12},{12,8},{16,20},{20,16},{24,28},{28,24},{1,5},{5... | collective-permute-start | bytes 5603336 | tf_op jit(solution)/shard_map/ppermute | solution.py:25
  246.9 18.2 %collective-permute-start.48 = (bf16[480,768]{1,0:T(8,128)(2,1)}, bf16[480,768]{1,0:T(8,128)(2,1)}, u32[]{:S(2)}, u32[]{:S(2)}) collective-permute-start(bf16[480,768]{1,0:T(8,128)(2,1)} %add_convert_fusion.1), channel_id=1, source_target_pairs={{0,16},{4,12},{8,24},{12,4},{16,0},{20,28},{24,8},{28,20},{1,17},{... | collective-permute-start | bytes 2211848 | tf_op jit(solution)/shard_map/ppermute | solution.py:80
  249.0 17.1 %collective-permute-start.47 = (bf16[480,768]{1,0:T(8,128)(2,1)}, bf16[480,768]{1,0:T(8,128)(2,1)}, u32[]{:S(2)}, u32[]{:S(2)}) collective-permute-start(bf16[480,768]{1,0:T(8,128)(2,1)} %add_convert_fusion.2), channel_id=1, source_target_pairs={{0,8},{4,20},{8,0},{12,28},{16,24},{20,4},{24,16},{28,12},{1,9},{5... | collective-permute-start | bytes 2211848 | tf_op jit(solution)/shard_map/ppermute | solution.py:80
  272.0 19.3 %collective-permute-start.57 = (bf16[2,120,768]{2,1,0:T(8,128)(2,1)S(1)}, bf16[2,120,768]{2,1,0:T(8,128)(2,1)S(1)}, u32[]{:S(2)}, u32[]{:S(2)}) collective-permute-start(bf16[2,120,768]{2,1,0:T(8,128)(2,1)S(1)} %fusion.11), channel_id=1, source_target_pairs={{0,2},{1,3},{2,0},{3,1},{4,6},{5,7},{6,4},{7,5},{8,10},{9,11},{10,... | collective-permute-start | bytes 1105928 | tf_op jit(solution)/shard_map/ppermute | solution.py:44
  281.2 22.1 %collective-permute-start.56 = (bf16[512,768]{1,0:T(8,128)(2,1)S(1)}, bf16[512,768]{1,0:T(8,128)(2,1)S(1)}, u32[]{:S(2)}, u32[]{:S(2)}) collective-permute-start(bf16[512,768]{1,0:T(8,128)(2,1)S(1)} %get-tuple-element.367), channel_id=1, source_target_pairs={{0,16},{4,12},{8,24},{12,4},{16,0},{20,28},{24,8},{28,20},{1,17},{... | collective-permute-start | bytes 2359304 | tf_op jit(solution)/shard_map/ppermute | solution.py:80
  282.5 20.8 %collective-permute-start.55 = (bf16[304,768]{1,0:T(8,128)(2,1)S(1)}, bf16[304,768]{1,0:T(8,128)(2,1)S(1)}, u32[]{:S(2)}, u32[]{:S(2)}) collective-permute-start(bf16[304,768]{1,0:T(8,128)(2,1)S(1)} %add_convert_fusion.6), channel_id=1, source_target_pairs={{0,16},{4,12},{8,24},{12,4},{16,0},{20,28},{24,8},{28,20},{1,17},{... | collective-permute-start | bytes 1400840 | tf_op jit(solution)/shard_map/ppermute | solution.py:80
  283.6 19.6 %collective-permute-start.54 = (bf16[304,768]{1,0:T(8,128)(2,1)S(1)}, bf16[304,768]{1,0:T(8,128)(2,1)S(1)}, u32[]{:S(2)}, u32[]{:S(2)}) collective-permute-start(bf16[304,768]{1,0:T(8,128)(2,1)S(1)} %add_convert_fusion.7), channel_id=1, source_target_pairs={{0,8},{4,20},{8,0},{12,28},{16,24},{20,4},{24,16},{28,12},{1,9},{5... | collective-permute-start | bytes 1400840 | tf_op jit(solution)/shard_map/ppermute | solution.py:80
  307.0 18.8 %collective-permute-start.58 = (bf16[512,768]{1,0:T(8,128)(2,1)S(1)}, bf16[512,768]{1,0:T(8,128)(2,1)S(1)}, u32[]{:S(2)}, u32[]{:S(2)}) collective-permute-start(bf16[512,768]{1,0:T(8,128)(2,1)S(1)} %add_convert_fusion), channel_id=1, source_target_pairs={{0,8},{4,20},{8,0},{12,28},{16,24},{20,4},{24,16},{28,12},{1,9},{5... | collective-permute-start | bytes 2359304 | tf_op jit(solution)/shard_map/ppermute | solution.py:80
  308.3 17.6 %collective-permute-start.59 = (bf16[512,768]{1,0:T(8,128)(2,1)S(1)}, bf16[512,768]{1,0:T(8,128)(2,1)S(1)}, u32[]{:S(2)}, u32[]{:S(2)}) collective-permute-start(bf16[512,768]{1,0:T(8,128)(2,1)S(1)} %get-tuple-element.355), channel_id=1, source_target_pairs={{0,16},{4,12},{8,24},{12,4},{16,0},{20,28},{24,8},{28,20},{1,17},{... | collective-permute-start | bytes 2359304 | tf_op jit(solution)/shard_map/ppermute | solution.py:80
  (84 other events, 869.8 us)

commit v6 on v5

--- a/solution.py
+++ b/solution.py
@@ -14,7 +14,6 @@
 CLIP = 128
 WINDOW = 256
 TILE = 256
-VMEM_BYTES = 56 * 1024 * 1024
 f32 = jnp.float32
 bf16 = jnp.bfloat16
 fence = lax.optimization_barrier
@@ -274,8 +273,8 @@
 ANY = pl.BlockSpec(memory_space=pl.ANY)
 
 
-def params():
-    return pltpu.CompilerParams(vmem_limit_bytes=VMEM_BYTES)
+def params(mib=56):
+    return pltpu.CompilerParams(vmem_limit_bytes=mib * 1024 * 1024)
 
 
 def cost(flops, moved, exps=0):
@@ -712,7 +711,8 @@
         jnp.zeros((8, width), bf16), jnp.stack([ln1_gain, lnx_gain, ln2_gain]), (0, device_me * part)
     )
     shard_one = jnp.concatenate([w_qkv.T, gain_rows])
-    shard_two = jnp.concatenate([w_ckv.T, w_out, w_cq, w_cout])
+    shard_first = jnp.concatenate([shard_one, w_ckv.T])
+    shard_rest = jnp.concatenate([w_out, w_cq, w_cout])
     shard_mlp = jnp.concatenate([w_up.T, w_down])
     sizes_two = (w_ckv.shape[1], w_out.shape[0], w_cq.shape[0], w_cout.shape[0])
     qkv_part, up_part = w_qkv.shape[1], w_up.shape[1]
@@ -726,33 +726,36 @@
     rows_two = at * fsdp_count
 
     held_tok = {0: tokens, **single_steps(tokens)}
-    came_one = inner_start(shard_one)
-    held_tok, came_one, shard_two = fence((held_tok, came_one, shard_two))
-
-    ones = inner_order(came_one)
+    came_first = inner_start(shard_first)
+    held_tok, came_first, shard_rest = fence((held_tok, came_first, shard_rest))
+
+    firsts = inner_order(came_first)
+    ones = firsts[:, : qkv_part + 8]
     gain_block = jnp.sum(ones[:, qkv_part:].astype(f32), axis=0).astype(bf16)
     block_one = jnp.concatenate(
         [ones[:, :qkv_part].reshape(qkv_rows, width), gain_block, jnp.zeros((8, width), bf16)]
     )
     held_one = {0: block_one, **single_steps(block_one)}
-    came_two = inner_start(shard_two)
-    held_tok, held_one, came_two, shard_mlp = fence((held_tok, held_one, came_two, shard_mlp))
-
-    mlp = inner_double(shard_mlp[None], 1)
+    came_rest = inner_start(shard_rest)
+    held_tok, held_one, came_rest, shard_mlp, firsts = fence((held_tok, held_one, came_rest, shard_mlp, firsts))
+
+    near_mlp = inner_swap(shard_mlp, 1)
     core_tok = core_steps(dict(held_tok))
     near_tok = set(held_tok)
     relay_steps(held_tok)
-    twos = inner_order(came_two)
-    split = []
+    rests = inner_order(came_rest)
+    split = [firsts[:, qkv_part + 8 :].reshape(sizes_two[0] * fsdp_count, width)]
     at = 0
-    for size in sizes_two:
-        split.append(twos[:, at : at + size].reshape(size * fsdp_count, width))
+    for size in sizes_two[1:]:
+        split.append(rests[:, at : at + size].reshape(size * fsdp_count, width))
         at += size
     block_two = jnp.concatenate(split)
-    held_one, core_tok, held_tok, block_two, mlp = fence((held_one, core_tok, held_tok, block_two, mlp))
-
-    cuts = (0, 2 * up_part // 3, 5 * up_part // 3, 2 * up_part)
-    mlp_cut = [mlp[:, first:last] for first, last in zip(cuts, cuts[1:])]
+    held_one, core_tok, held_tok, block_two, near_mlp = fence((held_one, core_tok, held_tok, block_two, near_mlp))
+
+    cuts = (0, up_part // 3, 3 * up_part // 2, 2 * up_part)
+    mlp_cut = [
+        inner_join(shard_mlp[None, first:last], near_mlp[None, first:last], 1) for first, last in zip(cuts, cuts[1:])
+    ]
     mlp_came = [inner_swap(mlp_cut[0], 2)]
     core_one = core_steps(dict(held_one))
     relay_steps(held_one)
@@ -764,6 +767,7 @@
     held_two = {0: block_two, **single_steps(block_two)}
     cotangent_near = swap(cotangent, CORE)
     mlp_came.append(inner_swap(mlp_cut[1], 2))
+    mlp_joined = [inner_rest(inner_join(mlp_cut[0], mlp_came[0], 2))]
     late_one = core_steps({e: b for e, b in held_one.items() if e not in near_tok})
     pieces_tok = {**core_tok, **late_tok}
     pieces_one = {**core_one, **late_one}
@@ -789,14 +793,18 @@
         cost_estimate=cost(1e9, 1e6),
         name="mix_self_attention",
     )(ints, mix_weight, seg_row, tokens, *arrays_tok, *arrays_one)
-    held_two, attended, mlp_came, cotangent_near, mlp_cut = fence((held_two, attended, mlp_came, cotangent_near, mlp_cut))
+    held_two, attended, mlp_came, cotangent_near, mlp_cut, mlp_joined = fence(
+        (held_two, attended, mlp_came, cotangent_near, mlp_cut, mlp_joined)
+    )
 
     core_two = core_steps(dict(held_two))
     relay_steps(held_two)
     mlp_came.append(inner_swap(mlp_cut[2], 2))
-    held_two, core_two, mlp_came, ints_near = fence((held_two, core_two, mlp_came, ints_near))
-
-    mlp = jnp.concatenate([inner_rest(inner_join(cut, came, 2)) for cut, came in zip(mlp_cut, mlp_came)], axis=1)
+    mlp_joined.append(inner_rest(inner_join(mlp_cut[1], mlp_came[1], 2)))
+    held_two, core_two, mlp_came, mlp_joined = fence((held_two, core_two, mlp_came, mlp_joined))
+
+    mlp_joined.append(inner_rest(inner_join(mlp_cut[2], mlp_came[2], 2)))
+    mlp = jnp.concatenate(mlp_joined, axis=1)
     block_mlp = jnp.concatenate([mlp[:, :up_part].reshape(up_rows, width), mlp[:, up_part:].reshape(up_rows, width)])
     held_mlp = {0: block_mlp, **single_steps(block_mlp)}
     late_two = core_steps({e: b for e, b in held_two.items() if e not in near_tok})
@@ -824,7 +832,7 @@
         name="cross_attention",
     )(ints, coarse_seg, coarse_view, blended, attended, gains, *arrays_two)
     second_near = swap(second, CORE)
-    held_mlp, second, second_near = fence((held_mlp, second, second_near))
+    held_mlp, second, second_near, ints_near = fence((held_mlp, second, second_near, ints_near))
 
     early = dict(held_mlp)
     relay_steps(held_mlp)
@@ -859,7 +867,7 @@
                 pltpu.VMEM((2, row_count, up_rows), bf16),
                 pltpu.SemaphoreType.DMA((2 * count,)),
             ],
-            compiler_params=params(),
+            compiler_params=params(32),
             cost_estimate=cost(1e9, 1e6),
             name="feed_forward",
         )(second, second_near, cotangent, cotangent_near, *[pieces[e] for e in groups])
@@ -899,7 +907,7 @@
             pltpu.VMEM((row_count, width), bf16),
             pltpu.SemaphoreType.DMA((n_two + dp_count,)),
         ],
-        compiler_params=params(),
+        compiler_params=params(32),
         cost_estimate=cost(1e9, 1e6),
         name="cross_attention_backward",
     )(ints, coarse_seg, gains, mlp_out, grad_second, own_b, came_a, came_b, joined, cotangent, crossed, cq, ckv, *arrays_two)
@@ -953,19 +961,21 @@
             + [pltpu.VMEM((row_count, columns), f32)] * 2
             + [pltpu.SemaphoreType.DMA((3,))],
             input_output_aliases={4: 0} if held else {},
-            compiler_params=params(),
+            compiler_params=params(32),
             cost_estimate=cost(1e9, 1e6),
             name="self_attention_backward",
         )(ints, seg_row, grad_att, qkv, *held)
 
+    inner_mlp = [InnerSum(sum_mlp.result(0).reshape(fsdp_count, up_part, width))]
+    inner_mlp[0].step()
     grad_proj = attention_back(0, HEADS // 2, ())
-    state, came_two, grad_proj = fence((sum_mlp.state(), came_two, grad_proj))
+    state, came_two, grad_proj, inner_mlp[0].came = fence((sum_mlp.state(), came_two, grad_proj, inner_mlp[0].came))
     sum_mlp.put(state)
 
     sum_two = OuterSum(keep_two, came_two)
     sum_two.relays()
-    inner_up = InnerSum(sum_mlp.result(0).reshape(fsdp_count, up_part, width))
-    inner_up.step()
+    inner_mlp.append(InnerSum(sum_mlp.result(1).reshape(fsdp_count, up_part, width)))
+    inner_mlp[1].step()
     keep_one, send_one = pl.pallas_call(
         functools.partial(sixth_kernel, (dp_count, places_one, qkv_rows, mirrors)),
         out_shape=(
@@ -984,13 +994,10 @@
         cost_estimate=cost(1e9, 1e6),
         name="self_attention_weights",
     )(ints, gains, gain_grads, blended, grad_proj, *arrays_one)
-    state, keep_one, send_one, up_came = fence((sum_two.state(), keep_one, send_one, inner_up.came))
+    state, keep_one, send_one, inner_mlp[1].came = fence((sum_two.state(), keep_one, send_one, inner_mlp[1].came))
     sum_two.put(state)
-    inner_up.came = up_came
 
     sum_two.singles()
-    inner_down = InnerSum(sum_mlp.result(1).reshape(fsdp_count, up_part, width))
-    inner_down.step()
     came_one = swap(send_one, CORE)
     base, going_tok = pl.pallas_call(
         functools.partial(fifth_kernel, (dp_count, blocks, places_one, qkv_rows, mirrors)),
@@ -1008,9 +1015,8 @@
         cost_estimate=cost(1e9, 1e6),
         name="self_attention_input",
     )(ints, mix_weight, gains, blended, grad_res, grad_proj, *arrays_one)
-    state, came_one, going_tok, down_came = fence((sum_two.state(), came_one, going_tok, inner_down.came))
+    state, came_one, going_tok = fence((sum_two.state(), came_one, going_tok))
     sum_two.put(state)
-    inner_down.came = down_came
 
     sum_one = OuterSum(keep_one, came_one)
     sum_one.relays()
@@ -1020,11 +1026,11 @@
         out_shape=whole((pairs, row_count, width), bf16),
         in_specs=[SMEM, SMEM] + [VMEM] * 2,
         out_specs=VMEM,
-        compiler_params=params(),
+        compiler_params=params(32),
         cost_estimate=cost(1e9, 1e6),
         name="place_partner_gradients",
     )(ints, ints_near, going_tok, came_tok)
-    mlp_parts = jnp.concatenate([inner_parts(inner_up), inner_parts(inner_down)], axis=1)
+    mlp_parts = jnp.concatenate([inner_parts(inner) for inner in inner_mlp], axis=1)
     inner_mlp = InnerSum(mlp_parts)
     inner_mlp.finish()
     state, placed, mlp_came = fence((sum_one.state(), placed, inner_mlp.came))

time: 333 us -> 314 us (0.943)
  Pallas kernels: 119 us -> 104 us
  other arithmetic: 20.3 us -> 16.9 us
    pallas_call x2, Pallas kernels: 29.3 us -> 22.9 us  [mlp_call(): pl.pallas_call(functools.partial(mlp_kernel, (groups, tuple(((e, None) fo...]
    ppermute x11, waiting for transfers between devices: 50.4 us -> 44.6 us  [inner_swap(): return lax.ppermute(values, 'fsdp', [(i, i ^ mask) for i in range(count)])]
    unnamed x106 -> x160, local copies, waits for them, and re-layouts: 6.34 us -> 10.9 us
    ppermute x26, waiting for transfers between devices: 34.1 us -> 37.8 us  [step_along(): lax.ppermute(values, 'dp', [(i, i ^ (mirrored(mask) if i & CORE else mask...]
  transfers between devices with their start and end apart: 63 -> 63, of which waited for: 25 -> 25; matrix products, arithmetic and copies ran while one was open for 10% -> 9% of each run, Pallas kernels for 36% -> 34%
where the time goes in v6:
time: 314 us; the launch traced here: 309 us
  Pallas kernels  104 us (33%)
  waiting for transfers between devices  102 us (32%)
  starting transfers between devices  58.1 us (19%)
  local copies, waits for them, and re-layouts  25.1 us (8%)
  other arithmetic  16.9 us (5%)
    ppermute x11, waiting for transfers between devices, inner_swap(): return lax.ppermute(values, 'fsdp', [(i, i ^ mask) for i in range(count)])  44.6 us
    ppermute x26, waiting for transfers between devices, step_along(): lax.ppermute(values, 'dp', [(i, i ^ (mirrored(mask) if i & CORE else mask...  37.8 us
    ppermute x26, starting transfers between devices, step_along(): lax.ppermute(values, 'dp', [(i, i ^ (mirrored(mask) if i & CORE else mask...  30.3 us
    pallas_call x2, Pallas kernels, mlp_call(): pl.pallas_call(functools.partial(mlp_kernel, (groups, tuple(((e, None) fo...  22.9 us
    ppermute x6, waiting for transfers between devices, shift(): lax.ppermute(values, 'fsdp', [(i, (i + step) % count) for i in range(coun...  16.2 us
    pallas_call x1, Pallas kernels, attention_back(): pl.pallas_call(functools.partial(fourth_kernel, (blocks, first, last)), o...  16.1 us
    pallas_call x1, Pallas kernels, shards(): pl.pallas_call(functools.partial(third_kernel, (blocks, places_two, layou...  13.3 us
    ppermute x6, starting transfers between devices, shift(): lax.ppermute(values, 'fsdp', [(i, (i + step) % count) for i in range(coun...  12.9 us
  transfers between devices with their start and end apart: 63, of which 25 were waited for; matrix products, arithmetic and copies ran while one was open for 9% of the time, Pallas kernels for 34%

profile of v6, /device:TPU:0, one launch (start us, length us, event | category | flops | bytes accessed | tf_op | source)
XLA Modules:
  0.0 308.6 jit_solution(4749638459951349495)
XLA Ops:
  13.7 3.2 %collective-permute-done.2 = bf16[128,768]{1,0:T(8,128)(2,1)S(1)} collective-permute-done((bf16[128,768]{1,0:T(8,128)(2,1)S(1)}, bf16[128,768]{1,0:T(8,128)(2,1)S(1)}, u32[]{:S(2)}, u32[]{:S(2)}) %collective-permute-start.2) | collective-permute-done | bytes 196640 | tf_op jit(solution)/shard_map/ppermute | solution.py:29
  16.9 6.9 %collective-permute-done.3 = bf16[128,768]{1,0:T(8,128)(2,1)S(1)} collective-permute-done((bf16[128,768]{1,0:T(8,128)(2,1)S(1)}, bf16[128,768]{1,0:T(8,128)(2,1)S(1)}, u32[]{:S(2)}, u32[]{:S(2)}) %collective-permute-start.3) | collective-permute-done | bytes 196640 | tf_op jit(solution)/shard_map/ppermute | solution.py:29
  26.5 4.7 %collective-permute-start.7 = (bf16[72,768]{1,0:T(8,128)(2,1)S(1)}, bf16[72,768]{1,0:T(8,128)(2,1)S(1)}, u32[]{:S(2)}, u32[]{:S(2)}) collective-permute-start(bf16[72,768]{1,0:T(8,128)(2,1)S(1)} %pad_maximum_fusion.13), channel_id=1, source_target_pairs={{0,1},{1,2},{2,3},{3,0},{4,5},{5,6},{6,7},{7,4},{8,9},{9,10},{10,1... | collective-permute-start | bytes 331784 | tf_op jit(solution)/shard_map/ppermute | solution.py:29
  36.2 3.5 %collective-permute-done.8 = bf16[72,768]{1,0:T(8,128)(2,1)S(1)} collective-permute-done((bf16[72,768]{1,0:T(8,128)(2,1)S(1)}, bf16[72,768]{1,0:T(8,128)(2,1)S(1)}, u32[]{:S(2)}, u32[]{:S(2)}) %collective-permute-start.8) | collective-permute-done | bytes 110624 | tf_op jit(solution)/shard_map/ppermute | solution.py:29
  45.2 7.1 %collective-permute-done.14 = bf16[192,768]{1,0:T(8,128)(2,1)S(1)} collective-permute-done((bf16[192,768]{1,0:T(8,128)(2,1)S(1)}, bf16[192,768]{1,0:T(8,128)(2,1)S(1)}, u32[]{:S(2)}, u32[]{:S(2)}) %collective-permute-start.14) | collective-permute-done | bytes 294944 | tf_op jit(solution)/shard_map/ppermute | solution.py:43
  56.1 4.7 %collective-permute-done.20 = bf16[2,32,768]{2,1,0:T(8,128)(2,1)S(1)} collective-permute-done((bf16[2,32,768]{2,1,0:T(8,128)(2,1)S(1)}, bf16[2,32,768]{2,1,0:T(8,128)(2,1)S(1)}, u32[]{:S(2)}, u32[]{:S(2)}) %collective-permute-start.20) | collective-permute-done | bytes 98336 | tf_op jit(solution)/shard_map/ppermute | solution.py:43
  70.9 12.5 %mix_self_attention.1 = (f32[512,768]{1,0:T(8,128)}, bf16[512,2304]{1,0:T(8,128)(2,1)}, bf16[512,768]{1,0:T(8,128)(2,1)}, f32[8,768]{1,0:T(8,128)}) custom-call(s32[17]{0:T(128)} %concatenate.78.ints, f32[4]{0:T(128)} %mix.3, s32[1,512]{1,0:T(1,128)} %seg_row.3, bf16[512,768]{1,0:T(8,128)(2,1)} %refs_0_, bf16[512,768]{1,0:T(8,128)(2,1)} %refs_0_, ...), custom_call_target="tpu_custom_call" | custom-call | flops 1000000000 | bytes 1000000 | tf_op jit(solution)/shard_map/mix_self_attention/pallas_call | solution.py:776
  83.4 3.5 %collective-permute-done.24 = bf16[2,112,768]{2,1,0:T(8,128)(2,1)S(1)} collective-permute-done((bf16[2,112,768]{2,1,0:T(8,128)(2,1)}, bf16[2,112,768]{2,1,0:T(8,128)(2,1)S(1)}, u32[]{:S(2)}, u32[]{:S(2)}) %collective-permute-start.24) | collective-permute-done | bytes 344096 | tf_op jit(solution)/shard_map/ppermute | solution.py:43
  88.2 10.0 %collective-permute-done.30 = bf16[2,48,768]{2,1,0:T(8,128)(2,1)S(1)} collective-permute-done((bf16[2,48,768]{2,1,0:T(8,128)(2,1)S(1)}, bf16[2,48,768]{2,1,0:T(8,128)(2,1)S(1)}, u32[]{:S(2)}, u32[]{:S(2)}) %collective-permute-start.30) | collective-permute-done | bytes 147488 | tf_op jit(solution)/shard_map/ppermute | solution.py:43
  104.7 11.1 %cross_attention.1 = (f32[512,768]{1,0:T(8,128)}, bf16[512,768]{1,0:T(8,128)(2,1)}, bf16[128,1536]{1,0:T(8,128)(2,1)}, bf16[512,768]{1,0:T(8,128)(2,1)}, f32[512,768]{1,0:T(8,128)}, /*index=5*/bf16[512,768]{1,0:T(8,128)(2,1)}) custom-call(s32[17]{0:T(128)} %concatenate.78.ints, s32[1,128]{1,0:T(1,128)} %bitcast.166, bf16[128,768]{1,0:T(8,128)(2,1)} %coarse.3, ...), custom_call_target="tpu_custom_call" | custom-call | flops 1000000000 | bytes 1000000 | tf_op jit(solution)/shard_map/cross_attention/pallas_call | solution.py:817
  117.9 10.7 %collective-permute-done.31.refs_1_ = bf16[768,768]{1,0:T(8,128)(2,1)} collective-permute-done((bf16[768,768]{1,0:T(8,128)(2,1)S(1)}, bf16[768,768]{1,0:T(8,128)(2,1)}, u32[]{:S(2)}, u32[]{:S(2)}) %collective-permute-start.31) | collective-permute-done | bytes 1179680 | tf_op jit(solution)/shard_map/ppermute | solution.py:79
  130.7 16.7 %feed_forward.2 = (bf16[3,2,384,768]{3,2,1,0:T(8,128)(2,1)S(1)}, bf16[2,512,768]{2,1,0:T(8,128)(2,1)S(1)}, f32[512,768]{1,0:T(8,128)S(1)}, f32[512,768]{1,0:T(8,128)S(1)}) custom-call(bf16[512,768]{1,0:T(8,128)(2,1)S(1)} %copy-done.16, bf16[512,768]{1,0:T(8,128)(2,1)S(1)} %collective-permute-done.34.second_near, bf16[512,768]{1,0:T(8,128)(2,1)S(1)} %copy-done.3, ...), custom_call_target="tpu_custom_call" | custom-call | flops 1000000000 | bytes 1000000 | tf_op jit(solution)/shard_map/feed_forward/pallas_call | solution.py:856
  147.6 6.2 %feed_forward.3 = (bf16[1,2,384,768]{3,2,1,0:T(8,128)(2,1)S(1)}, bf16[2,512,768]{2,1,0:T(8,128)(2,1)S(1)}, bf16[2,512,768]{2,1,0:T(8,128)(2,1)S(1)}) custom-call(bf16[512,768]{1,0:T(8,128)(2,1)S(1)} %copy-done.16, bf16[512,768]{1,0:T(8,128)(2,1)S(1)} %collective-permute-done.34.second_near, bf16[512,768]{1,0:T(8,128)(2,1)S(1)} %copy-done.3, ...), custom_call_target="tpu_custom_call" | custom-call | flops 1000000000 | bytes 1000000 | tf_op jit(solution)/shard_map/feed_forward/pallas_call | solution.py:856
  158.7 13.3 %cross_attention_backward.1 = (bf16[512,768]{1,0:T(8,128)(2,1)}, f32[512,768]{1,0:T(8,128)S(1)}, bf16[512,768]{1,0:T(8,128)(2,1)S(1)}, bf16[128,1536]{1,0:T(8,12...) custom-call(s32[17]{0:T(128)S(1)} %copy-done.30, ...), custom_call_target="tpu_custom_call" | custom-call | flops 1000000000 | bytes 1000000 | tf_op jit(solution)/shard_map/cross_attention_backward/pallas_call | solution.py:891
  176.2 10.5 %cross_attention_weights.1 = (f32[128,768]{1,0:T(8,128)}, f32[512,768]{1,0:T(8,128)}, bf16[512,768]{1,0:T(8,128)(2,1)}, f32[8,768]{1,0:T(8,128)}, bf16[4,480,768...) custom-call(s32[17]{0:T(128)} %concatenate.78.ints, ...), custom_call_target="tpu_custom_call", output_to_operand_aliasing={{4}: (9, {}), {5}: (10, {})} | custom-call | flops 1000000000 | bytes 1000000 | tf_op jit(solution)/shard_map/cross_attention_weights/pallas_call | solution.py:918
  195.8 16.1 %self_attention_backward.1.grad_proj = bf16[512,2304]{1,0:T(8,128)(2,1)S(1)} custom-call(s32[17]{0:T(128)S(1)} %copy-done.31, s32[1,512]{1,0:T(1,128)S(1)} %copy-done.29, bf16[512,768]{1,0:T(8,128)(2,1)S(1)} %copy-done.24, bf16[512,2304]{1,0:T(8,128)(2,1)S(1)} %copy-done.17), custom_call_target="tpu_custom_call" | custom-call | flops 1000000000 | bytes 1000000 | tf_op jit(solution)/shard_map/self_attention_backward/pallas_call | solution.py:955
  219.2 8.3 %self_attention_weights.1 = (bf16[4,304,768]{2,1,0:T(8,128)(2,1)}, bf16[4,304,768]{2,1,0:T(8,128)(2,1)}) custom-call(s32[17]{0:T(128)} %concatenate.78.ints, f32[8,768]{1,0:T(8,128)} %get-tuple-element.227.gains, f32[8,768]{1,0:T(8,128)} %get-tuple-element.315.gain_grads, f32[512,768]{1,0:T(8,128)} %get-tuple-element.244.blended, bf16[512,2304]{1,0:T(8,128)(2,1)} %copy-done, ...), custom_call_target="tpu_custom_call" | custom-call | flops 1000000000 | bytes 1000000 | tf_op jit(solution)/shard_map/self_attention_weights/pallas_call | solution.py:979
  238.0 8.5 %self_attention_input.1 = (f32[512,768]{1,0:T(8,128)}, bf16[512,768]{1,0:T(8,128)(2,1)}) custom-call(s32[17]{0:T(128)} %concatenate.78.ints, f32[4]{0:T(128)} %mix.3, f32[8,768]{1,0:T(8,128)} %get-tuple-element.227.gains, f32[512,768]{1,0:T(8,128)} %get-tuple-element.244.blended, f32[512,768]{1,0:T(8,128)} %get-tuple-element.294.grad_res, ...), custom_call_target="tpu_custom_call" | custom-call | flops 1000000000 | bytes 1000000 | tf_op jit(solution)/shard_map/self_attention_input/pallas_call | solution.py:1002
  248.2 3.4 %collective-permute-done.49 = bf16[480,768]{1,0:T(8,128)(2,1)S(1)} collective-permute-done((bf16[480,768]{1,0:T(8,128)(2,1)S(1)}, bf16[480,768]{1,0:T(8,128)(2,1)S(1)}, u32[]{:S(2)}, u32[]{:S(2)}) %collective-permute-start.49) | collective-permute-done | bytes 737312 | tf_op jit(solution)/shard_map/ppermute | solution.py:79
  259.4 4.0 %collective-permute-done.51 = bf16[304,768]{1,0:T(8,128)(2,1)S(1)} collective-permute-done((bf16[304,768]{1,0:T(8,128)(2,1)S(1)}, bf16[304,768]{1,0:T(8,128)(2,1)S(1)}, u32[]{:S(2)}, u32[]{:S(2)}) %collective-permute-start.51) | collective-permute-done | bytes 466976 | tf_op jit(solution)/shard_map/ppermute | solution.py:79
  268.3 6.5 %collective-permute-done.57 = bf16[2,120,768]{2,1,0:T(8,128)(2,1)S(1)} collective-permute-done((bf16[2,120,768]{2,1,0:T(8,128)(2,1)S(1)}, bf16[2,120,768]{2,1,0:T(8,128)(2,1)S(1)}, u32[]{:S(2)}, u32[]{:S(2)}) %collective-permute-start.57) | collective-permute-done | bytes 368672 | tf_op jit(solution)/shard_map/ppermute | solution.py:43
  274.8 10.9 %collective-permute-done.55 = bf16[304,768]{1,0:T(8,128)(2,1)S(1)} collective-permute-done((bf16[304,768]{1,0:T(8,128)(2,1)S(1)}, bf16[304,768]{1,0:T(8,128)(2,1)S(1)}, u32[]{:S(2)}, u32[]{:S(2)}) %collective-permute-start.55) | collective-permute-done | bytes 466976 | tf_op jit(solution)/shard_map/ppermute | solution.py:79
  294.9 3.9 %collective-permute-done.60 = bf16[2,80,768]{2,1,0:T(8,128)(2,1)S(1)} collective-permute-done((bf16[2,80,768]{2,1,0:T(8,128)(2,1)S(1)}, bf16[2,80,768]{2,1,0:T(8,128)(2,1)S(1)}, u32[]{:S(2)}, u32[]{:S(2)}) %collective-permute-start.60) | collective-permute-done | bytes 245792 | tf_op jit(solution)/shard_map/ppermute | solution.py:43
  299.6 4.2 %collective-permute-done.61 = bf16[1,80,768]{2,1,0:T(8,128)(2,1)S(1)} collective-permute-done((bf16[1,80,768]{2,1,0:T(8,128)(2,1)S(1)}, bf16[1,80,768]{2,1,0:T(8,128)(2,1)S(1)}, u32[]{:S(2)}, u32[]{:S(2)}) %collective-permute-start.61) | collective-permute-done | bytes 122912 | tf_op jit(solution)/shard_map/ppermute | solution.py:43
  (358 shorter events, 116.0 us)
Async XLA Ops:
  0.6 23.2 %collective-permute-start = (bf16[512,768]{1,0:T(8,128)(2,1)}, bf16[512,768]{1,0:T(8,128)(2,1)S(1)}, u32[]{:S(2)}, u32[]{:S(2)}) collective-permute-start(bf16[512,768]{1,0:T(8,128)(2,1)} %refs_0_), channel_id=1, source_target_pairs={{0,8},{4,20},{8,0},{12,28},{16,24},{20,4},{24,16},{28,12},{1,9},{5... | collective-permute-start | bytes 2359304 | tf_op jit(solution)/shard_map/ppermute | solution.py:79
  3.6 21.2 %collective-permute-start.1 = (bf16[512,768]{1,0:T(8,128)(2,1)}, bf16[512,768]{1,0:T(8,128)(2,1)}, u32[]{:S(2)}, u32[]{:S(2)}) collective-permute-start(bf16[512,768]{1,0:T(8,128)(2,1)} %refs_0_), channel_id=1, source_target_pairs={{0,16},{4,12},{8,24},{12,4},{16,0},{20,28},{24,8},{28,20},{1,17},{... | collective-permute-start | bytes 2359304 | tf_op jit(solution)/shard_map/ppermute | solution.py:79
  62.7 20.7 %collective-permute-start.25 = (bf16[512,768]{1,0:T(8,128)(2,1)S(1)}, bf16[512,768]{1,0:T(8,128)(2,1)}, u32[]{:S(2)}, u32[]{:S(2)}) collective-permute-start(bf16[512,768]{1,0:T(8,128)(2,1)S(1)} %copy-done.3), channel_id=1, source_target_pairs={{0,4},{4,0},{8,12},{12,8},{16,20},{20,16},{24,28},{28,24},{1,5},{5... | collective-permute-start | bytes 2359304 | tf_op jit(solution)/shard_map/ppermute | solution.py:24
  64.3 22.6 %collective-permute-start.22 = (bf16[480,768]{1,0:T(8,128)(2,1)S(1)}, bf16[480,768]{1,0:T(8,128)(2,1)S(1)}, u32[]{:S(2)}, u32[]{:S(2)}) collective-permute-start(bf16[480,768]{1,0:T(8,128)(2,1)S(1)} %pad_maximum_fusion.2.refs_0_), channel_id=1, source_target_pairs={{0,8},{4,20},{8,0},{12,28},{16,24},{20,4},{24,16},{28,12},{1,9},{5... | collective-permute-start | bytes 2211848 | tf_op jit(solution)/shard_map/ppermute | solution.py:79
  65.7 21.2 %collective-permute-start.23 = (bf16[480,768]{1,0:T(8,128)(2,1)S(1)}, bf16[480,768]{1,0:T(8,128)(2,1)S(1)}, u32[]{:S(2)}, u32[]{:S(2)}) collective-permute-start(bf16[480,768]{1,0:T(8,128)(2,1)S(1)} %pad_maximum_fusion.2.refs_0_), channel_id=1, source_target_pairs={{0,16},{4,12},{8,24},{12,4},{16,0},{20,28},{24,8},{28,20},{1,17},{... | collective-permute-start | bytes 2211848 | tf_op jit(solution)/shard_map/ppermute | solution.py:79
  67.9 18.9 %collective-permute-start.24 = (bf16[2,112,768]{2,1,0:T(8,128)(2,1)}, bf16[2,112,768]{2,1,0:T(8,128)(2,1)S(1)}, u32[]{:S(2)}, u32[]{:S(2)}) collective-permute-start(bf16[2,112,768]{2,1,0:T(8,128)(2,1)} %pad_maximum_fusion.8), channel_id=1, source_target_pairs={{0,2},{1,3},{2,0},{3,1},{4,6},{5,7},{6,4},{7,5},{8,10},{9,11},{10,... | collective-permute-start | bytes 1032200 | tf_op jit(solution)/shard_map/ppermute | solution.py:43
  100.1 28.5 %collective-permute-start.31 = (bf16[768,768]{1,0:T(8,128)(2,1)S(1)}, bf16[768,768]{1,0:T(8,128)(2,1)}, u32[]{:S(2)}, u32[]{:S(2)}) collective-permute-start(bf16[768,768]{1,0:T(8,128)(2,1)S(1)} %pad_maximum_fusion.1.refs_0_), channel_id=1, source_target_pairs={{0,8},{4,20},{8,0},{12,28},{16,24},{20,4},{24,16},{28,12},{1,9},{5... | collective-permute-start | bytes 3538952 | tf_op jit(solution)/shard_map/ppermute | solution.py:79
  100.8 27.8 %collective-permute-start.32 = (bf16[768,768]{1,0:T(8,128)(2,1)S(1)}, bf16[768,768]{1,0:T(8,128)(2,1)}, u32[]{:S(2)}, u32[]{:S(2)}) collective-permute-start(bf16[768,768]{1,0:T(8,128)(2,1)S(1)} %pad_maximum_fusion.1.refs_0_), channel_id=1, source_target_pairs={{0,16},{4,12},{8,24},{12,4},{16,0},{20,28},{24,8},{28,20},{1,17},{... | collective-permute-start | bytes 3538952 | tf_op jit(solution)/shard_map/ppermute | solution.py:79
  128.6 18.8 %collective-permute-start.36 = (bf16[768,768]{1,0:T(8,128)(2,1)}, bf16[768,768]{1,0:T(8,128)(2,1)S(1)}, u32[]{:S(2)}, u32[]{:S(2)}) collective-permute-start(bf16[768,768]{1,0:T(8,128)(2,1)} %collective-permute-done.31.refs_1_), channel_id=1, source_target_pairs={{0,16},{4,12},{8,24},{12,4},{16,0},{20,28},{24,8},{28,20},{1,17},{... | collective-permute-start | bytes 3538952 | tf_op jit(solution)/shard_map/ppermute | solution.py:79
  157.5 16.2 %collective-permute-start.39 = (bf16[768,768]{1,0:T(8,128)(2,1)S(1)}, bf16[768,768]{1,0:T(8,128)(2,1)S(1)}, u32[]{:S(2)}, u32[]{:S(2)}) collective-permute-start(bf16[768,768]{1,0:T(8,128)(2,1)S(1)} %bitcast.168), channel_id=1, source_target_pairs={{0,16},{4,12},{8,24},{12,4},{16,0},{20,28},{24,8},{28,20},{1,17},{... | collective-permute-start | bytes 3538952 | tf_op jit(solution)/shard_map/ppermute | solution.py:79
  190.4 23.4 %collective-permute-start.44 = (bf16[4,480,768]{2,1,0:T(8,128)(2,1)}, bf16[4,480,768]{2,1,0:T(8,128)(2,1)}, u32[]{:S(2)}, u32[]{:S(2)}) collective-permute-start(bf16[4,480,768]{2,1,0:T(8,128)(2,1)} %get-tuple-element.308), channel_id=1, source_target_pairs={{0,4},{4,0},{8,12},{12,8},{16,20},{20,16},{24,28},{28,24},{1,5},{5... | collective-permute-start | bytes 8847368 | tf_op jit(solution)/shard_map/ppermute | solution.py:24
  191.7 22.0 %collective-permute-start.42 = (bf16[384,768]{1,0:T(8,128)(2,1)S(1)}, bf16[384,768]{1,0:T(8,128)(2,1)S(1)}, u32[]{:S(2)}, u32[]{:S(2)}) collective-permute-start(bf16[384,768]{1,0:T(8,128)(2,1)S(1)} %add_convert_fusion.4), channel_id=1, source_target_pairs={{0,8},{4,20},{8,0},{12,28},{16,24},{20,4},{24,16},{28,12},{1,9},{5... | collective-permute-start | bytes 1769480 | tf_op jit(solution)/shard_map/ppermute | solution.py:79
  194.0 19.8 %collective-permute-start.43 = (bf16[384,768]{1,0:T(8,128)(2,1)S(1)}, bf16[384,768]{1,0:T(8,128)(2,1)S(1)}, u32[]{:S(2)}, u32[]{:S(2)}) collective-permute-start(bf16[384,768]{1,0:T(8,128)(2,1)S(1)} %slice.262), channel_id=1, source_target_pairs={{0,16},{4,12},{8,24},{12,4},{16,0},{20,28},{24,8},{28,20},{1,17},{... | collective-permute-start | bytes 1769480 | tf_op jit(solution)/shard_map/ppermute | solution.py:79
  195.1 18.7 %collective-permute-start.45 = (bf16[2,96,768]{2,1,0:T(8,128)(2,1)S(1)}, bf16[2,96,768]{2,1,0:T(8,128)(2,1)S(1)}, u32[]{:S(2)}, u32[]{:S(2)}) collective-permute-start(bf16[2,96,768]{2,1,0:T(8,128)(2,1)S(1)} %fusion.10), channel_id=1, source_target_pairs={{0,2},{1,3},{2,0},{3,1},{4,6},{5,7},{6,4},{7,5},{8,10},{9,11},{10,... | collective-permute-start | bytes 884744 | tf_op jit(solution)/shard_map/ppermute | solution.py:43
  215.2 17.3 %collective-permute-start.46 = (bf16[480,768]{1,0:T(8,128)(2,1)S(1)}, bf16[480,768]{1,0:T(8,128)(2,1)}, u32[]{:S(2)}, u32[]{:S(2)}) collective-permute-start(bf16[480,768]{1,0:T(8,128)(2,1)S(1)} %add_convert_fusion.3), channel_id=1, source_target_pairs={{0,16},{4,12},{8,24},{12,4},{16,0},{20,28},{24,8},{28,20},{1,17},{... | collective-permute-start | bytes 2211848 | tf_op jit(solution)/shard_map/ppermute | solution.py:79
  232.5 20.6 %collective-permute-start.50 = (bf16[4,304,768]{2,1,0:T(8,128)(2,1)}, bf16[4,304,768]{2,1,0:T(8,128)(2,1)}, u32[]{:S(2)}, u32[]{:S(2)}) collective-permute-start(bf16[4,304,768]{2,1,0:T(8,128)(2,1)} %get-tuple-element.329), channel_id=1, source_target_pairs={{0,4},{4,0},{8,12},{12,8},{16,20},{20,16},{24,28},{28,24},{1,5},{5... | collective-permute-start | bytes 5603336 | tf_op jit(solution)/shard_map/ppermute | solution.py:24
  234.1 17.4 %collective-permute-start.49 = (bf16[480,768]{1,0:T(8,128)(2,1)S(1)}, bf16[480,768]{1,0:T(8,128)(2,1)S(1)}, u32[]{:S(2)}, u32[]{:S(2)}) collective-permute-start(bf16[480,768]{1,0:T(8,128)(2,1)S(1)} %add_convert_fusion.1), channel_id=1, source_target_pairs={{0,16},{4,12},{8,24},{12,4},{16,0},{20,28},{24,8},{28,20},{1,17},{... | collective-permute-start | bytes 2211848 | tf_op jit(solution)/shard_map/ppermute | solution.py:79
  236.9 16.2 %collective-permute-start.48 = (bf16[480,768]{1,0:T(8,128)(2,1)S(1)}, bf16[480,768]{1,0:T(8,128)(2,1)S(1)}, u32[]{:S(2)}, u32[]{:S(2)}) collective-permute-start(bf16[480,768]{1,0:T(8,128)(2,1)S(1)} %add_convert_fusion.2), channel_id=1, source_target_pairs={{0,8},{4,20},{8,0},{12,28},{16,24},{20,4},{24,16},{28,12},{1,9},{5... | collective-permute-start | bytes 2211848 | tf_op jit(solution)/shard_map/ppermute | solution.py:79
  256.8 18.0 %collective-permute-start.57 = (bf16[2,120,768]{2,1,0:T(8,128)(2,1)S(1)}, bf16[2,120,768]{2,1,0:T(8,128)(2,1)S(1)}, u32[]{:S(2)}, u32[]{:S(2)}) collective-permute-start(bf16[2,120,768]{2,1,0:T(8,128)(2,1)S(1)} %fusion.9), channel_id=1, source_target_pairs={{0,2},{1,3},{2,0},{3,1},{4,6},{5,7},{6,4},{7,5},{8,10},{9,11},{10,... | collective-permute-start | bytes 1105928 | tf_op jit(solution)/shard_map/ppermute | solution.py:43
  263.7 22.1 %collective-permute-start.56 = (bf16[512,768]{1,0:T(8,128)(2,1)S(1)}, bf16[512,768]{1,0:T(8,128)(2,1)S(1)}, u32[]{:S(2)}, u32[]{:S(2)}) collective-permute-start(bf16[512,768]{1,0:T(8,128)(2,1)S(1)} %get-tuple-element.363), channel_id=1, source_target_pairs={{0,16},{4,12},{8,24},{12,4},{16,0},{20,28},{24,8},{28,20},{1,17},{... | collective-permute-start | bytes 2359304 | tf_op jit(solution)/shard_map/ppermute | solution.py:79
  265.1 20.6 %collective-permute-start.55 = (bf16[304,768]{1,0:T(8,128)(2,1)S(1)}, bf16[304,768]{1,0:T(8,128)(2,1)S(1)}, u32[]{:S(2)}, u32[]{:S(2)}) collective-permute-start(bf16[304,768]{1,0:T(8,128)(2,1)S(1)} %add_convert_fusion.6), channel_id=1, source_target_pairs={{0,16},{4,12},{8,24},{12,4},{16,0},{20,28},{24,8},{28,20},{1,17},{... | collective-permute-start | bytes 1400840 | tf_op jit(solution)/shard_map/ppermute | solution.py:79
  266.1 19.6 %collective-permute-start.54 = (bf16[304,768]{1,0:T(8,128)(2,1)S(1)}, bf16[304,768]{1,0:T(8,128)(2,1)S(1)}, u32[]{:S(2)}, u32[]{:S(2)}) collective-permute-start(bf16[304,768]{1,0:T(8,128)(2,1)S(1)} %add_convert_fusion.7), channel_id=1, source_target_pairs={{0,8},{4,20},{8,0},{12,28},{16,24},{20,4},{24,16},{28,12},{1,9},{5... | collective-permute-start | bytes 1400840 | tf_op jit(solution)/shard_map/ppermute | solution.py:79
  289.0 17.8 %collective-permute-start.58 = (bf16[512,768]{1,0:T(8,128)(2,1)S(1)}, bf16[512,768]{1,0:T(8,128)(2,1)S(1)}, u32[]{:S(2)}, u32[]{:S(2)}) collective-permute-start(bf16[512,768]{1,0:T(8,128)(2,1)S(1)} %add_convert_fusion), channel_id=1, source_target_pairs={{0,8},{4,20},{8,0},{12,28},{16,24},{20,4},{24,16},{28,12},{1,9},{5... | collective-permute-start | bytes 2359304 | tf_op jit(solution)/shard_map/ppermute | solution.py:79
  290.0 16.8 %collective-permute-start.59 = (bf16[512,768]{1,0:T(8,128)(2,1)S(1)}, bf16[512,768]{1,0:T(8,128)(2,1)S(1)}, u32[]{:S(2)}, u32[]{:S(2)}) collective-permute-start(bf16[512,768]{1,0:T(8,128)(2,1)S(1)} %get-tuple-element.351), channel_id=1, source_target_pairs={{0,16},{4,12},{8,24},{12,4},{16,0},{20,28},{24,8},{28,20},{1,17},{... | collective-permute-start | bytes 2359304 | tf_op jit(solution)/shard_map/ppermute | solution.py:79
  (111 other events, 936.6 us)
